TPU v7x, 256 devices: a whole 4x4x8 slice. The times are simulated.
256 devices in a mesh: leaf: 256 (over x, z, y, core).
Axes of the slice: x: 4, y: 4, z: 8, core: 2. Of those that a mesh axis runs over, the one named last changes fastest.
Arguments:
- rhs: bfloat16 [524288, 64], P('leaf'), may hold values from -6 to 6
- leaf_inverse: bfloat16 [524288, 2048], P('leaf')
- bases: bfloat16 [3, 524288, 256], P(None, 'leaf'), may hold values from -0.125 to 0.125
- coupling: bfloat16 [3, 256, 256], replicated
Outputs:
- solved: bfloat16 [524288, 64], P('leaf')
All inputs are finite; a program needn't handle non-finite values.
Results may differ from a plain program's by a relative error of at most 0.017.
Values sent between devices are 32-bit elements; how exact they have to be, the bound alone decides.
No kernel may reach another device: no remote copies, remote signals or barrier semaphores. Data moves between devices by JAX's collectives and lax.ppermute only.
A program may use at most 64 MiB of HBM per device.

v0:
```python
import jax
import jax.numpy as jnp
from jax import lax
from jax.sharding import PartitionSpec as P


def partner(value, axis, apart):
    mask = 2**apart
    pairs = [(source, source ^ mask) for source in range(lax.axis_size(axis))]
    return lax.ppermute(value, axis, pairs)


def child_total(partial_value, count):
    total = partial_value
    for bit in range(count):
        total = total + partner(total, "leaf", bit)
    return total


def apply_level(state, basis, weight, group_bits):
    projected = lax.dot_general(
        basis,
        state.astype(jnp.bfloat16),
        (((0,), (0,)), ((), ())),
        preferred_element_type=jnp.float32,
    )
    child = child_total(projected, group_bits - 1)
    other = partner(child, "leaf", group_bits - 1)
    coeff = jnp.dot(weight.astype(jnp.float32), other, precision=lax.Precision.HIGHEST)
    return state - jnp.dot(basis, coeff.astype(jnp.bfloat16), preferred_element_type=jnp.float32)


def shards(rhs, leaf_inverse, bases, coupling):
    total_bits = lax.axis_size("leaf").bit_length() - 1
    levels = bases.shape[0]
    state = jnp.dot(leaf_inverse, rhs, preferred_element_type=jnp.float32)
    for level in range(levels):
        state = apply_level(state, bases[level], coupling[level], total_bits - levels + 1 + level)
    for level in reversed(range(levels)):
        state = apply_level(state, bases[level], coupling[level].T, total_bits - levels + 1 + level)
    solved = lax.dot_general(
        leaf_inverse,
        state.astype(jnp.bfloat16),
        (((0,), (0,)), ((), ())),
        preferred_element_type=jnp.float32,
    )
    return solved.astype(jnp.bfloat16)


def solution(mesh):
    placed = (P("leaf", None), P("leaf", None), P(None, "leaf", None), P())
    return jax.shard_map(
        shards, mesh=mesh, in_specs=placed, out_specs=P("leaf", None), check_vma=False
    )
```

profile of v0, /device:TPU:1, one launch (start us, length us, event | category | flops | bytes accessed | tf_op | source)
XLA Modules:
  0.0 228.6 jit_solution(2114286275335200717)
XLA Ops:
  1.0 6.1 %fusion.52 = f32[2048,64]{0,1:T(8,128)S(1)} fusion(bf16[2048,2048]{1,0:T(8,128)(2,1)} %param.5, bf16[2048,64]{0,1:T(8,128)(2,1)S(1)} %copy-done), kind=kOutput, calls=%fused_computation.69 | convolution fusion | flops 536870912 | bytes 9175040 | tf_op jit(solution)/shard_map/dot_general | solution.py:36
  7.4 3.3 %collective-permute-start = (f32[256,64]{0,1:T(8,128)S(1)}, f32[256,64]{0,1:T(8,128)S(1)}, u32[]{:S(2)}, u32[]{:S(2)}) collective-permute-start(f32[256,64]{0,1:T(8,128)S(1)} %convolution_bitcast_fusion.11), channel_id=1, source_target_pairs={{0,1},{1,0},{2,3},{3,2},{4,5},{5,4},{6,7},{7,6},{8,9},{9,8},{10,11... | collective-permute-start | bytes 196616 | tf_op jit(solution)/shard_map/ppermute | solution.py:10
  11.7 3.1 %collective-permute-done.1 = f32[256,64]{0,1:T(8,128)S(1)} collective-permute-done((f32[256,64]{0,1:T(8,128)S(1)}, f32[256,64]{0,1:T(8,128)S(1)}, u32[]{:S(2)}, u32[]{:S(2)}) %collective-permute-start.1) | collective-permute-done | bytes 65568 | tf_op jit(solution)/shard_map/ppermute | solution.py:10
  16.1 3.4 %collective-permute-done.2 = f32[256,64]{0,1:T(8,128)S(1)} collective-permute-done((f32[256,64]{0,1:T(8,128)S(1)}, f32[256,64]{0,1:T(8,128)S(1)}, u32[]{:S(2)}, u32[]{:S(2)}) %collective-permute-start.2) | collective-permute-done | bytes 65568 | tf_op jit(solution)/shard_map/ppermute | solution.py:10
  19.7 3.1 %collective-permute-done.3 = f32[256,64]{0,1:T(8,128)S(1)} collective-permute-done((f32[256,64]{0,1:T(8,128)S(1)}, f32[256,64]{0,1:T(8,128)S(1)}, u32[]{:S(2)}, u32[]{:S(2)}) %collective-permute-start.3) | collective-permute-done | bytes 65568 | tf_op jit(solution)/shard_map/ppermute | solution.py:10
  24.3 3.0 %collective-permute-done.4 = f32[256,64]{0,1:T(8,128)S(1)} collective-permute-done((f32[256,64]{0,1:T(8,128)S(1)}, f32[256,64]{0,1:T(8,128)S(1)}, u32[]{:S(2)}, u32[]{:S(2)}) %collective-permute-start.4) | collective-permute-done | bytes 65568 | tf_op jit(solution)/shard_map/ppermute | solution.py:10
  27.3 5.5 %collective-permute-start.5 = (f32[256,64]{0,1:T(8,128)S(1)}, f32[256,64]{0,1:T(8,128)S(1)}, u32[]{:S(2)}, u32[]{:S(2)}) collective-permute-start(f32[256,64]{0,1:T(8,128)S(1)} %add.112), channel_id=1, source_target_pairs={{0,32},{1,33},{2,34},{3,35},{4,36},{5,37},{6,38},{7,39},{8,40},{9,... | collective-permute-start | bytes 196616 | tf_op jit(solution)/shard_map/ppermute | solution.py:10
  35.6 6.3 %collective-permute-start.6 = (f32[256,64]{0,1:T(8,128)S(1)}, f32[256,64]{0,1:T(8,128)S(1)}, u32[]{:S(2)}, u32[]{:S(2)}) collective-permute-start(f32[256,64]{0,1:T(8,128)S(1)} %convolution_bitcast_fusion.10), channel_id=1, source_target_pairs={{0,1},{1,0},{2,3},{3,2},{4,5},{5,4},{6,7},{7,6},{8,9},{9,8},{10,11... | collective-permute-start | bytes 196616 | tf_op jit(solution)/shard_map/ppermute | solution.py:10
  58.5 5.8 %collective-permute-start.11 = (f32[256,64]{0,1:T(8,128)S(1)}, f32[256,64]{0,1:T(8,128)S(1)}, u32[]{:S(2)}, u32[]{:S(2)}) collective-permute-start(f32[256,64]{0,1:T(8,128)S(1)} %add.117), channel_id=1, source_target_pairs={{0,32},{1,33},{2,34},{3,35},{4,36},{5,37},{6,38},{7,39},{8,40},{9,... | collective-permute-start | bytes 196616 | tf_op jit(solution)/shard_map/ppermute | solution.py:10
  66.8 3.4 %collective-permute-done.12 = f32[256,64]{0,1:T(8,128)S(1)} collective-permute-done((f32[256,64]{0,1:T(8,128)S(1)}, f32[256,64]{0,1:T(8,128)S(1)}, u32[]{:S(2)}, u32[]{:S(2)}) %collective-permute-start.12) | collective-permute-done | bytes 65568 | tf_op jit(solution)/shard_map/ppermute | solution.py:10
  71.2 6.4 %collective-permute-start.13 = (f32[256,64]{0,1:T(8,128)S(1)}, f32[256,64]{0,1:T(8,128)S(1)}, u32[]{:S(2)}, u32[]{:S(2)}) collective-permute-start(f32[256,64]{0,1:T(8,128)S(1)} %convolution_bitcast_fusion.9), channel_id=1, source_target_pairs={{0,1},{1,0},{2,3},{3,2},{4,5},{5,4},{6,7},{7,6},{8,9},{9,8},{10,11... | collective-permute-start | bytes 196616 | tf_op jit(solution)/shard_map/ppermute | solution.py:10
  78.9 2.8 %collective-permute-done.14 = f32[256,64]{0,1:T(8,128)S(1)} collective-permute-done((f32[256,64]{0,1:T(8,128)S(1)}, f32[256,64]{0,1:T(8,128)S(1)}, u32[]{:S(2)}, u32[]{:S(2)}) %collective-permute-start.14) | collective-permute-done | bytes 65568 | tf_op jit(solution)/shard_map/ppermute | solution.py:10
  93.9 6.0 %collective-permute-start.18 = (f32[256,64]{0,1:T(8,128)S(1)}, f32[256,64]{0,1:T(8,128)S(1)}, u32[]{:S(2)}, u32[]{:S(2)}) collective-permute-start(f32[256,64]{0,1:T(8,128)S(1)} %add.123), channel_id=1, source_target_pairs={{0,32},{1,33},{2,34},{3,35},{4,36},{5,37},{6,38},{7,39},{8,40},{9,... | collective-permute-start | bytes 196616 | tf_op jit(solution)/shard_map/ppermute | solution.py:10
  111.3 8.0 %collective-permute-start.21 = (f32[256,64]{0,1:T(8,128)S(1)}, f32[256,64]{0,1:T(8,128)S(1)}, u32[]{:S(2)}, u32[]{:S(2)}) collective-permute-start(f32[256,64]{0,1:T(8,128)S(1)} %convolution_bitcast_fusion.8), channel_id=1, source_target_pairs={{0,1},{1,0},{2,3},{3,2},{4,5},{5,4},{6,7},{7,6},{8,9},{9,8},{10,11... | collective-permute-start | bytes 196616 | tf_op jit(solution)/shard_map/ppermute | solution.py:10
  136.3 5.5 %collective-permute-start.26 = (f32[256,64]{0,1:T(8,128)S(1)}, f32[256,64]{0,1:T(8,128)S(1)}, u32[]{:S(2)}, u32[]{:S(2)}) collective-permute-start(f32[256,64]{0,1:T(8,128)S(1)} %add.130), channel_id=1, source_target_pairs={{0,32},{1,33},{2,34},{3,35},{4,36},{5,37},{6,38},{7,39},{8,40},{9,... | collective-permute-start | bytes 196616 | tf_op jit(solution)/shard_map/ppermute | solution.py:10
  144.1 3.4 %collective-permute-done.27 = f32[256,64]{0,1:T(8,128)S(1)} collective-permute-done((f32[256,64]{0,1:T(8,128)S(1)}, f32[256,64]{0,1:T(8,128)S(1)}, u32[]{:S(2)}, u32[]{:S(2)}) %collective-permute-start.27) | collective-permute-done | bytes 65568 | tf_op jit(solution)/shard_map/ppermute | solution.py:10
  149.2 3.1 %collective-permute-done.28 = f32[256,64]{0,1:T(8,128)S(1)} collective-permute-done((f32[256,64]{0,1:T(8,128)S(1)}, f32[256,64]{0,1:T(8,128)S(1)}, u32[]{:S(2)}, u32[]{:S(2)}) %collective-permute-start.28) | collective-permute-done | bytes 65568 | tf_op jit(solution)/shard_map/ppermute | solution.py:10
  153.2 7.6 %collective-permute-start.29 = (f32[256,64]{0,1:T(8,128)S(1)}, f32[256,64]{0,1:T(8,128)S(1)}, u32[]{:S(2)}, u32[]{:S(2)}) collective-permute-start(f32[256,64]{0,1:T(8,128)S(1)} %convolution_bitcast_fusion.7), channel_id=1, source_target_pairs={{0,1},{1,0},{2,3},{3,2},{4,5},{5,4},{6,7},{7,6},{8,9},{9,8},{10,11... | collective-permute-start | bytes 196616 | tf_op jit(solution)/shard_map/ppermute | solution.py:10
  162.1 2.8 %collective-permute-done.30 = f32[256,64]{0,1:T(8,128)S(1)} collective-permute-done((f32[256,64]{0,1:T(8,128)S(1)}, f32[256,64]{0,1:T(8,128)S(1)}, u32[]{:S(2)}, u32[]{:S(2)}) %collective-permute-start.30) | collective-permute-done | bytes 65568 | tf_op jit(solution)/shard_map/ppermute | solution.py:10
  177.7 5.1 %collective-permute-start.34 = (f32[256,64]{0,1:T(8,128)S(1)}, f32[256,64]{0,1:T(8,128)S(1)}, u32[]{:S(2)}, u32[]{:S(2)}) collective-permute-start(f32[256,64]{0,1:T(8,128)S(1)} %add.137), channel_id=1, source_target_pairs={{0,32},{1,33},{2,34},{3,35},{4,36},{5,37},{6,38},{7,39},{8,40},{9,... | collective-permute-start | bytes 196616 | tf_op jit(solution)/shard_map/ppermute | solution.py:10
  186.4 2.9 %collective-permute-done.35 = f32[256,64]{0,1:T(8,128)S(1)} collective-permute-done((f32[256,64]{0,1:T(8,128)S(1)}, f32[256,64]{0,1:T(8,128)S(1)}, u32[]{:S(2)}, u32[]{:S(2)}) %collective-permute-start.35) | collective-permute-done | bytes 65568 | tf_op jit(solution)/shard_map/ppermute | solution.py:10
  191.0 6.4 %collective-permute-start.36 = (f32[256,64]{0,1:T(8,128)S(1)}, f32[256,64]{0,1:T(8,128)S(1)}, u32[]{:S(2)}, u32[]{:S(2)}) collective-permute-start(f32[256,64]{0,1:T(8,128)S(1)} %convolution_bitcast_fusion.6), channel_id=1, source_target_pairs={{0,1},{1,0},{2,3},{3,2},{4,5},{5,4},{6,7},{7,6},{8,9},{9,8},{10,11... | collective-permute-start | bytes 196616 | tf_op jit(solution)/shard_map/ppermute | solution.py:10
  214.3 5.7 %collective-permute-start.41 = (f32[256,64]{0,1:T(8,128)S(1)}, f32[256,64]{0,1:T(8,128)S(1)}, u32[]{:S(2)}, u32[]{:S(2)}) collective-permute-start(f32[256,64]{0,1:T(8,128)S(1)} %add.143), channel_id=1, source_target_pairs={{0,32},{1,33},{2,34},{3,35},{4,36},{5,37},{6,38},{7,39},{8,40},{9,... | collective-permute-start | bytes 196616 | tf_op jit(solution)/shard_map/ppermute | solution.py:10
  222.4 6.2 %fusion.7 = bf16[2048,64]{0,1:T(8,128)(2,1)} fusion(bf16[2048,2048]{1,0:T(8,128)(2,1)} %param.5, f32[2048,64]{0,1:T(8,128)} %copy-done.2, bf16[64,256]{1,0:T(8,128)(2,1)S(1)} %convolution_convert_fusion.1, bf16[3,2048,256]{2,1,0:T(8,128)(2,1)S(1)} %copy-done.1), kind=kOutput, calls=%fused_computation.14 | convolution fusion | flops 604372992 | bytes 10256384 | tf_op jit(solution)/shard_map/dot_general | solution.py:41
  (123 shorter events, 113.4 us)
Async XLA Ops:
  14.8 4.7 %collective-permute-start.2 = (f32[256,64]{0,1:T(8,128)S(1)}, f32[256,64]{0,1:T(8,128)S(1)}, u32[]{:S(2)}, u32[]{:S(2)}) collective-permute-start(f32[256,64]{0,1:T(8,128)S(1)} %add.109), channel_id=1, source_target_pairs={{0,4},{1,5},{2,6},{3,7},{4,0},{5,1},{6,2},{7,3},{8,12},{9,13},{10,... | collective-permute-start | bytes 196616 | tf_op jit(solution)/shard_map/ppermute | solution.py:10
  22.8 4.5 %collective-permute-start.4 = (f32[256,64]{0,1:T(8,128)S(1)}, f32[256,64]{0,1:T(8,128)S(1)}, u32[]{:S(2)}, u32[]{:S(2)}) collective-permute-start(f32[256,64]{0,1:T(8,128)S(1)} %add.111), channel_id=1, source_target_pairs={{0,16},{1,17},{2,18},{3,19},{4,20},{5,21},{6,22},{7,23},{8,24},{9,... | collective-permute-start | bytes 196616 | tf_op jit(solution)/shard_map/ppermute | solution.py:10
  27.3 7.2 %collective-permute-start.5 = (f32[256,64]{0,1:T(8,128)S(1)}, f32[256,64]{0,1:T(8,128)S(1)}, u32[]{:S(2)}, u32[]{:S(2)}) collective-permute-start(f32[256,64]{0,1:T(8,128)S(1)} %add.112), channel_id=1, source_target_pairs={{0,32},{1,33},{2,34},{3,35},{4,36},{5,37},{6,38},{7,39},{8,40},{9,... | collective-permute-start | bytes 196616 | tf_op jit(solution)/shard_map/ppermute | solution.py:10
  35.6 7.2 %collective-permute-start.6 = (f32[256,64]{0,1:T(8,128)S(1)}, f32[256,64]{0,1:T(8,128)S(1)}, u32[]{:S(2)}, u32[]{:S(2)}) collective-permute-start(f32[256,64]{0,1:T(8,128)S(1)} %convolution_bitcast_fusion.10), channel_id=1, source_target_pairs={{0,1},{1,0},{2,3},{3,2},{4,5},{5,4},{6,7},{7,6},{8,9},{9,8},{10,11... | collective-permute-start | bytes 196616 | tf_op jit(solution)/shard_map/ppermute | solution.py:10
  46.0 4.7 %collective-permute-start.8 = (f32[256,64]{0,1:T(8,128)S(1)}, f32[256,64]{0,1:T(8,128)S(1)}, u32[]{:S(2)}, u32[]{:S(2)}) collective-permute-start(f32[256,64]{0,1:T(8,128)S(1)} %add.114), channel_id=1, source_target_pairs={{0,4},{1,5},{2,6},{3,7},{4,0},{5,1},{6,2},{7,3},{8,12},{9,13},{10,... | collective-permute-start | bytes 196616 | tf_op jit(solution)/shard_map/ppermute | solution.py:10
  54.0 4.6 %collective-permute-start.10 = (f32[256,64]{0,1:T(8,128)S(1)}, f32[256,64]{0,1:T(8,128)S(1)}, u32[]{:S(2)}, u32[]{:S(2)}) collective-permute-start(f32[256,64]{0,1:T(8,128)S(1)} %add.116), channel_id=1, source_target_pairs={{0,16},{1,17},{2,18},{3,19},{4,20},{5,21},{6,22},{7,23},{8,24},{9,... | collective-permute-start | bytes 196616 | tf_op jit(solution)/shard_map/ppermute | solution.py:10
  58.5 8.2 %collective-permute-start.11 = (f32[256,64]{0,1:T(8,128)S(1)}, f32[256,64]{0,1:T(8,128)S(1)}, u32[]{:S(2)}, u32[]{:S(2)}) collective-permute-start(f32[256,64]{0,1:T(8,128)S(1)} %add.117), channel_id=1, source_target_pairs={{0,32},{1,33},{2,34},{3,35},{4,36},{5,37},{6,38},{7,39},{8,40},{9,... | collective-permute-start | bytes 196616 | tf_op jit(solution)/shard_map/ppermute | solution.py:10
  71.2 7.3 %collective-permute-start.13 = (f32[256,64]{0,1:T(8,128)S(1)}, f32[256,64]{0,1:T(8,128)S(1)}, u32[]{:S(2)}, u32[]{:S(2)}) collective-permute-start(f32[256,64]{0,1:T(8,128)S(1)} %convolution_bitcast_fusion.9), channel_id=1, source_target_pairs={{0,1},{1,0},{2,3},{3,2},{4,5},{5,4},{6,7},{7,6},{8,9},{9,8},{10,11... | collective-permute-start | bytes 196616 | tf_op jit(solution)/shard_map/ppermute | solution.py:10
  81.7 4.7 %collective-permute-start.15 = (f32[256,64]{0,1:T(8,128)S(1)}, f32[256,64]{0,1:T(8,128)S(1)}, u32[]{:S(2)}, u32[]{:S(2)}) collective-permute-start(f32[256,64]{0,1:T(8,128)S(1)} %add.120), channel_id=1, source_target_pairs={{0,4},{1,5},{2,6},{3,7},{4,0},{5,1},{6,2},{7,3},{8,12},{9,13},{10,... | collective-permute-start | bytes 196616 | tf_op jit(solution)/shard_map/ppermute | solution.py:10
  93.9 8.1 %collective-permute-start.18 = (f32[256,64]{0,1:T(8,128)S(1)}, f32[256,64]{0,1:T(8,128)S(1)}, u32[]{:S(2)}, u32[]{:S(2)}) collective-permute-start(f32[256,64]{0,1:T(8,128)S(1)} %add.123), channel_id=1, source_target_pairs={{0,32},{1,33},{2,34},{3,35},{4,36},{5,37},{6,38},{7,39},{8,40},{9,... | collective-permute-start | bytes 196616 | tf_op jit(solution)/shard_map/ppermute | solution.py:10
  105.6 4.7 %collective-permute-start.20 = (f32[256,64]{0,1:T(8,128)S(1)}, f32[256,64]{0,1:T(8,128)S(1)}, u32[]{:S(2)}, u32[]{:S(2)}) collective-permute-start(f32[256,64]{0,1:T(8,128)S(1)} %add.125), channel_id=1, source_target_pairs={{0,128},{1,129},{2,130},{3,131},{4,132},{5,133},{6,134},{7,135},{8... | collective-permute-start | bytes 196616 | tf_op jit(solution)/shard_map/ppermute | solution.py:10
  111.3 8.9 %collective-permute-start.21 = (f32[256,64]{0,1:T(8,128)S(1)}, f32[256,64]{0,1:T(8,128)S(1)}, u32[]{:S(2)}, u32[]{:S(2)}) collective-permute-start(f32[256,64]{0,1:T(8,128)S(1)} %convolution_bitcast_fusion.8), channel_id=1, source_target_pairs={{0,1},{1,0},{2,3},{3,2},{4,5},{5,4},{6,7},{7,6},{8,9},{9,8},{10,11... | collective-permute-start | bytes 196616 | tf_op jit(solution)/shard_map/ppermute | solution.py:10
  123.4 4.7 %collective-permute-start.23 = (f32[256,64]{0,1:T(8,128)S(1)}, f32[256,64]{0,1:T(8,128)S(1)}, u32[]{:S(2)}, u32[]{:S(2)}) collective-permute-start(f32[256,64]{0,1:T(8,128)S(1)} %add.127), channel_id=1, source_target_pairs={{0,4},{1,5},{2,6},{3,7},{4,0},{5,1},{6,2},{7,3},{8,12},{9,13},{10,... | collective-permute-start | bytes 196616 | tf_op jit(solution)/shard_map/ppermute | solution.py:10
  131.4 5.0 %collective-permute-start.25 = (f32[256,64]{0,1:T(8,128)S(1)}, f32[256,64]{0,1:T(8,128)S(1)}, u32[]{:S(2)}, u32[]{:S(2)}) collective-permute-start(f32[256,64]{0,1:T(8,128)S(1)} %add.129), channel_id=1, source_target_pairs={{0,16},{1,17},{2,18},{3,19},{4,20},{5,21},{6,22},{7,23},{8,24},{9,... | collective-permute-start | bytes 196616 | tf_op jit(solution)/shard_map/ppermute | solution.py:10
  136.3 7.7 %collective-permute-start.26 = (f32[256,64]{0,1:T(8,128)S(1)}, f32[256,64]{0,1:T(8,128)S(1)}, u32[]{:S(2)}, u32[]{:S(2)}) collective-permute-start(f32[256,64]{0,1:T(8,128)S(1)} %add.130), channel_id=1, source_target_pairs={{0,32},{1,33},{2,34},{3,35},{4,36},{5,37},{6,38},{7,39},{8,40},{9,... | collective-permute-start | bytes 196616 | tf_op jit(solution)/shard_map/ppermute | solution.py:10
  147.5 4.7 %collective-permute-start.28 = (f32[256,64]{0,1:T(8,128)S(1)}, f32[256,64]{0,1:T(8,128)S(1)}, u32[]{:S(2)}, u32[]{:S(2)}) collective-permute-start(f32[256,64]{0,1:T(8,128)S(1)} %add.132), channel_id=1, source_target_pairs={{0,128},{1,129},{2,130},{3,131},{4,132},{5,133},{6,134},{7,135},{8... | collective-permute-start | bytes 196616 | tf_op jit(solution)/shard_map/ppermute | solution.py:10
  153.2 8.5 %collective-permute-start.29 = (f32[256,64]{0,1:T(8,128)S(1)}, f32[256,64]{0,1:T(8,128)S(1)}, u32[]{:S(2)}, u32[]{:S(2)}) collective-permute-start(f32[256,64]{0,1:T(8,128)S(1)} %convolution_bitcast_fusion.7), channel_id=1, source_target_pairs={{0,1},{1,0},{2,3},{3,2},{4,5},{5,4},{6,7},{7,6},{8,9},{9,8},{10,11... | collective-permute-start | bytes 196616 | tf_op jit(solution)/shard_map/ppermute | solution.py:10
  164.9 4.7 %collective-permute-start.31 = (f32[256,64]{0,1:T(8,128)S(1)}, f32[256,64]{0,1:T(8,128)S(1)}, u32[]{:S(2)}, u32[]{:S(2)}) collective-permute-start(f32[256,64]{0,1:T(8,128)S(1)} %add.134), channel_id=1, source_target_pairs={{0,4},{1,5},{2,6},{3,7},{4,0},{5,1},{6,2},{7,3},{8,12},{9,13},{10,... | collective-permute-start | bytes 196616 | tf_op jit(solution)/shard_map/ppermute | solution.py:10
  172.8 4.9 %collective-permute-start.33 = (f32[256,64]{0,1:T(8,128)S(1)}, f32[256,64]{0,1:T(8,128)S(1)}, u32[]{:S(2)}, u32[]{:S(2)}) collective-permute-start(f32[256,64]{0,1:T(8,128)S(1)} %add.136), channel_id=1, source_target_pairs={{0,16},{1,17},{2,18},{3,19},{4,20},{5,21},{6,22},{7,23},{8,24},{9,... | collective-permute-start | bytes 196616 | tf_op jit(solution)/shard_map/ppermute | solution.py:10
  177.7 7.8 %collective-permute-start.34 = (f32[256,64]{0,1:T(8,128)S(1)}, f32[256,64]{0,1:T(8,128)S(1)}, u32[]{:S(2)}, u32[]{:S(2)}) collective-permute-start(f32[256,64]{0,1:T(8,128)S(1)} %add.137), channel_id=1, source_target_pairs={{0,32},{1,33},{2,34},{3,35},{4,36},{5,37},{6,38},{7,39},{8,40},{9,... | collective-permute-start | bytes 196616 | tf_op jit(solution)/shard_map/ppermute | solution.py:10
  191.0 7.3 %collective-permute-start.36 = (f32[256,64]{0,1:T(8,128)S(1)}, f32[256,64]{0,1:T(8,128)S(1)}, u32[]{:S(2)}, u32[]{:S(2)}) collective-permute-start(f32[256,64]{0,1:T(8,128)S(1)} %convolution_bitcast_fusion.6), channel_id=1, source_target_pairs={{0,1},{1,0},{2,3},{3,2},{4,5},{5,4},{6,7},{7,6},{8,9},{9,8},{10,11... | collective-permute-start | bytes 196616 | tf_op jit(solution)/shard_map/ppermute | solution.py:10
  201.5 4.7 %collective-permute-start.38 = (f32[256,64]{0,1:T(8,128)S(1)}, f32[256,64]{0,1:T(8,128)S(1)}, u32[]{:S(2)}, u32[]{:S(2)}) collective-permute-start(f32[256,64]{0,1:T(8,128)S(1)} %add.140), channel_id=1, source_target_pairs={{0,4},{1,5},{2,6},{3,7},{4,0},{5,1},{6,2},{7,3},{8,12},{9,13},{10,... | collective-permute-start | bytes 196616 | tf_op jit(solution)/shard_map/ppermute | solution.py:10
  209.5 4.8 %collective-permute-start.40 = (f32[256,64]{0,1:T(8,128)S(1)}, f32[256,64]{0,1:T(8,128)S(1)}, u32[]{:S(2)}, u32[]{:S(2)}) collective-permute-start(f32[256,64]{0,1:T(8,128)S(1)} %add.142), channel_id=1, source_target_pairs={{0,16},{1,17},{2,18},{3,19},{4,20},{5,21},{6,22},{7,23},{8,24},{9,... | collective-permute-start | bytes 196616 | tf_op jit(solution)/shard_map/ppermute | solution.py:10
  214.3 7.9 %collective-permute-start.41 = (f32[256,64]{0,1:T(8,128)S(1)}, f32[256,64]{0,1:T(8,128)S(1)}, u32[]{:S(2)}, u32[]{:S(2)}) collective-permute-start(f32[256,64]{0,1:T(8,128)S(1)} %add.143), channel_id=1, source_target_pairs={{0,32},{1,33},{2,34},{3,35},{4,36},{5,37},{6,38},{7,39},{8,40},{9,... | collective-permute-start | bytes 196616 | tf_op jit(solution)/shard_map/ppermute | solution.py:10
  (22 other events, 103.6 us)
where the time goes:
time: 232 us; the launch traced here: 229 us
  starting transfers between devices  110 us (47%)
  waiting for transfers between devices  98.2 us (42%)
  matrix products  17.7 us (8%)
    ppermute x42, starting transfers between devices, partner(): return lax.ppermute(value, axis, pairs)  110 us
    ppermute x42, waiting for transfers between devices, partner(): return lax.ppermute(value, axis, pairs)  98.2 us
    dot_general x1, matrix products, shards(): lax.dot_general(leaf_inverse, state.astype(jnp.bfloat16), (((0,), (0,)),...  6.18 us
    dot_general x1, matrix products, shards(): state = jnp.dot(leaf_inverse, rhs, preferred_element_type=jnp.float32)  6.11 us
  transfers between devices with their start and end apart: 42, of which 42 were waited for; matrix products, arithmetic and copies ran while one was open for 0% of the time, Pallas kernels for 0%

commit v1 on v0

v1 whole, which is shorter than its diff:
```python
import jax
import jax.numpy as jnp
from jax import lax
from jax.experimental import pallas as pl
from jax.experimental.pallas import tpu as pltpu
from jax.sharding import PartitionSpec as P

F32, BF16 = jnp.float32, jnp.bfloat16
AXIS = "leaf"
N = 256
CHIPS = 128
SMEM, VMEM = pltpu.SMEM, pltpu.VMEM
BLOCK = 256


def params(mib):
    return pltpu.CompilerParams(vmem_limit_bytes=mib << 20)


def cost(flops, size):
    return pl.CostEstimate(flops=flops, bytes_accessed=size, transcendentals=0)


def whole(count, space=None):
    return [pl.BlockSpec(memory_space=space or VMEM)] * count


def dot(a, b, dims=((1,), (0,))):
    return lax.dot_general(a, b, (dims, ((), ())), preferred_element_type=F32)


def high(a, b, dims=((1,), (0,))):
    return lax.dot_general(a, b, (dims, ((), ())), precision=lax.Precision.HIGHEST, preferred_element_type=F32)


NT, TN = ((1,), (1,)), ((0,), (0,))


def rounded(value):
    return value.astype(BF16).astype(F32)


def swap(value, mask):
    return lax.ppermute(value, AXIS, [(i, i ^ mask) for i in range(N)])


def line(size, stride):
    return [
        [base + low + stride * k for k in range(size)]
        for base in range(0, N, size * stride)
        for low in range(stride)
    ]


def over_chips(value):
    return lax.all_to_all(value, AXIS, 0, 0, axis_index_groups=line(CHIPS, 2), tiled=True)


def pick(index, low, high):
    return jnp.where(index == 0, low, high)


def xor_order(parts, y):
    a, b, c, d = parts
    one = y & 1
    a, b, c, d = pick(one, a, b), pick(one, b, a), pick(one, c, d), pick(one, d, c)
    two = y & 2
    return pick(two, a, c), pick(two, b, d), pick(two, c, a), pick(two, d, b)


def halve(value, core):
    half = value.shape[0] // 2
    low, high_ = value[:half], value[half:]
    return pick(core, low, high_) + swap(pick(core, high_, low), 1)


def unhalve(value, core):
    other = swap(value, 1)
    return jnp.concatenate([pick(core, value, other), pick(core, other, value)], axis=0)


def gram_kernel(core_ref, u_ref, keep_ref, send_ref, acc):
    step = pl.program_id(0)
    rank = u_ref.shape[2]

    @pl.when(step == 0)
    def _():
        acc[...] = jnp.zeros_like(acc)

    for place, (a, b) in enumerate(((1, 0), (1, 1), (1, 2), (2, 0), (2, 2))):
        acc[:, place * rank : (place + 1) * rank] += dot(u_ref[a], u_ref[b], TN)

    @pl.when(step == pl.num_programs(0) - 1)
    def _():
        half = rank // 2
        low = core_ref[0] == 0
        keep_ref[...] = jnp.where(low, acc[:half], acc[half:])
        send_ref[...] = jnp.where(low, acc[half:], acc[:half])


def gram(core, bases):
    levels, leaf, rank = bases.shape
    rows = min(512, leaf)
    shape = jax.ShapeDtypeStruct((rank // 2, 5 * rank), F32)
    return pl.pallas_call(
        gram_kernel,
        grid=(leaf // rows,),
        in_specs=[
            pl.BlockSpec(memory_space=SMEM),
            pl.BlockSpec((levels, rows, rank), lambda i: (0, i, 0)),
        ],
        out_specs=[pl.BlockSpec((rank // 2, 5 * rank), lambda i: (0, 0))] * 2,
        out_shape=[shape, shape],
        scratch_shapes=[pltpu.VMEM((rank, 5 * rank), F32)],
        compiler_params=params(32),
        cost_estimate=cost(10 * leaf * rank * rank, 6 * leaf * rank),
        name="gram",
    )(core, bases)


def table_kernel(rows_ref, out_ref):
    width = rows_ref.shape[2]
    rank = width // 5
    sub = [rows_ref[16 * c : 16 * c + 16].sum(axis=0) for c in range(8)]
    node = [sub[2 * c] + sub[2 * c + 1] for c in range(4)]
    child = [node[0] + node[1], node[2] + node[3]]
    for c in range(8):
        other, beside, across = sub[c ^ 1], node[(c >> 1) ^ 1], child[(c >> 2) ^ 1]
        row = jnp.concatenate(
            [
                other[:, :rank],
                beside[:, rank : 3 * rank],
                other[:, 3 * rank : 4 * rank],
                across[:, 4 * rank :],
            ],
            axis=1,
        )
        out_ref[16 * c : 16 * c + 16] = jnp.broadcast_to(row[None], (16, 1, width))


def table(rows):
    return pl.pallas_call(
        table_kernel,
        in_specs=whole(1),
        out_specs=whole(1)[0],
        out_shape=jax.ShapeDtypeStruct(rows.shape, F32),
        compiler_params=params(32),
        cost_estimate=cost(rows.size, 8 * rows.size),
        name="table",
    )(rows)


def first_kernel(b_ref, f_ref, u_ref, z_ref, p_ref, bt):
    step = pl.program_id(0)

    @pl.when(step == 0)
    def _():
        bt[...] = b_ref[...].astype(F32).T.astype(BF16)
        p_ref[...] = jnp.zeros_like(p_ref)

    z = dot(bt[...], f_ref[...], NT)
    z_ref[...] = z
    p_ref[...] += dot(z.astype(BF16), u_ref[0])


def first(rhs, inverse, bases):
    leaf, cols = rhs.shape
    rank = bases.shape[2]
    return pl.pallas_call(
        first_kernel,
        grid=(leaf // BLOCK,),
        in_specs=[
            pl.BlockSpec((leaf, cols), lambda i: (0, 0)),
            pl.BlockSpec((BLOCK, leaf), lambda i: (i, 0)),
            pl.BlockSpec((1, BLOCK, rank), lambda i: (0, i, 0)),
        ],
        out_specs=[
            pl.BlockSpec((cols, BLOCK), lambda i: (0, i)),
            pl.BlockSpec((cols, rank), lambda i: (0, 0)),
        ],
        out_shape=[
            jax.ShapeDtypeStruct((cols, leaf), F32),
            jax.ShapeDtypeStruct((cols, rank), F32),
        ],
        scratch_shapes=[pltpu.VMEM((cols, leaf), BF16)],
        compiler_params=params(32),
        cost_estimate=cost(2 * leaf * leaf * cols, 2 * leaf * leaf),
        name="first",
    )(rhs, inverse, bases)


def project_kernel(q_ref, u_ref, z_ref, new_ref, s_ref):
    rank = u_ref.shape[2]
    new = z_ref[...] - dot(q_ref[...].astype(BF16), u_ref[0], NT)
    new_ref[...] = new
    zb = new.astype(BF16)
    for level in range(3):
        s_ref[:, level * rank : (level + 1) * rank] = dot(zb, u_ref[level])


def project(q, bases, state):
    cols, leaf = state.shape
    rank = bases.shape[2]
    return pl.pallas_call(
        project_kernel,
        in_specs=whole(3),
        out_specs=whole(2),
        out_shape=[
            jax.ShapeDtypeStruct((cols, leaf), F32),
            jax.ShapeDtypeStruct((cols, 3 * rank), F32),
        ],
        compiler_params=params(32),
        cost_estimate=cost(8 * leaf * rank * cols, 6 * leaf * rank),
        name="project",
    )(q, bases, state)


def last_kernel(q_ref, u_ref, z_ref, f_ref, out_ref, acc):
    step = pl.program_id(0)
    rank = u_ref.shape[2]

    @pl.when(step == 0)
    def _():
        acc[...] = jnp.zeros_like(acc)

    z = z_ref[...]
    for level in range(3):
        z -= dot(q_ref[:, level * rank : (level + 1) * rank].astype(BF16), u_ref[level], NT)
    acc[...] += dot(z.astype(BF16), f_ref[...])

    @pl.when(step == pl.num_programs(0) - 1)
    def _():
        out_ref[...] = acc[...].T.astype(BF16)


def last(q, bases, state, inverse):
    cols, leaf = state.shape
    rank = bases.shape[2]
    return pl.pallas_call(
        last_kernel,
        grid=(leaf // BLOCK,),
        in_specs=[
            pl.BlockSpec((cols, 3 * rank), lambda i: (0, 0)),
            pl.BlockSpec((3, BLOCK, rank), lambda i: (0, i, 0)),
            pl.BlockSpec((cols, BLOCK), lambda i: (0, i)),
            pl.BlockSpec((BLOCK, leaf), lambda i: (i, 0)),
        ],
        out_specs=pl.BlockSpec((leaf, cols), lambda i: (0, 0)),
        out_shape=jax.ShapeDtypeStruct((leaf, cols), BF16),
        scratch_shapes=[pltpu.VMEM((cols, leaf), F32)],
        compiler_params=params(32),
        cost_estimate=cost(2 * leaf * leaf * cols, 2 * leaf * leaf),
        name="last",
    )(q, bases, state, inverse)


def shards(rhs, leaf_inverse, bases, coupling):
    index = lax.axis_index(AXIS)
    core, y = index & 1, (index >> 1) & 3
    rank, cols = bases.shape[2], rhs.shape[1]
    w0, w1, w2 = (coupling[k].astype(F32) for k in range(3))

    keep, send = gram(core.reshape(1), bases)
    mine = (keep + swap(send, 1)).reshape(CHIPS, 1, 5 * rank)
    mine, rhs = lax.optimization_barrier((mine, rhs))
    back = over_chips(table(over_chips(mine))).reshape(CHIPS, 5 * rank)
    sums = unhalve(back, core)
    m10, m11, m12, m20, m22 = (sums[:, k * rank : (k + 1) * rank] for k in range(5))

    state, proj = first(rhs, leaf_inverse, bases)

    half = halve(proj, core)
    half = half + swap(half, 2) + swap(half, 4) + swap(half, 6)
    pair = half + swap(half, 8)
    other = swap(pair, 40) + swap(pair, 56)
    q0 = unhalve(high(other, w0, NT), core)

    state, proj = project(q0, bases, state)
    half = halve(proj, core)
    eighth = cols // 8
    parts = xor_order([half[k * eighth : (k + 1) * eighth] for k in range(4)], y)
    part = parts[0] + swap(parts[1], 2) + swap(parts[2], 4) + swap(parts[3], 6)
    pair = part + swap(part, 8)
    own = pair[:, rank:] + swap(pair[:, rank:], 16)
    other = swap(pair, 40) + swap(pair, 56)
    s0o, node = other[:, :rank], own + other[:, rank:]
    s1, s2 = node[:, :rank], node[:, rank:]

    q1o = high(s1, w1, NT)
    v = s2 - high(rounded(q1o), m12)
    beside = swap(jnp.concatenate([v, s1], axis=1), 64)
    c2, s1o = v + beside[:, :rank], beside[:, rank:]
    c2o = swap(v, 128) + swap(v, 192)
    q1 = high(s1o, w1, NT)
    q2 = high(c2o, w2, NT)
    q2o = high(c2, w2, NT)
    t2 = q2 + high(c2o - high(rounded(q2o), m22), w2)
    t1 = q1 + high(s1o - high(rounded(q1o), m11) - high(rounded(t2), m12, NT), w1)
    t0 = high(s0o - high(rounded(t1), m10) - high(rounded(t2), m20), w0)

    mine = jnp.concatenate([t0, t1, t2], axis=1)
    parts = [mine, swap(mine, 2), swap(mine, 4), swap(mine, 6)]
    half = jnp.concatenate(xor_order(parts, y), axis=0)
    return last(unhalve(half, core), bases, state, leaf_inverse)


def solution(mesh):
    placed = (P(AXIS, None), P(AXIS, None), P(None, AXIS, None), P())
    return jax.shard_map(
        shards, mesh=mesh, in_specs=placed, out_specs=P(AXIS, None), check_vma=False
    )
```

time: 232 us -> 136 us (0.59); the launches traced: 229 us -> 135 us
  waiting for transfers between devices: 98.2 us -> 21.4 us
  starting transfers between devices: 110 us -> 71.7 us
  local copies, waits for them, and re-layouts: 1.74 us -> 19.9 us
  Pallas kernels: 0 us -> 15 us
  matrix products: 17.7 us -> 3.88 us
  other arithmetic: 0.34 us -> 2.93 us
    ppermute x42 -> x25, waiting for transfers between devices: 98.2 us -> 20.6 us  [swap(): return lax.ppermute(value, AXIS, [(i, i ^ mask) for i in range(N)])]
    ppermute x42 -> x25, starting transfers between devices: 110 us -> 46.1 us  [swap(): return lax.ppermute(value, AXIS, [(i, i ^ mask) for i in range(N)])]
    all_to_all x0 -> x2, starting transfers between devices: none -> 25.5 us  [over_chips(): lax.all_to_all(value, AXIS, 0, 0, axis_index_groups=line(CHIPS, 2), tiled...]
    pallas_call x0 -> x5, Pallas kernels: none -> 15 us  [the longest x1 5.16 us: last(): pl.pallas_call(last_kernel, grid=(leaf // BLOCK,), in_specs=[pl.BlockSpec...]
    unnamed x8 -> x31, local copies, waits for them, and re-layouts: 1.74 us -> 15.7 us
    dot_general x19 -> x14, matrix products: 17.7 us -> 3.88 us  [high(): lax.dot_general(a, b, (dims, ((), ())), precision=lax.Precision.HIGHEST,...]
  transfers between devices with their start and end apart: 42 -> 27, of which waited for: 42 -> 17; matrix products, arithmetic and copies ran while one was open for 0% -> 4% of each run, Pallas kernels for 0% -> 5%
where the time goes in v1:
time: 136 us; the launch traced here: 135 us
  starting transfers between devices  71.7 us (53%)
  waiting for transfers between devices  21.4 us (16%)
  local copies, waits for them, and re-layouts  19.9 us (15%)
  Pallas kernels  15 us (11%)
  matrix products  3.88 us (3%)
  other arithmetic  2.93 us (2%)
    ppermute x25, starting transfers between devices, swap(): return lax.ppermute(value, AXIS, [(i, i ^ mask) for i in range(N)])  46.1 us
    all_to_all x2, starting transfers between devices, over_chips(): lax.all_to_all(value, AXIS, 0, 0, axis_index_groups=line(CHIPS, 2), tiled...  25.5 us
    ppermute x25, waiting for transfers between devices, swap(): return lax.ppermute(value, AXIS, [(i, i ^ mask) for i in range(N)])  20.6 us
    unnamed x31, local copies, waits for them, and re-layouts  15.7 us
    pallas_call x1, Pallas kernels, last(): pl.pallas_call(last_kernel, grid=(leaf // BLOCK,), in_specs=[pl.BlockSpec...  5.16 us
    pallas_call x1, Pallas kernels, first(): pl.pallas_call(first_kernel, grid=(leaf // BLOCK,), in_specs=[pl.BlockSpe...  4.71 us
    dot_general x14, matrix products, high(): lax.dot_general(a, b, (dims, ((), ())), precision=lax.Precision.HIGHEST,...  3.88 us
  transfers between devices with their start and end apart: 27, of which 17 were waited for; matrix products, arithmetic and copies ran while one was open for 4% of the time, Pallas kernels for 5%

profile of v1, /device:TPU:1, one launch (start us, length us, event | category | flops | bytes accessed | tf_op | source)
XLA Modules:
  0.0 135.1 jit_solution(11066769703990258511)
XLA Ops:
  0.0 1.9 %copy-done.2 = bf16[3,2048,256]{2,1,0:T(8,128)(2,1)S(1)} copy-done((bf16[3,2048,256]{2,1,0:T(8,128)(2,1)S(1)}, bf16[3,2048,256]{2,1,0:T(8,128)(2,1)}, u32[]{:S(2)}) %copy-start.2) | copy-done | bytes 3145752
  1.9 2.7 %gram.1 = (f32[128,1280]{1,0:T(8,128)S(1)}, f32[128,1280]{1,0:T(8,128)S(1)}) custom-call(s32[1]{0:T(128)} %bitcast.core_ref, bf16[3,2048,256]{2,1,0:T(8,128)(2,1)S(1)} %copy-done.2), custom_call_target="tpu_custom_call" | custom-call | flops 1342177280 | bytes 3145728 | tf_op jit(solution)/shard_map/gram/pallas_call | solution.py:105
  4.6 3.3 %collective-permute-start = (f32[128,1280]{1,0:T(8,128)S(1)}, f32[128,1280]{1,0:T(8,128)S(1)}, u32[]{:S(2)}, u32[]{:S(2)}) collective-permute-start(f32[128,1280]{1,0:T(8,128)S(1)} %get-tuple-element.14), channel_id=1, source_target_pairs={{0,1},{1,0},{2,3},{3,2},{4,5},{5,4},{6,7},{7,6},{8,9},{9,8},{10,11... | collective-permute-start | bytes 1966088 | tf_op jit(solution)/shard_map/ppermute | solution.py:44
  11.0 14.2 %all-to-all-start = ((f32[128,1,1280]{2,1,0:T(1,128)}), f32[128,1,1280]{2,1,0:T(1,128)}, u32[]{:S(2)}, u32[]{:S(2)}) async-start(f32[128,1,1280]{2,1,0:T(1,128)} %reshape.10), calls=%async_computation | async-start | bytes 1310720 | tf_op jit(solution)/shard_map/all_to_all | solution.py:56
  26.3 3.4 %copy-done = bf16[2048,2048]{1,0:T(8,128)(2,1)S(1)} copy-done((bf16[2048,2048]{1,0:T(8,128)(2,1)S(1)}, bf16[2048,2048]{1,0:T(8,128)(2,1)}, u32[]{:S(2)}) %copy-start) | copy-done | bytes 8388632
  30.7 4.7 %first.1 = (f32[64,2048]{1,0:T(8,128)S(1)}, f32[64,256]{1,0:T(8,128)S(1)}) custom-call(bf16[2048,64]{1,0:T(8,128)(2,1)S(1)} %copy-done.5, bf16[2048,2048]{1,0:T(8,128)(2,1)S(1)} %copy-done, bf16[3,2048,256]{2,1,0:T(8,128)(2,1)S(1)} %copy-done.3), custom_call_target="tpu_custom_call" | custom-call | flops 536870912 | bytes 8388608 | tf_op jit(solution)/shard_map/first/pallas_call | solution.py:169
  37.8 2.0 %collective-permute-start.4 = (f32[32,256]{1,0:T(8,128)S(1)}, f32[32,256]{1,0:T(8,128)S(1)}, u32[]{:S(2)}, u32[]{:S(2)}) collective-permute-start(f32[32,256]{1,0:T(8,128)S(1)} %select_add_fusion.1), channel_id=1, source_target_pairs={{0,6},{1,7},{2,4},{3,5},{4,2},{5,3},{6,0},{7,1},{8,14},{9,15},{10,... | collective-permute-start | bytes 98312 | tf_op jit(solution)/shard_map/ppermute | solution.py:44
  42.5 2.2 %collective-permute-done.3 = f32[32,256]{1,0:T(8,128)S(1)} collective-permute-done((f32[32,256]{1,0:T(8,128)S(1)}, f32[32,256]{1,0:T(8,128)S(1)}, u32[]{:S(2)}, u32[]{:S(2)}) %collective-permute-start.3) | collective-permute-done | bytes 32800 | tf_op jit(solution)/shard_map/ppermute | solution.py:44
  47.6 2.2 %collective-permute-start.7 = (f32[32,256]{1,0:T(8,128)S(1)}, f32[32,256]{1,0:T(8,128)S(1)}, u32[]{:S(2)}, u32[]{:S(2)}) collective-permute-start(f32[32,256]{1,0:T(8,128)S(1)} %add.62), channel_id=1, source_target_pairs={{0,56},{1,57},{2,58},{3,59},{4,60},{5,61},{6,62},{7,63},{8,48},{9,... | collective-permute-start | bytes 98312 | tf_op jit(solution)/shard_map/ppermute | solution.py:44
  49.8 3.0 %collective-permute-start.6 = (f32[32,256]{1,0:T(8,128)S(1)}, f32[32,256]{1,0:T(8,128)S(1)}, u32[]{:S(2)}, u32[]{:S(2)}) collective-permute-start(f32[32,256]{1,0:T(8,128)S(1)} %add.62), channel_id=1, source_target_pairs={{0,40},{1,41},{2,42},{3,43},{4,44},{5,45},{6,46},{7,47},{8,32},{9,... | collective-permute-start | bytes 98312 | tf_op jit(solution)/shard_map/ppermute | solution.py:44
  55.1 11.3 %all-to-all-start.1 = ((f32[128,1,1280]{2,1,0:T(1,128)}), f32[128,1,1280]{2,1,0:T(1,128)}, u32[]{:S(2)}, u32[]{:S(2)}) async-start(f32[128,1,1280]{2,1,0:T(1,128)} %copy-done.4), calls=%async_computation.1 | async-start | bytes 1310720 | tf_op jit(solution)/shard_map/all_to_all | solution.py:56
  67.6 3.9 %collective-permute-start.8 = (f32[32,256]{1,0:T(8,128)S(1)}, f32[32,256]{1,0:T(8,128)S(1)}, u32[]{:S(2)}, u32[]{:S(2)}) collective-permute-start(f32[32,256]{1,0:T(8,128)S(1)} %fusion.21), channel_id=1, source_target_pairs={{0,1},{1,0},{2,3},{3,2},{4,5},{5,4},{6,7},{7,6},{8,9},{9,8},{10,11... | collective-permute-start | bytes 98312 | tf_op jit(solution)/shard_map/ppermute | solution.py:44
  78.7 2.4 %collective-permute-start.11 = (f32[8,768]{1,0:T(8,128)}, f32[8,768]{1,0:T(8,128)}, u32[]{:S(2)}, u32[]{:S(2)}) collective-permute-start(f32[8,768]{1,0:T(8,128)} %get-tuple-element.30), channel_id=1, source_target_pairs={{0,4},{1,5},{2,6},{3,7},{4,0},{5,1},{6,2},{7,3},{8,12},{9,13},{10,... | collective-permute-start | bytes 73736 | tf_op jit(solution)/shard_map/ppermute | solution.py:44
  83.7 6.5 %collective-permute-start.17 = (f32[128,1280]{1,0:T(8,128)S(1)}, f32[128,1280]{1,0:T(8,128)S(1)}, u32[]{:S(2)}, u32[]{:S(2)}) collective-permute-start(f32[128,1280]{1,0:T(8,128)S(1)} %bitcast.34), channel_id=1, source_target_pairs={{0,1},{1,0},{2,3},{3,2},{4,5},{5,4},{6,7},{7,6},{8,9},{9,8},{10,11... | collective-permute-start | bytes 1966088 | tf_op jit(solution)/shard_map/ppermute | solution.py:44
  91.9 1.9 %collective-permute-done.13 = f32[8,768]{1,0:T(8,128)S(1)} collective-permute-done((f32[8,768]{1,0:T(8,128)S(1)}, f32[8,768]{1,0:T(8,128)S(1)}, u32[]{:S(2)}, u32[]{:S(2)}) %collective-permute-start.13) | collective-permute-done | bytes 24608 | tf_op jit(solution)/shard_map/ppermute | solution.py:44
  93.8 2.0 %collective-permute-start.15 = (f32[8,768]{1,0:T(8,128)S(1)}, f32[8,768]{1,0:T(8,128)S(1)}, u32[]{:S(2)}, u32[]{:S(2)}) collective-permute-start(f32[8,768]{1,0:T(8,128)S(1)} %add.68), channel_id=1, source_target_pairs={{0,56},{1,57},{2,58},{3,59},{4,60},{5,61},{6,62},{7,63},{8,48},{9,... | collective-permute-start | bytes 73736 | tf_op jit(solution)/shard_map/ppermute | solution.py:44
  95.8 3.1 %collective-permute-start.14 = (f32[8,768]{1,0:T(8,128)S(1)}, f32[8,768]{1,0:T(8,128)S(1)}, u32[]{:S(2)}, u32[]{:S(2)}) collective-permute-start(f32[8,768]{1,0:T(8,128)S(1)} %add.68), channel_id=1, source_target_pairs={{0,40},{1,41},{2,42},{3,43},{4,44},{5,45},{6,46},{7,47},{8,32},{9,... | collective-permute-start | bytes 73736 | tf_op jit(solution)/shard_map/ppermute | solution.py:44
  98.9 2.5 %collective-permute-done.14 = f32[8,768]{1,0:T(8,128)S(1)} collective-permute-done((f32[8,768]{1,0:T(8,128)S(1)}, f32[8,768]{1,0:T(8,128)S(1)}, u32[]{:S(2)}, u32[]{:S(2)}) %collective-permute-start.14) | collective-permute-done | bytes 24608 | tf_op jit(solution)/shard_map/ppermute | solution.py:44
  105.4 2.4 %collective-permute-start.19 = (f32[8,256]{1,0:T(8,128)S(1)}, f32[8,256]{1,0:T(8,128)S(1)}, u32[]{:S(2)}, u32[]{:S(2)}) collective-permute-start(f32[8,256]{1,0:T(8,128)S(1)} %get-tuple-element.35), channel_id=1, source_target_pairs={{0,128},{1,129},{2,130},{3,131},{4,132},{5,133},{6,134},{7,135},{8... | collective-permute-start | bytes 24584 | tf_op jit(solution)/shard_map/ppermute | solution.py:44
  112.2 2.0 %collective-permute-start.23 = (f32[8,768]{1,0:T(8,128)S(1)}, f32[8,768]{1,0:T(8,128)S(1)}, u32[]{:S(2)}, u32[]{:S(2)}) collective-permute-start(f32[8,768]{1,0:T(8,128)S(1)} %pad_maximum_fusion.5), channel_id=1, source_target_pairs={{0,6},{1,7},{2,4},{3,5},{4,2},{5,3},{6,0},{7,1},{8,14},{9,15},{10,... | collective-permute-start | bytes 73736 | tf_op jit(solution)/shard_map/ppermute | solution.py:44
  116.9 5.9 %collective-permute-start.24 = (f32[32,768]{1,0:T(8,128)S(1)}, f32[32,768]{1,0:T(8,128)S(1)}, u32[]{:S(2)}, u32[]{:S(2)}) collective-permute-start(f32[32,768]{1,0:T(8,128)S(1)} %pad_maximum_fusion.3), channel_id=1, source_target_pairs={{0,1},{1,0},{2,3},{3,2},{4,5},{5,4},{6,7},{7,6},{8,9},{9,8},{10,11... | collective-permute-start | bytes 294920 | tf_op jit(solution)/shard_map/ppermute | solution.py:44
  123.8 3.4 %copy-done.1 = bf16[2048,2048]{1,0:T(8,128)(2,1)S(1)} copy-done((bf16[2048,2048]{1,0:T(8,128)(2,1)S(1)}, bf16[2048,2048]{1,0:T(8,128)(2,1)}, u32[]{:S(2)}) %copy-start.1) | copy-done | bytes 8388632
  127.2 5.2 %last.1 = bf16[2048,64]{1,0:T(8,128)(2,1)S(1)} custom-call(f32[64,768]{1,0:T(8,128)S(1)} %pad_maximum_fusion.2.q_ref, bf16[3,2048,256]{2,1,0:T(8,128)(2,1)S(1)} %copy-done.3, f32[64,2048]{1,0:T(8,128)S(1)} %copy-done.8, bf16[2048,2048]{1,0:T(8,128)(2,1)S(1)} %copy-done.1), custom_call_target="tpu_custom_call" | custom-call | flops 536870912 | bytes 8388608 | tf_op jit(solution)/shard_map/last/pallas_call | solution.py:239
  133.2 1.9 %copy.6 = bf16[2048,64]{0,1:T(8,128)(2,1)} copy(bf16[2048,64]{1,0:T(8,128)(2,1)} %copy-done.6) | data formatting | bytes 524288 | tf_op jit(solution)/shard_map/last/pallas_call | solution.py:239
  (106 shorter events, 40.7 us)
Async XLA Ops:
  4.6 5.0 %collective-permute-start = (f32[128,1280]{1,0:T(8,128)S(1)}, f32[128,1280]{1,0:T(8,128)S(1)}, u32[]{:S(2)}, u32[]{:S(2)}) collective-permute-start(f32[128,1280]{1,0:T(8,128)S(1)} %get-tuple-element.14), channel_id=1, source_target_pairs={{0,1},{1,0},{2,3},{3,2},{4,5},{5,4},{6,7},{7,6},{8,9},{9,8},{10,11... | collective-permute-start | bytes 1966088 | tf_op jit(solution)/shard_map/ppermute | solution.py:44
  11.0 41.8 %all-to-all-start = ((f32[128,1,1280]{2,1,0:T(1,128)}), f32[128,1,1280]{2,1,0:T(1,128)}, u32[]{:S(2)}, u32[]{:S(2)}) async-start(f32[128,1,1280]{2,1,0:T(1,128)} %reshape.10), calls=%async_computation | async-start | bytes 1310720 | tf_op jit(solution)/shard_map/all_to_all | solution.py:56
  37.8 4.7 %collective-permute-start.4 = (f32[32,256]{1,0:T(8,128)S(1)}, f32[32,256]{1,0:T(8,128)S(1)}, u32[]{:S(2)}, u32[]{:S(2)}) collective-permute-start(f32[32,256]{1,0:T(8,128)S(1)} %select_add_fusion.1), channel_id=1, source_target_pairs={{0,6},{1,7},{2,4},{3,5},{4,2},{5,3},{6,0},{7,1},{8,14},{9,15},{10,... | collective-permute-start | bytes 98312 | tf_op jit(solution)/shard_map/ppermute | solution.py:44
  39.8 4.9 %collective-permute-start.3 = (f32[32,256]{1,0:T(8,128)S(1)}, f32[32,256]{1,0:T(8,128)S(1)}, u32[]{:S(2)}, u32[]{:S(2)}) collective-permute-start(f32[32,256]{1,0:T(8,128)S(1)} %select_add_fusion.1), channel_id=1, source_target_pairs={{0,4},{1,5},{2,6},{3,7},{4,0},{5,1},{6,2},{7,3},{8,12},{9,13},{10,... | collective-permute-start | bytes 98312 | tf_op jit(solution)/shard_map/ppermute | solution.py:44
  40.3 4.4 %collective-permute-start.2 = (f32[32,256]{1,0:T(8,128)S(1)}, f32[32,256]{1,0:T(8,128)S(1)}, u32[]{:S(2)}, u32[]{:S(2)}) collective-permute-start(f32[32,256]{1,0:T(8,128)S(1)} %select_add_fusion.1), channel_id=1, source_target_pairs={{0,2},{1,3},{2,0},{3,1},{4,6},{5,7},{6,4},{7,5},{8,10},{9,11},{10,... | collective-permute-start | bytes 98312 | tf_op jit(solution)/shard_map/ppermute | solution.py:44
  44.7 2.9 %collective-permute-start.5 = (f32[32,256]{1,0:T(8,128)S(1)}, f32[32,256]{1,0:T(8,128)S(1)}, u32[]{:S(2)}, u32[]{:S(2)}) collective-permute-start(f32[32,256]{1,0:T(8,128)S(1)} %add_add_fusion), channel_id=1, source_target_pairs={{0,8},{1,9},{2,10},{3,11},{4,12},{5,13},{6,14},{7,15},{8,0},{9,1},... | collective-permute-start | bytes 98312 | tf_op jit(solution)/shard_map/ppermute | solution.py:44
  47.6 18.8 %collective-permute-start.7 = (f32[32,256]{1,0:T(8,128)S(1)}, f32[32,256]{1,0:T(8,128)S(1)}, u32[]{:S(2)}, u32[]{:S(2)}) collective-permute-start(f32[32,256]{1,0:T(8,128)S(1)} %add.62), channel_id=1, source_target_pairs={{0,56},{1,57},{2,58},{3,59},{4,60},{5,61},{6,62},{7,63},{8,48},{9,... | collective-permute-start | bytes 98312 | tf_op jit(solution)/shard_map/ppermute | solution.py:44
  49.8 16.6 %collective-permute-start.6 = (f32[32,256]{1,0:T(8,128)S(1)}, f32[32,256]{1,0:T(8,128)S(1)}, u32[]{:S(2)}, u32[]{:S(2)}) collective-permute-start(f32[32,256]{1,0:T(8,128)S(1)} %add.62), channel_id=1, source_target_pairs={{0,40},{1,41},{2,42},{3,43},{4,44},{5,45},{6,46},{7,47},{8,32},{9,... | collective-permute-start | bytes 98312 | tf_op jit(solution)/shard_map/ppermute | solution.py:44
  55.1 27.3 %all-to-all-start.1 = ((f32[128,1,1280]{2,1,0:T(1,128)}), f32[128,1,1280]{2,1,0:T(1,128)}, u32[]{:S(2)}, u32[]{:S(2)}) async-start(f32[128,1,1280]{2,1,0:T(1,128)} %copy-done.4), calls=%async_computation.1 | async-start | bytes 1310720 | tf_op jit(solution)/shard_map/all_to_all | solution.py:56
  67.6 4.7 %collective-permute-start.8 = (f32[32,256]{1,0:T(8,128)S(1)}, f32[32,256]{1,0:T(8,128)S(1)}, u32[]{:S(2)}, u32[]{:S(2)}) collective-permute-start(f32[32,256]{1,0:T(8,128)S(1)} %fusion.21), channel_id=1, source_target_pairs={{0,1},{1,0},{2,3},{3,2},{4,5},{5,4},{6,7},{7,6},{8,9},{9,8},{10,11... | collective-permute-start | bytes 98312 | tf_op jit(solution)/shard_map/ppermute | solution.py:44
  77.9 12.3 %collective-permute-start.10 = (f32[8,768]{1,0:T(8,128)}, f32[8,768]{1,0:T(8,128)}, u32[]{:S(2)}, u32[]{:S(2)}) collective-permute-start(f32[8,768]{1,0:T(8,128)} %get-tuple-element.29), channel_id=1, source_target_pairs={{0,2},{1,3},{2,0},{3,1},{4,6},{5,7},{6,4},{7,5},{8,10},{9,11},{10,... | collective-permute-start | bytes 73736 | tf_op jit(solution)/shard_map/ppermute | solution.py:44
  78.7 11.5 %collective-permute-start.11 = (f32[8,768]{1,0:T(8,128)}, f32[8,768]{1,0:T(8,128)}, u32[]{:S(2)}, u32[]{:S(2)}) collective-permute-start(f32[8,768]{1,0:T(8,128)} %get-tuple-element.30), channel_id=1, source_target_pairs={{0,4},{1,5},{2,6},{3,7},{4,0},{5,1},{6,2},{7,3},{8,12},{9,13},{10,... | collective-permute-start | bytes 73736 | tf_op jit(solution)/shard_map/ppermute | solution.py:44
  81.1 9.1 %collective-permute-start.12 = (f32[8,768]{1,0:T(8,128)}, f32[8,768]{1,0:T(8,128)}, u32[]{:S(2)}, u32[]{:S(2)}) collective-permute-start(f32[8,768]{1,0:T(8,128)} %get-tuple-element.31), channel_id=1, source_target_pairs={{0,6},{1,7},{2,4},{3,5},{4,2},{5,3},{6,0},{7,1},{8,14},{9,15},{10,... | collective-permute-start | bytes 73736 | tf_op jit(solution)/shard_map/ppermute | solution.py:44
  83.7 19.3 %collective-permute-start.17 = (f32[128,1280]{1,0:T(8,128)S(1)}, f32[128,1280]{1,0:T(8,128)S(1)}, u32[]{:S(2)}, u32[]{:S(2)}) collective-permute-start(f32[128,1280]{1,0:T(8,128)S(1)} %bitcast.34), channel_id=1, source_target_pairs={{0,1},{1,0},{2,3},{3,2},{4,5},{5,4},{6,7},{7,6},{8,9},{9,8},{10,11... | collective-permute-start | bytes 1966088 | tf_op jit(solution)/shard_map/ppermute | solution.py:44
  91.0 2.8 %collective-permute-start.13 = (f32[8,768]{1,0:T(8,128)S(1)}, f32[8,768]{1,0:T(8,128)S(1)}, u32[]{:S(2)}, u32[]{:S(2)}) collective-permute-start(f32[8,768]{1,0:T(8,128)S(1)} %add_add_fusion.1), channel_id=1, source_target_pairs={{0,8},{1,9},{2,10},{3,11},{4,12},{5,13},{6,14},{7,15},{8,0},{9,1},... | collective-permute-start | bytes 73736 | tf_op jit(solution)/shard_map/ppermute | solution.py:44
  93.8 5.1 %collective-permute-start.15 = (f32[8,768]{1,0:T(8,128)S(1)}, f32[8,768]{1,0:T(8,128)S(1)}, u32[]{:S(2)}, u32[]{:S(2)}) collective-permute-start(f32[8,768]{1,0:T(8,128)S(1)} %add.68), channel_id=1, source_target_pairs={{0,56},{1,57},{2,58},{3,59},{4,60},{5,61},{6,62},{7,63},{8,48},{9,... | collective-permute-start | bytes 73736 | tf_op jit(solution)/shard_map/ppermute | solution.py:44
  95.8 5.7 %collective-permute-start.14 = (f32[8,768]{1,0:T(8,128)S(1)}, f32[8,768]{1,0:T(8,128)S(1)}, u32[]{:S(2)}, u32[]{:S(2)}) collective-permute-start(f32[8,768]{1,0:T(8,128)S(1)} %add.68), channel_id=1, source_target_pairs={{0,40},{1,41},{2,42},{3,43},{4,44},{5,45},{6,46},{7,47},{8,32},{9,... | collective-permute-start | bytes 73736 | tf_op jit(solution)/shard_map/ppermute | solution.py:44
  98.9 3.9 %collective-permute-start.16 = (f32[8,512]{1,0:T(8,128)S(1)}, f32[8,512]{1,0:T(8,128)S(1)}, u32[]{:S(2)}, u32[]{:S(2)}) collective-permute-start(f32[8,512]{1,0:T(8,128)S(1)} %slice.98), channel_id=1, source_target_pairs={{0,16},{1,17},{2,18},{3,19},{4,20},{5,21},{6,22},{7,23},{8,24},{9,... | collective-permute-start | bytes 49160 | tf_op jit(solution)/shard_map/ppermute | solution.py:44
  104.5 3.3 %collective-permute-start.18 = (f32[8,512]{1,0:T(8,128)S(1)}, f32[8,512]{1,0:T(8,128)S(1)}, u32[]{:S(2)}, u32[]{:S(2)}) collective-permute-start(f32[8,512]{1,0:T(8,128)S(1)} %pad_maximum_fusion.6), channel_id=1, source_target_pairs={{0,64},{1,65},{2,66},{3,67},{4,68},{5,69},{6,70},{7,71},{8,72},{9,... | collective-permute-start | bytes 49160 | tf_op jit(solution)/shard_map/ppermute | solution.py:44
  104.6 3.7 %collective-permute-start.20 = (f32[8,256]{1,0:T(8,128)S(1)}, f32[8,256]{1,0:T(8,128)S(1)}, u32[]{:S(2)}, u32[]{:S(2)}) collective-permute-start(f32[8,256]{1,0:T(8,128)S(1)} %get-tuple-element.35), channel_id=1, source_target_pairs={{0,192},{1,193},{2,194},{3,195},{4,196},{5,197},{6,198},{7,199},{8... | collective-permute-start | bytes 24584 | tf_op jit(solution)/shard_map/ppermute | solution.py:44
  105.4 4.0 %collective-permute-start.19 = (f32[8,256]{1,0:T(8,128)S(1)}, f32[8,256]{1,0:T(8,128)S(1)}, u32[]{:S(2)}, u32[]{:S(2)}) collective-permute-start(f32[8,256]{1,0:T(8,128)S(1)} %get-tuple-element.35), channel_id=1, source_target_pairs={{0,128},{1,129},{2,130},{3,131},{4,132},{5,133},{6,134},{7,135},{8... | collective-permute-start | bytes 24584 | tf_op jit(solution)/shard_map/ppermute | solution.py:44
  111.6 4.2 %collective-permute-start.22 = (f32[8,768]{1,0:T(8,128)S(1)}, f32[8,768]{1,0:T(8,128)S(1)}, u32[]{:S(2)}, u32[]{:S(2)}) collective-permute-start(f32[8,768]{1,0:T(8,128)S(1)} %pad_maximum_fusion.5), channel_id=1, source_target_pairs={{0,4},{1,5},{2,6},{3,7},{4,0},{5,1},{6,2},{7,3},{8,12},{9,13},{10,... | collective-permute-start | bytes 73736 | tf_op jit(solution)/shard_map/ppermute | solution.py:44
  112.2 3.9 %collective-permute-start.23 = (f32[8,768]{1,0:T(8,128)S(1)}, f32[8,768]{1,0:T(8,128)S(1)}, u32[]{:S(2)}, u32[]{:S(2)}) collective-permute-start(f32[8,768]{1,0:T(8,128)S(1)} %pad_maximum_fusion.5), channel_id=1, source_target_pairs={{0,6},{1,7},{2,4},{3,5},{4,2},{5,3},{6,0},{7,1},{8,14},{9,15},{10,... | collective-permute-start | bytes 73736 | tf_op jit(solution)/shard_map/ppermute | solution.py:44
  116.9 6.9 %collective-permute-start.24 = (f32[32,768]{1,0:T(8,128)S(1)}, f32[32,768]{1,0:T(8,128)S(1)}, u32[]{:S(2)}, u32[]{:S(2)}) collective-permute-start(f32[32,768]{1,0:T(8,128)S(1)} %pad_maximum_fusion.3), channel_id=1, source_target_pairs={{0,1},{1,0},{2,3},{3,2},{4,5},{5,4},{6,7},{7,6},{8,9},{9,8},{10,11... | collective-permute-start | bytes 294920 | tf_op jit(solution)/shard_map/ppermute | solution.py:44
  (18 other events, 98.3 us)

commit v2 on v0

v2 whole, which is shorter than its diff:
```python
import jax
import jax.numpy as jnp
from jax import lax
from jax.experimental import pallas as pl
from jax.experimental.pallas import tpu as pltpu
from jax.sharding import PartitionSpec as P

F32, BF16 = jnp.float32, jnp.bfloat16
AXIS = "leaf"
N = 256
VMEM = pltpu.VMEM
CHUNKS = 4


def params(mib):
    return pltpu.CompilerParams(vmem_limit_bytes=mib << 20)


def cost(flops, size):
    return pl.CostEstimate(flops=flops, bytes_accessed=size, transcendentals=0)


def whole(count, space=None):
    return [pl.BlockSpec(memory_space=space or VMEM)] * count


def dot(a, b, dims=((1,), (0,))):
    return lax.dot_general(a, b, (dims, ((), ())), preferred_element_type=F32)


NN, NT, TN = ((1,), (0,)), ((1,), (1,)), ((0,), (0,))


def swap(value, mask):
    return lax.ppermute(value, AXIS, [(i, i ^ mask) for i in range(N)])


def line(size, stride):
    return [
        [base + low + stride * k for k in range(size)]
        for base in range(0, N, size * stride)
        for low in range(stride)
    ]


def over_chips(value):
    groups = [[(xz * 4 + y) * 2 + core for y in range(4) for xz in range(32)] for core in range(2)]
    return lax.all_to_all(value, AXIS, 0, 0, axis_index_groups=groups, tiled=True)


def over_xz(value):
    return lax.all_to_all(value, AXIS, 0, 0, axis_index_groups=line(32, 8), tiled=True)


def thrice(value):
    a = value.astype(BF16)
    rest = value - a.astype(F32)
    b = rest.astype(BF16)
    return jnp.concatenate([a, b, (rest - b.astype(F32)).astype(BF16)], axis=0)


def exact(value, weight, dims):
    rows = value.shape[0]
    out = dot(thrice(value), weight, dims)
    return out[:rows] + out[rows : 2 * rows] + out[2 * rows :]


def apply(value, matrix, dims):
    value, top = value.astype(BF16), matrix.astype(BF16)
    return dot(value, top, dims) + dot(value, (matrix - top.astype(F32)).astype(BF16), dims)


def core_index():
    return lax.axis_index(AXIS) & 1


def both(own, other):
    low = core_index() == 0
    return jnp.concatenate([jnp.where(low, own, other), jnp.where(low, other, own)], axis=0)


def split_halves(value, keep_ref, send_ref):
    half = value.shape[0] // 2
    low = core_index() == 0
    keep_ref[...] = jnp.where(low, value[:half], value[half:])
    send_ref[...] = jnp.where(low, value[half:], value[:half])


def split_kernel(keep_ref, other_ref, *outs):
    rows = outs[0].shape[0]
    y = (lax.axis_index(AXIS) >> 1) & 3
    for m, out in enumerate(outs):
        at = pl.ds(pl.multiple_of((y ^ m) * rows, rows), rows)
        out[...] = keep_ref[at, :] + other_ref[at, :]


def split(keep, other):
    shape = jax.ShapeDtypeStruct((keep.shape[0] // 4, keep.shape[1]), F32)
    return pl.pallas_call(
        split_kernel,
        in_specs=whole(2),
        out_specs=whole(4),
        out_shape=[shape] * 4,
        compiler_params=params(16),
        cost_estimate=cost(keep.size, 12 * keep.size),
        name="split",
    )(keep, other)


def join_kernel(*refs):
    parts, out_ref = refs[:4], refs[4]
    rows = parts[0].shape[0]
    y = (lax.axis_index(AXIS) >> 1) & 3
    for m, part in enumerate(parts):
        at = pl.ds(pl.multiple_of((y ^ m) * rows, rows), rows)
        out_ref[at, :] = part[...].reshape(rows, out_ref.shape[1])


def join(parts):
    rows, width = parts[0].shape[0], parts[0].shape[-1]
    return pl.pallas_call(
        join_kernel,
        in_specs=whole(4),
        out_specs=whole(1)[0],
        out_shape=jax.ShapeDtypeStruct((4 * rows, width), F32),
        compiler_params=params(16),
        cost_estimate=cost(0, 32 * rows * width),
        name="join",
    )(*parts)


def add_kernel(a, b, out):
    out[...] = (a[...] + b[...]).reshape(out.shape)


def add_rows(a, b):
    rows, width = a.shape
    return pl.pallas_call(
        add_kernel,
        in_specs=whole(2),
        out_specs=whole(1)[0],
        out_shape=jax.ShapeDtypeStruct((rows, 1, width), F32),
        compiler_params=params(16),
        cost_estimate=cost(rows * width, 12 * rows * width),
        name="add_rows",
    )(a, b)


def table_kernel(rows_ref, out_ref):
    rank = rows_ref.shape[2] // 6
    sub = []
    for c in range(8):
        total = rows_ref[4 * c : 4 * c + 4].sum(axis=0)
        for y in range(1, 4):
            total += rows_ref[32 * y + 4 * c : 32 * y + 4 * c + 4].sum(axis=0)
        sub.append(total)
    node = [sub[2 * c] + sub[2 * c + 1] for c in range(4)]
    child = [node[0] + node[1], node[2] + node[3]]
    for c in range(8):
        own, other, beside, across = sub[c], sub[c ^ 1], node[(c >> 1) ^ 1], child[(c >> 2) ^ 1]
        row = jnp.concatenate(
            [own[:, : 2 * rank], other[:, : 3 * rank], beside[:, 3 * rank : 5 * rank], across[:, 5 * rank :]], axis=1
        )
        out_ref[4 * c : 4 * c + 4] = jnp.broadcast_to(row[None], (4, 1, row.shape[1]))


def table(rows):
    return pl.pallas_call(
        table_kernel,
        in_specs=whole(1),
        out_specs=whole(1)[0],
        out_shape=jax.ShapeDtypeStruct((32, 1, rows.shape[2] // 6 * 8), F32),
        compiler_params=params(16),
        cost_estimate=cost(rows.size, 8 * rows.size),
        name="table",
    )(rows)


PAIRS = ((1, 0), (2, 0), (0, 0), (1, 1), (1, 2), (2, 2))


def gram_kernel(u_ref, keep_ref, send_ref, u_buf, g_buf, sems):
    rank = u_ref.shape[2]
    copies = [pltpu.make_async_copy(u_ref.at[k], u_buf.at[k], sems.at[k]) for k in range(3)]
    for copy in copies:
        copy.start()
    ready = 0
    for a, b in sorted(PAIRS, key=max):
        while ready <= max(a, b):
            copies[ready].wait()
            ready += 1
        place = PAIRS.index((a, b))
        g_buf[:, place * rank : (place + 1) * rank] = dot(u_buf[a], u_buf[b], TN)
    split_halves(g_buf[...], keep_ref, send_ref)


def gram(bases):
    levels, leaf, rank = bases.shape
    width = len(PAIRS) * rank
    shape = jax.ShapeDtypeStruct((rank // 2, width), F32)
    return pl.pallas_call(
        gram_kernel,
        in_specs=whole(1, pl.ANY),
        out_specs=whole(2),
        out_shape=[shape, shape],
        scratch_shapes=[
            pltpu.VMEM((levels, leaf, rank), BF16),
            pltpu.VMEM((rank, width), F32),
            pltpu.SemaphoreType.DMA((levels,)),
        ],
        compiler_params=params(56),
        cost_estimate=cost(12 * leaf * rank * rank, 6 * leaf * rank),
        name="gram",
    )(bases)


def first_kernel(b_ref, f_ref, u_ref, z_ref, keep_ref, send_ref, f_buf, u_buf, sems):
    leaf = f_ref.shape[0]
    rows = leaf // CHUNKS
    copies = [
        pltpu.make_async_copy(f_ref.at[pl.ds(i * rows, rows)], f_buf.at[pl.ds(i * rows, rows)], sems.at[i])
        for i in range(CHUNKS)
    ]
    copies.append(pltpu.make_async_copy(u_ref, u_buf, sems.at[CHUNKS]))
    for copy in copies:
        copy.start()
    b = b_ref[...]
    for i in range(CHUNKS):
        copies[i].wait()
        z_ref[:, i * rows : (i + 1) * rows] = dot(b, f_buf[i * rows : (i + 1) * rows], NT)
    copies[CHUNKS].wait()
    zb = z_ref[...].astype(BF16)
    split_halves(jnp.concatenate([dot(zb, u_buf[k]) for k in range(3)], axis=1), keep_ref, send_ref)


def first(rhs, inverse, bases):
    cols, leaf = rhs.shape
    rank = bases.shape[2]
    shape = jax.ShapeDtypeStruct((cols // 2, 3 * rank), F32)
    return pl.pallas_call(
        first_kernel,
        in_specs=whole(1) + whole(2, pl.ANY),
        out_specs=whole(3),
        out_shape=[jax.ShapeDtypeStruct((cols, leaf), F32), shape, shape],
        scratch_shapes=[
            pltpu.VMEM((leaf, leaf), BF16),
            pltpu.VMEM((3, leaf, rank), BF16),
            pltpu.SemaphoreType.DMA((CHUNKS + 1,)),
        ],
        compiler_params=params(56),
        cost_estimate=cost(2 * leaf * leaf * cols, 2 * leaf * leaf),
        name="first",
    )(rhs, inverse, bases)


def block(own_ref, other_ref, place):
    rank = own_ref.shape[1] // 8
    at = slice(place * rank, (place + 1) * rank)
    return both(own_ref[:, at], other_ref[:, at])


def up_kernel(own_ref, other_ref, w_ref, p_ref, po_ref, vs_ref, q_ref):
    m10, m20, m10o, m20o, m00o, _, m12o = (block(own_ref, other_ref, k) for k in range(7))
    rank = m10.shape[0]
    q0 = exact(po_ref[:, :rank], w_ref[0], NT)
    q0o = exact(p_ref[:, :rank], w_ref[0], NT)
    s0o = po_ref[:, :rank] - apply(q0o, m00o, NN)
    s1 = p_ref[:, rank : 2 * rank] + po_ref[:, rank : 2 * rank] - apply(q0, m10, NT) - apply(q0o, m10o, NT)
    s2 = p_ref[:, 2 * rank :] + po_ref[:, 2 * rank :] - apply(q0, m20, NT) - apply(q0o, m20o, NT)
    q1o = exact(s1, w_ref[1], NT)
    vs_ref[...] = jnp.concatenate([s2 - apply(q1o, m12o, NN), s1], axis=1)
    q_ref[...] = jnp.concatenate([s0o, q0, q1o], axis=1)


def up(own, other, coupling, p, po):
    rows, width = p.shape
    rank = width // 3
    return pl.pallas_call(
        up_kernel,
        in_specs=whole(5),
        out_specs=whole(2),
        out_shape=[jax.ShapeDtypeStruct((rows, 2 * rank), F32), jax.ShapeDtypeStruct((rows, width), F32)],
        compiler_params=params(16),
        cost_estimate=cost(32 * rows * rank * rank, 8 * own.size),
        name="up",
    )(own, other, coupling, p, po)


def down_kernel(own_ref, other_ref, w_ref, vs_ref, b_ref, r2_ref, r3_ref, q_ref, out_ref):
    m10o, m20o, _, m11o, m12o, m22o = (block(own_ref, other_ref, k) for k in range(2, 8))
    rank = m10o.shape[0]
    s0o, q0, q1o = (q_ref[:, k * rank : (k + 1) * rank] for k in range(3))
    c2 = vs_ref[:, :rank] + b_ref[:, :rank]
    c2o = r2_ref[...] + r3_ref[...]
    s1o = b_ref[:, rank:]
    q1 = exact(s1o, w_ref[1], NT)
    q2 = exact(c2o, w_ref[2], NT)
    q2o = exact(c2, w_ref[2], NT)
    t2 = q2 + exact(c2o - apply(q2o, m22o, NN), w_ref[2], NN)
    t1 = q1 + exact(s1o - apply(q1o, m11o, NN) - apply(t2, m12o, NT), w_ref[1], NN)
    t0 = q0 + exact(s0o - apply(t1, m10o, NN) - apply(t2, m20o, NN), w_ref[0], NN)
    out_ref[...] = jnp.concatenate([t0, t1, t2], axis=1)


def down(own, other, coupling, vs, beside, r2, r3, q):
    rows, width = q.shape
    return pl.pallas_call(
        down_kernel,
        in_specs=whole(8),
        out_specs=whole(1)[0],
        out_shape=jax.ShapeDtypeStruct((rows, width), F32),
        compiler_params=params(16),
        cost_estimate=cost(4 * rows * width * width, 8 * own.size),
        name="down",
    )(own, other, coupling, vs, beside, r2, r3, q)


def last_kernel(own_ref, other_ref, u_ref, z_ref, f_ref, out_ref):
    leaf = f_ref.shape[0]
    rank = u_ref.shape[2]
    width = leaf // CHUNKS
    q = both(own_ref[...], other_ref[...]).astype(BF16)
    z = z_ref[...]
    for level in range(3):
        z -= dot(q[:, level * rank : (level + 1) * rank], u_ref[level], NT)
    zb = z.astype(BF16)
    for i in range(CHUNKS):
        at = slice(i * width, (i + 1) * width)
        out_ref[:, at] = dot(zb, f_ref[:, at]).astype(BF16)


def last(own, other, bases, state, inverse):
    cols, leaf = state.shape
    return pl.pallas_call(
        last_kernel,
        in_specs=whole(5),
        out_specs=whole(1)[0],
        out_shape=jax.ShapeDtypeStruct((cols, leaf), BF16),
        compiler_params=params(24),
        cost_estimate=cost(2 * leaf * leaf * cols, 2 * leaf * leaf),
        name="last",
    )(own, other, bases, state, inverse)


def after(value, *others):
    return lax.optimization_barrier((value, *others))[0]


def shards(rhs, leaf_inverse, bases, coupling):
    rank = bases.shape[2]

    keep, send = gram(bases)
    mine = add_rows(keep, swap(send, 1))
    summed = table(over_chips(mine))

    state, keep, send = first(after(rhs.T, mine), leaf_inverse, bases)
    parts = split(keep, swap(send, 1))
    part = parts[0] + swap(parts[1], 2) + swap(parts[2], 4) + swap(parts[3], 6)
    pair = part + swap(part, 8)
    p = pair + swap(pair, 16)
    po = swap(pair, 40) + swap(pair, 56)

    back = over_xz(after(summed, pair))
    own = join([back] + [swap(back, 2 * m) for m in (1, 2, 3)])
    sums = (own, swap(own, 1), coupling)

    vs, q = up(*sums, p, po)
    v = vs[:, :rank]
    mine = down(*sums, vs, swap(vs, 64), swap(v, 128), swap(v, 192), q)

    half = join([mine, swap(mine, 2), swap(mine, 4), swap(mine, 6)])
    return last(half, swap(half, 1), bases, state, leaf_inverse).T


def solution(mesh):
    placed = (P(AXIS, None), P(AXIS, None), P(None, AXIS, None), P())
    return jax.shard_map(
        shards, mesh=mesh, in_specs=placed, out_specs=P(AXIS, None), check_vma=False
    )
```

time: 232 us -> 119 us (0.51); the launches traced: 229 us -> 118 us
  waiting for transfers between devices: 98.2 us -> 26 us
  starting transfers between devices: 110 us -> 48.9 us
  Pallas kernels: 0 us -> 20.6 us
  matrix products: 17.7 us -> 0 us
  blocking collectives: 0 us -> 15.9 us
  local copies, waits for them, and re-layouts: 1.74 us -> 5.42 us
    ppermute x42 -> x20, starting transfers between devices: 110 us -> 34.6 us  [swap(): return lax.ppermute(value, AXIS, [(i, i ^ mask) for i in range(N)])]
    ppermute x42 -> x20, waiting for transfers between devices: 98.2 us -> 23.5 us  [swap(): return lax.ppermute(value, AXIS, [(i, i ^ mask) for i in range(N)])]
    pallas_call x0 -> x10, Pallas kernels: none -> 20.6 us  [the longest x1 7.35 us: first(): pl.pallas_call(first_kernel, in_specs=whole(1) + whole(2, pl.ANY), out_sp...]
    dot_general x19 -> x0, matrix products: 17.7 us -> none  [the longest x1 6.18 us: shards(): lax.dot_general(leaf_inverse, state.astype(jnp.bfloat16), (((0,), (0,)),...]
    all_to_all x0 -> x1, blocking collectives: none -> 15.9 us  [over_xz(): lax.all_to_all(value, AXIS, 0, 0, axis_index_groups=line(32, 8), tiled=True)]
    all_to_all x0 -> x1, starting transfers between devices: none -> 14.2 us  [over_chips(): lax.all_to_all(value, AXIS, 0, 0, axis_index_groups=groups, tiled=True)]
    unnamed x8 -> x12, local copies, waits for them, and re-layouts: 1.74 us -> 5.42 us
    all_to_all x0 -> x1, waiting for transfers between devices: none -> 2.57 us  [over_chips(): lax.all_to_all(value, AXIS, 0, 0, axis_index_groups=groups, tiled=True)]
  transfers between devices with their start and end apart: 42 -> 21, of which waited for: 42 -> 13; matrix products, arithmetic and copies ran while one was open for 0% -> 1% of each run, Pallas kernels for 0% -> 6%
where the time goes in v2:
time: 119 us; the launch traced here: 118 us
  starting transfers between devices  48.9 us (41%)
  waiting for transfers between devices  26 us (22%)
  Pallas kernels  20.6 us (17%)
  blocking collectives  15.9 us (13%)
  local copies, waits for them, and re-layouts  5.42 us (5%)
  other arithmetic  1.4 us (1%)
    ppermute x20, starting transfers between devices, swap(): return lax.ppermute(value, AXIS, [(i, i ^ mask) for i in range(N)])  34.6 us
    ppermute x20, waiting for transfers between devices, swap(): return lax.ppermute(value, AXIS, [(i, i ^ mask) for i in range(N)])  23.5 us
    all_to_all x1, blocking collectives, over_xz(): lax.all_to_all(value, AXIS, 0, 0, axis_index_groups=line(32, 8), tiled=True)  15.9 us
    all_to_all x1, starting transfers between devices, over_chips(): lax.all_to_all(value, AXIS, 0, 0, axis_index_groups=groups, tiled=True)  14.2 us
    pallas_call x1, Pallas kernels, first(): pl.pallas_call(first_kernel, in_specs=whole(1) + whole(2, pl.ANY), out_sp...  7.35 us
    unnamed x12, local copies, waits for them, and re-layouts  5.42 us
    pallas_call x1, Pallas kernels, gram(): pl.pallas_call(gram_kernel, in_specs=whole(1, pl.ANY), out_specs=whole(2)...  5.18 us
    pallas_call x1, Pallas kernels, last(): pl.pallas_call(last_kernel, in_specs=whole(5), out_specs=whole(1)[0], out...  3.24 us
  transfers between devices with their start and end apart: 21, of which 13 were waited for; matrix products, arithmetic and copies ran while one was open for 1% of the time, Pallas kernels for 6%

profile of v2, /device:TPU:1, one launch (start us, length us, event | category | flops | bytes accessed | tf_op | source)
XLA Modules:
  0.0 118.4 jit_solution(18261485194410248179)
XLA Ops:
  0.0 5.2 %gram.1 = (f32[128,1536]{1,0:T(8,128)}, f32[128,1536]{1,0:T(8,128)}) custom-call(bf16[3,2048,256]{2,1,0:T(8,128)(2,1)} %u_ref.5), custom_call_target="tpu_custom_call" | custom-call | flops 1610612736 | bytes 3145728 | tf_op jit(solution)/shard_map/gram/pallas_call | solution.py:201
  5.2 3.3 %collective-permute-start = (f32[128,1536]{1,0:T(8,128)}, f32[128,1536]{1,0:T(8,128)S(1)}, u32[]{:S(2)}, u32[]{:S(2)}) collective-permute-start(f32[128,1536]{1,0:T(8,128)} %get-tuple-element.19), channel_id=1, source_target_pairs={{0,1},{1,0},{2,3},{3,2},{4,5},{5,4},{6,7},{7,6},{8,9},{9,8},{10,11... | collective-permute-start | bytes 2359304 | tf_op jit(solution)/shard_map/ppermute | solution.py:35
  8.5 2.1 %collective-permute-done.b = f32[128,1536]{1,0:T(8,128)S(1)} collective-permute-done((f32[128,1536]{1,0:T(8,128)}, f32[128,1536]{1,0:T(8,128)S(1)}, u32[]{:S(2)}, u32[]{:S(2)}) %collective-permute-start) | collective-permute-done | bytes 786464 | tf_op jit(solution)/shard_map/ppermute | solution.py:35
  12.9 14.2 %all-to-all-start = ((f32[128,1,1536]{2,1,0:T(1,128)}), f32[128,1,1536]{2,1,0:T(1,128)}, u32[]{:S(2)}, u32[]{:S(2)}) async-start(f32[128,1,1536]{2,1,0:T(1,128)} %add_rows.1), calls=%async_computation | async-start | bytes 1572864 | tf_op jit(solution)/shard_map/all_to_all | solution.py:48
  27.2 7.3 %first.1 = (f32[64,2048]{1,0:T(8,128)}, f32[32,768]{1,0:T(8,128)}, f32[32,768]{1,0:T(8,128)}) custom-call(bf16[64,2048]{1,0:T(8,128)(2,1)} %bitcast.2, bf16[2048,2048]{1,0:T(8,128)(2,1)} %f_ref.3, bf16[3,2048,256]{2,1,0:T(8,128)(2,1)} %u_ref.5), custom_call_target="tpu_custom_call" | custom-call | flops 536870912 | bytes 8388608 | tf_op jit(solution)/shard_map/first/pallas_call | solution.py:240
  38.3 2.8 %collective-permute-start.3 = (f32[8,768]{1,0:T(8,128)S(1)}, f32[8,768]{1,0:T(8,128)S(1)}, u32[]{:S(2)}, u32[]{:S(2)}) collective-permute-start(f32[8,768]{1,0:T(8,128)S(1)} %get-tuple-element.25), channel_id=1, source_target_pairs={{0,4},{1,5},{2,6},{3,7},{4,0},{5,1},{6,2},{7,3},{8,12},{9,13},{10,... | collective-permute-start | bytes 73736 | tf_op jit(solution)/shard_map/ppermute | solution.py:35
  41.3 2.0 %collective-permute-done.3 = f32[8,768]{1,0:T(8,128)S(1)} collective-permute-done((f32[8,768]{1,0:T(8,128)S(1)}, f32[8,768]{1,0:T(8,128)S(1)}, u32[]{:S(2)}, u32[]{:S(2)}) %collective-permute-start.3) | collective-permute-done | bytes 24608 | tf_op jit(solution)/shard_map/ppermute | solution.py:35
  43.3 2.2 %collective-permute-done.4 = f32[8,768]{1,0:T(8,128)S(1)} collective-permute-done((f32[8,768]{1,0:T(8,128)S(1)}, f32[8,768]{1,0:T(8,128)S(1)}, u32[]{:S(2)}, u32[]{:S(2)}) %collective-permute-start.4) | collective-permute-done | bytes 24608 | tf_op jit(solution)/shard_map/ppermute | solution.py:35
  45.5 1.3 %collective-permute-start.5 = (f32[8,768]{1,0:T(8,128)S(1)}, f32[8,768]{1,0:T(8,128)S(1)}, u32[]{:S(2)}, u32[]{:S(2)}) collective-permute-start(f32[8,768]{1,0:T(8,128)S(1)} %add_add_fusion), channel_id=1, source_target_pairs={{0,8},{1,9},{2,10},{3,11},{4,12},{5,13},{6,14},{7,15},{8,0},{9,1},... | collective-permute-start | bytes 73736 | tf_op jit(solution)/shard_map/ppermute | solution.py:35
  46.8 1.9 %collective-permute-done.5 = f32[8,768]{1,0:T(8,128)S(1)} collective-permute-done((f32[8,768]{1,0:T(8,128)S(1)}, f32[8,768]{1,0:T(8,128)S(1)}, u32[]{:S(2)}, u32[]{:S(2)}) %collective-permute-start.5) | collective-permute-done | bytes 24608 | tf_op jit(solution)/shard_map/ppermute | solution.py:35
  49.3 2.6 %all-to-all-done.rows_ref = f32[128,1,1536]{2,1,0:T(1,128)} async-done(((f32[128,1,1536]{2,1,0:T(1,128)}), f32[128,1,1536]{2,1,0:T(1,128)}, u32[]{:S(2)}, u32[]{:S(2)}) %all-to-all-start) | async-done | bytes 786464 | tf_op jit(solution)/shard_map/all_to_all | solution.py:48
  51.8 1.7 %table.1 = f32[32,1,2048]{2,1,0:T(1,128)S(1)} custom-call(f32[128,1,1536]{2,1,0:T(1,128)} %all-to-all-done.rows_ref), custom_call_target="tpu_custom_call" | custom-call | flops 196608 | bytes 1572864 | tf_op jit(solution)/shard_map/table/pallas_call | solution.py:168
  53.5 15.9 %all_to_all.10.refs_0_ = f32[32,1,2048]{2,1,0:T(1,128)S(1)} all-to-all(f32[32,1,2048]{2,1,0:T(1,128)S(1)} %table.1), channel_id=1, replica_groups={{0,8,16,24,32,40,48,56,64,72,80,88,96,104,112,120,128,136,144,152,160,1..., dimensions={0} | all-to-all | bytes 524288 | tf_op jit(solution)/shard_map/all_to_all | solution.py:52
  70.4 2.3 %collective-permute-start.6 = (f32[32,1,2048]{2,1,0:T(1,128)S(1)}, f32[32,1,2048]{2,1,0:T(1,128)S(1)}, u32[]{:S(2)}, u32[]{:S(2)}) collective-permute-start(f32[32,1,2048]{2,1,0:T(1,128)S(1)} %all_to_all.10.refs_0_), channel_id=1, source_target_pairs={{0,2},{1,3},{2,0},{3,1},{4,6},{5,7},{6,4},{7,5},{8,10},{9,11},{10,... | collective-permute-start | bytes 786440 | tf_op jit(solution)/shard_map/ppermute | solution.py:35
  72.7 7.9 %collective-permute-done.8.refs_3_ = f32[32,1,2048]{2,1,0:T(1,128)S(1)} collective-permute-done((f32[32,1,2048]{2,1,0:T(1,128)S(1)}, f32[32,1,2048]{2,1,0:T(1,128)S(1)}, u32[]{:S(2)}, u32[]{:S(2)}) %collective-permute-start.8) | collective-permute-done | bytes 262176 | tf_op jit(solution)/shard_map/ppermute | solution.py:35
  80.7 5.2 %collective-permute-start.9 = (f32[128,2048]{1,0:T(8,128)S(1)}, f32[128,2048]{1,0:T(8,128)S(1)}, u32[]{:S(2)}, u32[]{:S(2)}) collective-permute-start(f32[128,2048]{1,0:T(8,128)S(1)} %join.2.own_ref), channel_id=1, source_target_pairs={{0,1},{1,0},{2,3},{3,2},{4,5},{5,4},{6,7},{7,6},{8,9},{9,8},{10,11... | collective-permute-start | bytes 3145736 | tf_op jit(solution)/shard_map/ppermute | solution.py:35
  85.9 1.7 %collective-permute-start.10 = (f32[8,768]{1,0:T(8,128)}, f32[8,768]{1,0:T(8,128)S(1)}, u32[]{:S(2)}, u32[]{:S(2)}) collective-permute-start(f32[8,768]{1,0:T(8,128)} %add.21), channel_id=1, source_target_pairs={{0,16},{1,17},{2,18},{3,19},{4,20},{5,21},{6,22},{7,23},{8,24},{9,... | collective-permute-start | bytes 73736 | tf_op jit(solution)/shard_map/ppermute | solution.py:35
  87.6 4.0 %collective-permute-start.11 = (f32[8,768]{1,0:T(8,128)}, f32[8,768]{1,0:T(8,128)S(1)}, u32[]{:S(2)}, u32[]{:S(2)}) collective-permute-start(f32[8,768]{1,0:T(8,128)} %add.21), channel_id=1, source_target_pairs={{0,40},{1,41},{2,42},{3,43},{4,44},{5,45},{6,46},{7,47},{8,32},{9,... | collective-permute-start | bytes 73736 | tf_op jit(solution)/shard_map/ppermute | solution.py:35
  96.1 1.4 %collective-permute-start.14 = (f32[8,256]{1,0:T(8,128)S(1)}, f32[8,256]{1,0:T(8,128)S(1)}, u32[]{:S(2)}, u32[]{:S(2)}) collective-permute-start(f32[8,256]{1,0:T(8,128)S(1)} %slice.3), channel_id=1, source_target_pairs={{0,128},{1,129},{2,130},{3,131},{4,132},{5,133},{6,134},{7,135},{8... | collective-permute-start | bytes 24584 | tf_op jit(solution)/shard_map/ppermute | solution.py:35
  98.7 1.4 %collective-permute-done.14.r2_ref = f32[8,256]{1,0:T(8,128)S(1)} collective-permute-done((f32[8,256]{1,0:T(8,128)S(1)}, f32[8,256]{1,0:T(8,128)S(1)}, u32[]{:S(2)}, u32[]{:S(2)}) %collective-permute-start.14) | collective-permute-done | bytes 8224 | tf_op jit(solution)/shard_map/ppermute | solution.py:35
  102.4 2.2 %collective-permute-start.16 = (f32[8,768]{1,0:T(8,128)S(1)}, f32[8,768]{1,0:T(8,128)S(1)}, u32[]{:S(2)}, u32[]{:S(2)}) collective-permute-start(f32[8,768]{1,0:T(8,128)S(1)} %down.1.refs_0_), channel_id=1, source_target_pairs={{0,2},{1,3},{2,0},{3,1},{4,6},{5,7},{6,4},{7,5},{8,10},{9,11},{10,... | collective-permute-start | bytes 73736 | tf_op jit(solution)/shard_map/ppermute | solution.py:35
  106.1 4.7 %collective-permute-start.19 = (f32[32,768]{1,0:T(8,128)S(1)}, f32[32,768]{1,0:T(8,128)S(1)}, u32[]{:S(2)}, u32[]{:S(2)}) collective-permute-start(f32[32,768]{1,0:T(8,128)S(1)} %join.3.own_ref), channel_id=1, source_target_pairs={{0,1},{1,0},{2,3},{3,2},{4,5},{5,4},{6,7},{7,6},{8,9},{9,8},{10,11... | collective-permute-start | bytes 294920 | tf_op jit(solution)/shard_map/ppermute | solution.py:35
  111.8 3.4 %copy-done = bf16[2048,2048]{1,0:T(8,128)(2,1)S(1)} copy-done((bf16[2048,2048]{1,0:T(8,128)(2,1)S(1)}, bf16[2048,2048]{1,0:T(8,128)(2,1)}, u32[]{:S(2)}) %copy-start) | copy-done | bytes 8388632
  115.1 3.2 %last.1 = bf16[64,2048]{1,0:T(8,128)(2,1)} custom-call(f32[32,768]{1,0:T(8,128)S(1)} %join.3.own_ref, f32[32,768]{1,0:T(8,128)S(1)} %collective-permute-done.19.other_ref, bf16[3,2048,256]{2,1,0:T(8,128)(2,1)S(1)} %copy-done.1, f32[64,2048]{1,0:T(8,128)S(1)} %copy-done.4, bf16[2048,2048]{1,0:T(8,128)(2,1)S(1)} %copy-done), custom_call_target="tpu_custom_call" | custom-call | flops 536870912 | bytes 8388608 | tf_op jit(solution)/shard_map/last/pallas_call | solution.py:334
  (46 shorter events, 18.4 us)
Async XLA Ops:
  5.2 5.5 %collective-permute-start = (f32[128,1536]{1,0:T(8,128)}, f32[128,1536]{1,0:T(8,128)S(1)}, u32[]{:S(2)}, u32[]{:S(2)}) collective-permute-start(f32[128,1536]{1,0:T(8,128)} %get-tuple-element.19), channel_id=1, source_target_pairs={{0,1},{1,0},{2,3},{3,2},{4,5},{5,4},{6,7},{7,6},{8,9},{9,8},{10,11... | collective-permute-start | bytes 2359304 | tf_op jit(solution)/shard_map/ppermute | solution.py:35
  12.9 38.9 %all-to-all-start = ((f32[128,1,1536]{2,1,0:T(1,128)}), f32[128,1,1536]{2,1,0:T(1,128)}, u32[]{:S(2)}, u32[]{:S(2)}) async-start(f32[128,1,1536]{2,1,0:T(1,128)} %add_rows.1), calls=%async_computation | async-start | bytes 1572864 | tf_op jit(solution)/shard_map/all_to_all | solution.py:48
  27.1 66.4 %copy-start.2 = (bf16[3,256,256]{2,1,0:T(8,128)(2,1)S(1)}, bf16[3,256,256]{2,1,0:T(8,128)(2,1)}, u32[]{:S(2)}) copy-start(bf16[3,256,256]{2,1,0:T(8,128)(2,1)} %w_ref.3) | copy-start | bytes 1179652
  27.1 84.6 %copy-start.1 = (bf16[3,2048,256]{2,1,0:T(8,128)(2,1)S(1)}, bf16[3,2048,256]{2,1,0:T(8,128)(2,1)}, u32[]{:S(2)}) copy-start(bf16[3,2048,256]{2,1,0:T(8,128)(2,1)} %u_ref.5) | copy-start | bytes 9437188
  34.5 1.9 %collective-permute-start.1 = (f32[32,768]{1,0:T(8,128)}, f32[32,768]{1,0:T(8,128)S(1)}, u32[]{:S(2)}, u32[]{:S(2)}) collective-permute-start(f32[32,768]{1,0:T(8,128)} %get-tuple-element.22), channel_id=1, source_target_pairs={{0,1},{1,0},{2,3},{3,2},{4,5},{5,4},{6,7},{7,6},{8,9},{9,8},{10,11... | collective-permute-start | bytes 294920 | tf_op jit(solution)/shard_map/ppermute | solution.py:35
  37.3 3.9 %collective-permute-start.2 = (f32[8,768]{1,0:T(8,128)S(1)}, f32[8,768]{1,0:T(8,128)S(1)}, u32[]{:S(2)}, u32[]{:S(2)}) collective-permute-start(f32[8,768]{1,0:T(8,128)S(1)} %get-tuple-element.24), channel_id=1, source_target_pairs={{0,2},{1,3},{2,0},{3,1},{4,6},{5,7},{6,4},{7,5},{8,10},{9,11},{10,... | collective-permute-start | bytes 73736 | tf_op jit(solution)/shard_map/ppermute | solution.py:35
  38.3 5.0 %collective-permute-start.3 = (f32[8,768]{1,0:T(8,128)S(1)}, f32[8,768]{1,0:T(8,128)S(1)}, u32[]{:S(2)}, u32[]{:S(2)}) collective-permute-start(f32[8,768]{1,0:T(8,128)S(1)} %get-tuple-element.25), channel_id=1, source_target_pairs={{0,4},{1,5},{2,6},{3,7},{4,0},{5,1},{6,2},{7,3},{8,12},{9,13},{10,... | collective-permute-start | bytes 73736 | tf_op jit(solution)/shard_map/ppermute | solution.py:35
  41.1 4.3 %collective-permute-start.4 = (f32[8,768]{1,0:T(8,128)S(1)}, f32[8,768]{1,0:T(8,128)S(1)}, u32[]{:S(2)}, u32[]{:S(2)}) collective-permute-start(f32[8,768]{1,0:T(8,128)S(1)} %get-tuple-element.26), channel_id=1, source_target_pairs={{0,6},{1,7},{2,4},{3,5},{4,2},{5,3},{6,0},{7,1},{8,14},{9,15},{10,... | collective-permute-start | bytes 73736 | tf_op jit(solution)/shard_map/ppermute | solution.py:35
  45.5 3.2 %collective-permute-start.5 = (f32[8,768]{1,0:T(8,128)S(1)}, f32[8,768]{1,0:T(8,128)S(1)}, u32[]{:S(2)}, u32[]{:S(2)}) collective-permute-start(f32[8,768]{1,0:T(8,128)S(1)} %add_add_fusion), channel_id=1, source_target_pairs={{0,8},{1,9},{2,10},{3,11},{4,12},{5,13},{6,14},{7,15},{8,0},{9,1},... | collective-permute-start | bytes 73736 | tf_op jit(solution)/shard_map/ppermute | solution.py:35
  51.8 59.9 %copy-start.4 = (f32[64,2048]{1,0:T(8,128)S(1)}, f32[64,2048]{1,0:T(8,128)}, u32[]{:S(2)}) copy-start(f32[64,2048]{1,0:T(8,128)} %get-tuple-element.30.z_ref) | copy-start | bytes 1572868
  69.4 11.1 %collective-permute-start.8 = (f32[32,1,2048]{2,1,0:T(1,128)S(1)}, f32[32,1,2048]{2,1,0:T(1,128)S(1)}, u32[]{:S(2)}, u32[]{:S(2)}) collective-permute-start(f32[32,1,2048]{2,1,0:T(1,128)S(1)} %all_to_all.10.refs_0_), channel_id=1, source_target_pairs={{0,6},{1,7},{2,4},{3,5},{4,2},{5,3},{6,0},{7,1},{8,14},{9,15},{10,... | collective-permute-start | bytes 786440 | tf_op jit(solution)/shard_map/ppermute | solution.py:35
  69.9 10.7 %collective-permute-start.7 = (f32[32,1,2048]{2,1,0:T(1,128)S(1)}, f32[32,1,2048]{2,1,0:T(1,128)S(1)}, u32[]{:S(2)}, u32[]{:S(2)}) collective-permute-start(f32[32,1,2048]{2,1,0:T(1,128)S(1)} %all_to_all.10.refs_0_), channel_id=1, source_target_pairs={{0,4},{1,5},{2,6},{3,7},{4,0},{5,1},{6,2},{7,3},{8,12},{9,13},{10,... | collective-permute-start | bytes 786440 | tf_op jit(solution)/shard_map/ppermute | solution.py:35
  70.4 10.2 %collective-permute-start.6 = (f32[32,1,2048]{2,1,0:T(1,128)S(1)}, f32[32,1,2048]{2,1,0:T(1,128)S(1)}, u32[]{:S(2)}, u32[]{:S(2)}) collective-permute-start(f32[32,1,2048]{2,1,0:T(1,128)S(1)} %all_to_all.10.refs_0_), channel_id=1, source_target_pairs={{0,2},{1,3},{2,0},{3,1},{4,6},{5,7},{6,4},{7,5},{8,10},{9,11},{10,... | collective-permute-start | bytes 786440 | tf_op jit(solution)/shard_map/ppermute | solution.py:35
  80.7 12.8 %collective-permute-start.9 = (f32[128,2048]{1,0:T(8,128)S(1)}, f32[128,2048]{1,0:T(8,128)S(1)}, u32[]{:S(2)}, u32[]{:S(2)}) collective-permute-start(f32[128,2048]{1,0:T(8,128)S(1)} %join.2.own_ref), channel_id=1, source_target_pairs={{0,1},{1,0},{2,3},{3,2},{4,5},{5,4},{6,7},{7,6},{8,9},{9,8},{10,11... | collective-permute-start | bytes 3145736 | tf_op jit(solution)/shard_map/ppermute | solution.py:35
  85.9 5.7 %collective-permute-start.10 = (f32[8,768]{1,0:T(8,128)}, f32[8,768]{1,0:T(8,128)S(1)}, u32[]{:S(2)}, u32[]{:S(2)}) collective-permute-start(f32[8,768]{1,0:T(8,128)} %add.21), channel_id=1, source_target_pairs={{0,16},{1,17},{2,18},{3,19},{4,20},{5,21},{6,22},{7,23},{8,24},{9,... | collective-permute-start | bytes 73736 | tf_op jit(solution)/shard_map/ppermute | solution.py:35
  87.6 4.8 %collective-permute-start.12 = (f32[8,768]{1,0:T(8,128)}, f32[8,768]{1,0:T(8,128)S(1)}, u32[]{:S(2)}, u32[]{:S(2)}) collective-permute-start(f32[8,768]{1,0:T(8,128)} %add.21), channel_id=1, source_target_pairs={{0,56},{1,57},{2,58},{3,59},{4,60},{5,61},{6,62},{7,63},{8,48},{9,... | collective-permute-start | bytes 73736 | tf_op jit(solution)/shard_map/ppermute | solution.py:35
  87.6 5.9 %collective-permute-start.11 = (f32[8,768]{1,0:T(8,128)}, f32[8,768]{1,0:T(8,128)S(1)}, u32[]{:S(2)}, u32[]{:S(2)}) collective-permute-start(f32[8,768]{1,0:T(8,128)} %add.21), channel_id=1, source_target_pairs={{0,40},{1,41},{2,42},{3,43},{4,44},{5,45},{6,46},{7,47},{8,32},{9,... | collective-permute-start | bytes 73736 | tf_op jit(solution)/shard_map/ppermute | solution.py:35
  94.2 5.9 %collective-permute-start.13 = (f32[8,512]{1,0:T(8,128)S(1)}, f32[8,512]{1,0:T(8,128)S(1)}, u32[]{:S(2)}, u32[]{:S(2)}) collective-permute-start(f32[8,512]{1,0:T(8,128)S(1)} %get-tuple-element.28.vs_ref), channel_id=1, source_target_pairs={{0,64},{1,65},{2,66},{3,67},{4,68},{5,69},{6,70},{7,71},{8,72},{9,... | collective-permute-start | bytes 49160 | tf_op jit(solution)/shard_map/ppermute | solution.py:35
  95.0 3.7 %collective-permute-start.15 = (f32[8,256]{1,0:T(8,128)S(1)}, f32[8,256]{1,0:T(8,128)S(1)}, u32[]{:S(2)}, u32[]{:S(2)}) collective-permute-start(f32[8,256]{1,0:T(8,128)S(1)} %slice.3), channel_id=1, source_target_pairs={{0,192},{1,193},{2,194},{3,195},{4,196},{5,197},{6,198},{7,199},{8... | collective-permute-start | bytes 24584 | tf_op jit(solution)/shard_map/ppermute | solution.py:35
  96.1 4.0 %collective-permute-start.14 = (f32[8,256]{1,0:T(8,128)S(1)}, f32[8,256]{1,0:T(8,128)S(1)}, u32[]{:S(2)}, u32[]{:S(2)}) collective-permute-start(f32[8,256]{1,0:T(8,128)S(1)} %slice.3), channel_id=1, source_target_pairs={{0,128},{1,129},{2,130},{3,131},{4,132},{5,133},{6,134},{7,135},{8... | collective-permute-start | bytes 24584 | tf_op jit(solution)/shard_map/ppermute | solution.py:35
  101.3 3.9 %collective-permute-start.18 = (f32[8,768]{1,0:T(8,128)S(1)}, f32[8,768]{1,0:T(8,128)S(1)}, u32[]{:S(2)}, u32[]{:S(2)}) collective-permute-start(f32[8,768]{1,0:T(8,128)S(1)} %down.1.refs_0_), channel_id=1, source_target_pairs={{0,6},{1,7},{2,4},{3,5},{4,2},{5,3},{6,0},{7,1},{8,14},{9,15},{10,... | collective-permute-start | bytes 73736 | tf_op jit(solution)/shard_map/ppermute | solution.py:35
  101.9 4.2 %collective-permute-start.17 = (f32[8,768]{1,0:T(8,128)S(1)}, f32[8,768]{1,0:T(8,128)S(1)}, u32[]{:S(2)}, u32[]{:S(2)}) collective-permute-start(f32[8,768]{1,0:T(8,128)S(1)} %down.1.refs_0_), channel_id=1, source_target_pairs={{0,4},{1,5},{2,6},{3,7},{4,0},{5,1},{6,2},{7,3},{8,12},{9,13},{10,... | collective-permute-start | bytes 73736 | tf_op jit(solution)/shard_map/ppermute | solution.py:35
  102.4 3.7 %collective-permute-start.16 = (f32[8,768]{1,0:T(8,128)S(1)}, f32[8,768]{1,0:T(8,128)S(1)}, u32[]{:S(2)}, u32[]{:S(2)}) collective-permute-start(f32[8,768]{1,0:T(8,128)S(1)} %down.1.refs_0_), channel_id=1, source_target_pairs={{0,2},{1,3},{2,0},{3,1},{4,6},{5,7},{6,4},{7,5},{8,10},{9,11},{10,... | collective-permute-start | bytes 73736 | tf_op jit(solution)/shard_map/ppermute | solution.py:35
  106.1 5.6 %collective-permute-start.19 = (f32[32,768]{1,0:T(8,128)S(1)}, f32[32,768]{1,0:T(8,128)S(1)}, u32[]{:S(2)}, u32[]{:S(2)}) collective-permute-start(f32[32,768]{1,0:T(8,128)S(1)} %join.3.own_ref), channel_id=1, source_target_pairs={{0,1},{1,0},{2,3},{3,2},{4,5},{5,4},{6,7},{7,6},{8,9},{9,8},{10,11... | collective-permute-start | bytes 294920 | tf_op jit(solution)/shard_map/ppermute | solution.py:35
  (3 other events, 5.4 us)

commit v3 on v2

--- a/solution.py
+++ b/solution.py
@@ -41,11 +41,6 @@
         for base in range(0, N, size * stride)
         for low in range(stride)
     ]
-
-
-def over_chips(value):
-    groups = [[(xz * 4 + y) * 2 + core for y in range(4) for xz in range(32)] for core in range(2)]
-    return lax.all_to_all(value, AXIS, 0, 0, axis_index_groups=groups, tiled=True)
 
 
 def over_xz(value):
@@ -129,31 +124,26 @@
     )(*parts)
 
 
-def add_kernel(a, b, out):
-    out[...] = (a[...] + b[...]).reshape(out.shape)
-
-
-def add_rows(a, b):
-    rows, width = a.shape
+def add_kernel(a, b, c, d, out):
+    out[...] = (a[...] + b[...] + c[...] + d[...]).reshape(out.shape)
+
+
+def add_rows(parts):
+    rows, width = parts[0].shape
     return pl.pallas_call(
         add_kernel,
-        in_specs=whole(2),
+        in_specs=whole(4),
         out_specs=whole(1)[0],
         out_shape=jax.ShapeDtypeStruct((rows, 1, width), F32),
         compiler_params=params(16),
         cost_estimate=cost(rows * width, 12 * rows * width),
         name="add_rows",
-    )(a, b)
+    )(*parts)
 
 
 def table_kernel(rows_ref, out_ref):
     rank = rows_ref.shape[2] // 6
-    sub = []
-    for c in range(8):
-        total = rows_ref[4 * c : 4 * c + 4].sum(axis=0)
-        for y in range(1, 4):
-            total += rows_ref[32 * y + 4 * c : 32 * y + 4 * c + 4].sum(axis=0)
-        sub.append(total)
+    sub = [rows_ref[4 * c : 4 * c + 4].sum(axis=0) for c in range(8)]
     node = [sub[2 * c] + sub[2 * c + 1] for c in range(4)]
     child = [node[0] + node[1], node[2] + node[3]]
     for c in range(8):
@@ -200,7 +190,7 @@
     shape = jax.ShapeDtypeStruct((rank // 2, width), F32)
     return pl.pallas_call(
         gram_kernel,
-        in_specs=whole(1, pl.ANY),
+        in_specs=whole(1, pltpu.HBM),
         out_specs=whole(2),
         out_shape=[shape, shape],
         scratch_shapes=[
@@ -239,7 +229,7 @@
     shape = jax.ShapeDtypeStruct((cols // 2, 3 * rank), F32)
     return pl.pallas_call(
         first_kernel,
-        in_specs=whole(1) + whole(2, pl.ANY),
+        in_specs=whole(1) + whole(2, pltpu.HBM),
         out_specs=whole(3),
         out_shape=[jax.ShapeDtypeStruct((cols, leaf), F32), shape, shape],
         scratch_shapes=[
@@ -247,7 +237,7 @@
             pltpu.VMEM((3, leaf, rank), BF16),
             pltpu.SemaphoreType.DMA((CHUNKS + 1,)),
         ],
-        compiler_params=params(56),
+        compiler_params=params(61),
         cost_estimate=cost(2 * leaf * leaf * cols, 2 * leaf * leaf),
         name="first",
     )(rhs, inverse, bases)
@@ -259,9 +249,10 @@
     return both(own_ref[:, at], other_ref[:, at])
 
 
-def up_kernel(own_ref, other_ref, w_ref, p_ref, po_ref, vs_ref, q_ref):
+def up_kernel(own_ref, other_ref, w_ref, both_ref, vs_ref, q_ref):
     m10, m20, m10o, m20o, m00o, _, m12o = (block(own_ref, other_ref, k) for k in range(7))
     rank = m10.shape[0]
+    p_ref, po_ref = both_ref[:, : 3 * rank], both_ref[:, 3 * rank :]
     q0 = exact(po_ref[:, :rank], w_ref[0], NT)
     q0o = exact(p_ref[:, :rank], w_ref[0], NT)
     s0o = po_ref[:, :rank] - apply(q0o, m00o, NN)
@@ -272,18 +263,18 @@
     q_ref[...] = jnp.concatenate([s0o, q0, q1o], axis=1)
 
 
-def up(own, other, coupling, p, po):
-    rows, width = p.shape
+def up(own, other, coupling, sums):
+    rows, width = sums.shape[0], sums.shape[1] // 2
     rank = width // 3
     return pl.pallas_call(
         up_kernel,
-        in_specs=whole(5),
+        in_specs=whole(4),
         out_specs=whole(2),
         out_shape=[jax.ShapeDtypeStruct((rows, 2 * rank), F32), jax.ShapeDtypeStruct((rows, width), F32)],
         compiler_params=params(16),
         cost_estimate=cost(32 * rows * rank * rank, 8 * own.size),
         name="up",
-    )(own, other, coupling, p, po)
+    )(own, other, coupling, sums)
 
 
 def down_kernel(own_ref, other_ref, w_ref, vs_ref, b_ref, r2_ref, r3_ref, q_ref, out_ref):
@@ -342,6 +333,32 @@
     )(own, other, bases, state, inverse)
 
 
+def stage_kernel(f_ref, u_ref, f_out, u_out, sems):
+    rows = f_ref.shape[0] // 8
+    copies = [
+        pltpu.make_async_copy(f_ref.at[pl.ds(i * rows, rows)], f_out.at[pl.ds(i * rows, rows)], sems.at[i])
+        for i in range(8)
+    ]
+    copies.append(pltpu.make_async_copy(u_ref, u_out, sems.at[8]))
+    for copy in copies:
+        copy.start()
+    for copy in copies:
+        copy.wait()
+
+
+def stage(inverse, bases):
+    return pl.pallas_call(
+        stage_kernel,
+        in_specs=whole(2, pltpu.HBM),
+        out_specs=whole(2),
+        out_shape=[pltpu.VMEM(inverse.shape, BF16), pltpu.VMEM(bases.shape, BF16)],
+        scratch_shapes=[pltpu.SemaphoreType.DMA((9,))],
+        compiler_params=params(48),
+        cost_estimate=cost(0, 4 * inverse.size),
+        name="stage",
+    )(inverse, bases)
+
+
 def after(value, *others):
     return lax.optimization_barrier((value, *others))[0]
 
@@ -350,26 +367,28 @@
     rank = bases.shape[2]
 
     keep, send = gram(bases)
-    mine = add_rows(keep, swap(send, 1))
-    summed = table(over_chips(mine))
-
-    state, keep, send = first(after(rhs.T, mine), leaf_inverse, bases)
+    rows = split(keep, swap(send, 1))
+    state, keep, send = first(after(rhs.T, *rows), leaf_inverse, bases)
     parts = split(keep, swap(send, 1))
+    mine = add_rows([rows[0]] + [swap(rows[m], 2 * m) for m in (1, 2, 3)])
+    summed = table(over_xz(after(mine, parts[0])))
     part = parts[0] + swap(parts[1], 2) + swap(parts[2], 4) + swap(parts[3], 6)
     pair = part + swap(part, 8)
+    back = over_xz(after(summed, pair))
     p = pair + swap(pair, 16)
     po = swap(pair, 40) + swap(pair, 56)
 
-    back = over_xz(after(summed, pair))
-    own = join([back] + [swap(back, 2 * m) for m in (1, 2, 3)])
+    back, mine = lax.optimization_barrier((back, jnp.concatenate([p, po], axis=1)))
+    parts = [swap(back, 2 * m) for m in (1, 2, 3)]
+    half = join([mine] + [swap(mine, 2 * m) for m in (1, 2, 3)])
+    own = join([after(back, half)] + parts)
     sums = (own, swap(own, 1), coupling)
 
-    vs, q = up(*sums, p, po)
+    vs, q = up(*sums, half)
     v = vs[:, :rank]
-    mine = down(*sums, vs, swap(vs, 64), swap(v, 128), swap(v, 192), q)
-
-    half = join([mine, swap(mine, 2), swap(mine, 4), swap(mine, 6)])
-    return last(half, swap(half, 1), bases, state, leaf_inverse).T
+    inverse_v, bases_v = stage(*lax.optimization_barrier((leaf_inverse, bases, q))[:2])
+    mine = down(*sums, vs, swap(vs, 64), swap(v, 128), swap(v, 192), after(q, inverse_v))
+    return last(mine, swap(mine, 1), bases_v, state, inverse_v).T
 
 
 def solution(mesh):

time: 119 us -> 108 us (0.908)
  blocking collectives: 15.9 us -> 0 us
  starting transfers between devices: 48.9 us -> 55.5 us
  local copies, waits for them, and re-layouts: 5.42 us -> 2.04 us
  Pallas kernels: 20.6 us -> 23.9 us
  other arithmetic: 1.4 us -> 0.03 us
    all_to_all x1 -> x0, blocking collectives: 15.9 us -> none  [over_xz(): lax.all_to_all(value, AXIS, 0, 0, axis_index_groups=line(32, 8), tiled=True)]
    all_to_all x1 -> x2, starting transfers between devices: 14.2 us -> 18.6 us  [over_xz(): lax.all_to_all(value, AXIS, 0, 0, axis_index_groups=line(32, 8), tiled=True)]
    pallas_call x4 -> x5, Pallas kernels: 14.4 us -> 18.4 us  [the longest x1 7.24 us: first(): pl.pallas_call(first_kernel, in_specs=whole(1) + whole(2, pltpu.HBM), out...]
    unnamed x12 -> x8, local copies, waits for them, and re-layouts: 5.42 us -> 2.03 us
    all_to_all x1 -> x2, waiting for transfers between devices: 2.57 us -> 0.01 us  [over_xz(): lax.all_to_all(value, AXIS, 0, 0, axis_index_groups=line(32, 8), tiled=True)]
    ppermute x20 -> x23, waiting for transfers between devices: 23.5 us -> 25.9 us  [swap(): return lax.ppermute(value, AXIS, [(i, i ^ mask) for i in range(N)])]
    ppermute x20 -> x23, starting transfers between devices: 34.6 us -> 36.9 us  [swap(): return lax.ppermute(value, AXIS, [(i, i ^ mask) for i in range(N)])]
  transfers between devices with their start and end apart: 21 -> 25, of which waited for: 13 -> 13; matrix products, arithmetic and copies ran while one was open for 1% -> 0% of each run, Pallas kernels for 6% -> 11%
where the time goes in v3:
time: 108 us
  starting transfers between devices  55.5 us (51%)
  waiting for transfers between devices  25.9 us (24%)
  Pallas kernels  23.9 us (22%)
  local copies, waits for them, and re-layouts  2.04 us (2%)
    ppermute x23, starting transfers between devices, swap(): return lax.ppermute(value, AXIS, [(i, i ^ mask) for i in range(N)])  36.9 us
    ppermute x23, waiting for transfers between devices, swap(): return lax.ppermute(value, AXIS, [(i, i ^ mask) for i in range(N)])  25.9 us
    all_to_all x2, starting transfers between devices, over_xz(): lax.all_to_all(value, AXIS, 0, 0, axis_index_groups=line(32, 8), tiled=True)  18.6 us
    pallas_call x1, Pallas kernels, first(): pl.pallas_call(first_kernel, in_specs=whole(1) + whole(2, pltpu.HBM), out...  7.24 us
    pallas_call x1, Pallas kernels, gram(): pl.pallas_call(gram_kernel, in_specs=whole(1, pltpu.HBM), out_specs=whole...  5.16 us
    pallas_call x1, Pallas kernels, stage(): pl.pallas_call(stage_kernel, in_specs=whole(2, pltpu.HBM), out_specs=whol...  4.46 us
    pallas_call x1, Pallas kernels, last(): pl.pallas_call(last_kernel, in_specs=whole(5), out_specs=whole(1)[0], out...  3.24 us
  transfers between devices with their start and end apart: 25, of which 13 were waited for; matrix products, arithmetic and copies ran while one was open for 0% of the time, Pallas kernels for 11%

profile of v3, /device:TPU:1, one launch (start us, length us, event | category | flops | bytes accessed | tf_op | source)
XLA Modules:
  0.0 107.6 jit_solution(17818466221915387421)
XLA Ops:
  0.0 5.2 %gram.1 = (f32[128,1536]{1,0:T(8,128)}, f32[128,1536]{1,0:T(8,128)}) custom-call(bf16[3,2048,256]{2,1,0:T(8,128)(2,1)} %u_ref.4), custom_call_target="tpu_custom_call" | custom-call | flops 1610612736 | bytes 3145728 | tf_op jit(solution)/shard_map/gram/pallas_call | solution.py:191
  5.2 3.3 %collective-permute-start = (f32[128,1536]{1,0:T(8,128)}, f32[128,1536]{1,0:T(8,128)S(1)}, u32[]{:S(2)}, u32[]{:S(2)}) collective-permute-start(f32[128,1536]{1,0:T(8,128)} %get-tuple-element.32), channel_id=1, source_target_pairs={{0,1},{1,0},{2,3},{3,2},{4,5},{5,4},{6,7},{7,6},{8,9},{9,8},{10,11... | collective-permute-start | bytes 2359304 | tf_op jit(solution)/shard_map/ppermute | solution.py:35
  8.5 2.1 %collective-permute-done.other_ref = f32[128,1536]{1,0:T(8,128)S(1)} collective-permute-done((f32[128,1536]{1,0:T(8,128)}, f32[128,1536]{1,0:T(8,128)S(1)}, u32[]{:S(2)}, u32[]{:S(2)}) %collective-permute-start) | collective-permute-done | bytes 786464 | tf_op jit(solution)/shard_map/ppermute | solution.py:35
  11.9 2.2 %collective-permute-start.2 = (f32[32,1536]{1,0:T(8,128)S(1)}, f32[32,1536]{1,0:T(8,128)S(1)}, u32[]{:S(2)}, u32[]{:S(2)}) collective-permute-start(f32[32,1536]{1,0:T(8,128)S(1)} %get-tuple-element.35), channel_id=1, source_target_pairs={{0,4},{1,5},{2,6},{3,7},{4,0},{5,1},{6,2},{7,3},{8,12},{9,13},{10,... | collective-permute-start | bytes 589832 | tf_op jit(solution)/shard_map/ppermute | solution.py:35
  14.1 1.7 %collective-permute-start.3 = (f32[32,1536]{1,0:T(8,128)S(1)}, f32[32,1536]{1,0:T(8,128)S(1)}, u32[]{:S(2)}, u32[]{:S(2)}) collective-permute-start(f32[32,1536]{1,0:T(8,128)S(1)} %get-tuple-element.36), channel_id=1, source_target_pairs={{0,6},{1,7},{2,4},{3,5},{4,2},{5,3},{6,0},{7,1},{8,14},{9,15},{10,... | collective-permute-start | bytes 589832 | tf_op jit(solution)/shard_map/ppermute | solution.py:35
  15.8 7.2 %first.1 = (f32[64,2048]{1,0:T(8,128)}, f32[32,768]{1,0:T(8,128)}, f32[32,768]{1,0:T(8,128)}) custom-call(bf16[64,2048]{1,0:T(8,128)(2,1)} %bitcast.2, bf16[2048,2048]{1,0:T(8,128)(2,1)} %f_ref.2, bf16[3,2048,256]{2,1,0:T(8,128)(2,1)} %u_ref.4), custom_call_target="tpu_custom_call" | custom-call | flops 536870912 | bytes 8388608 | tf_op jit(solution)/shard_map/first/pallas_call | solution.py:230
  23.0 1.3 %collective-permute-start.4 = (f32[32,768]{1,0:T(8,128)}, f32[32,768]{1,0:T(8,128)S(1)}, u32[]{:S(2)}, u32[]{:S(2)}) collective-permute-start(f32[32,768]{1,0:T(8,128)} %get-tuple-element.39), channel_id=1, source_target_pairs={{0,1},{1,0},{2,3},{3,2},{4,5},{5,4},{6,7},{7,6},{8,9},{9,8},{10,11... | collective-permute-start | bytes 294920 | tf_op jit(solution)/shard_map/ppermute | solution.py:35
  27.2 9.9 %all-to-all-start = ((f32[32,1,1536]{2,1,0:T(1,128)}), f32[32,1,1536]{2,1,0:T(1,128)S(1)}, u32[]{:S(2)}, u32[]{:S(2)}) async-start(f32[32,1,1536]{2,1,0:T(1,128)} %add_rows.1), calls=%async_computation | async-start | bytes 393216 | tf_op jit(solution)/shard_map/all_to_all | solution.py:47
  37.2 3.3 %collective-permute-start.6 = (f32[8,768]{1,0:T(8,128)S(1)}, f32[8,768]{1,0:T(8,128)S(1)}, u32[]{:S(2)}, u32[]{:S(2)}) collective-permute-start(f32[8,768]{1,0:T(8,128)S(1)} %get-tuple-element.43), channel_id=1, source_target_pairs={{0,4},{1,5},{2,6},{3,7},{4,0},{5,1},{6,2},{7,3},{8,12},{9,13},{10,... | collective-permute-start | bytes 73736 | tf_op jit(solution)/shard_map/ppermute | solution.py:35
  41.9 2.7 %collective-permute-done.7 = f32[8,768]{1,0:T(8,128)S(1)} collective-permute-done((f32[8,768]{1,0:T(8,128)S(1)}, f32[8,768]{1,0:T(8,128)S(1)}, u32[]{:S(2)}, u32[]{:S(2)}) %collective-permute-start.7) | collective-permute-done | bytes 24608 | tf_op jit(solution)/shard_map/ppermute | solution.py:35
  44.7 1.3 %collective-permute-start.8 = (f32[8,768]{1,0:T(8,128)S(1)}, f32[8,768]{1,0:T(8,128)S(1)}, u32[]{:S(2)}, u32[]{:S(2)}) collective-permute-start(f32[8,768]{1,0:T(8,128)S(1)} %add_add_fusion), channel_id=1, source_target_pairs={{0,8},{1,9},{2,10},{3,11},{4,12},{5,13},{6,14},{7,15},{8,0},{9,1},... | collective-permute-start | bytes 73736 | tf_op jit(solution)/shard_map/ppermute | solution.py:35
  46.0 1.7 %collective-permute-done.8 = f32[8,768]{1,0:T(8,128)S(1)} collective-permute-done((f32[8,768]{1,0:T(8,128)S(1)}, f32[8,768]{1,0:T(8,128)S(1)}, u32[]{:S(2)}, u32[]{:S(2)}) %collective-permute-start.8) | collective-permute-done | bytes 24608 | tf_op jit(solution)/shard_map/ppermute | solution.py:35
  48.6 8.6 %all-to-all-start.1 = ((f32[32,1,2048]{2,1,0:T(1,128)}), f32[32,1,2048]{2,1,0:T(1,128)S(1)}, u32[]{:S(2)}, u32[]{:S(2)}) async-start(f32[32,1,2048]{2,1,0:T(1,128)} %table.1), calls=%async_computation.1 | async-start | bytes 524288 | tf_op jit(solution)/shard_map/all_to_all | solution.py:47
  57.2 2.2 %collective-permute-start.9 = (f32[8,768]{1,0:T(8,128)S(1)}, f32[8,768]{1,0:T(8,128)S(1)}, u32[]{:S(2)}, u32[]{:S(2)}) collective-permute-start(f32[8,768]{1,0:T(8,128)S(1)} %add.21), channel_id=1, source_target_pairs={{0,16},{1,17},{2,18},{3,19},{4,20},{5,21},{6,22},{7,23},{8,24},{9,... | collective-permute-start | bytes 73736 | tf_op jit(solution)/shard_map/ppermute | solution.py:35
  59.4 2.4 %collective-permute-start.11 = (f32[8,768]{1,0:T(8,128)S(1)}, f32[8,768]{1,0:T(8,128)S(1)}, u32[]{:S(2)}, u32[]{:S(2)}) collective-permute-start(f32[8,768]{1,0:T(8,128)S(1)} %add.21), channel_id=1, source_target_pairs={{0,56},{1,57},{2,58},{3,59},{4,60},{5,61},{6,62},{7,63},{8,48},{9,... | collective-permute-start | bytes 73736 | tf_op jit(solution)/shard_map/ppermute | solution.py:35
  63.4 4.7 %collective-permute-done.10 = f32[8,768]{1,0:T(8,128)S(1)} collective-permute-done((f32[8,768]{1,0:T(8,128)S(1)}, f32[8,768]{1,0:T(8,128)S(1)}, u32[]{:S(2)}, u32[]{:S(2)}) %collective-permute-start.10) | collective-permute-done | bytes 24608 | tf_op jit(solution)/shard_map/ppermute | solution.py:35
  68.9 2.5 %collective-permute-start.15 = (f32[32,1,2048]{2,1,0:T(1,128)S(1)}, f32[32,1,2048]{2,1,0:T(1,128)S(1)}, u32[]{:S(2)}, u32[]{:S(2)}) collective-permute-start(f32[32,1,2048]{2,1,0:T(1,128)S(1)} %all-to-all-done.1.refs_0_), channel_id=1, source_target_pairs={{0,2},{1,3},{2,0},{3,1},{4,6},{5,7},{6,4},{7,5},{8,10},{9,11},{10,... | collective-permute-start | bytes 786440 | tf_op jit(solution)/shard_map/ppermute | solution.py:35
  73.2 5.1 %collective-permute-done.14.refs_3_ = f32[8,1536]{1,0:T(8,128)S(1)} collective-permute-done((f32[8,1536]{1,0:T(8,128)S(1)}, f32[8,1536]{1,0:T(8,128)S(1)}, u32[]{:S(2)}, u32[]{:S(2)}) %collective-permute-start.14) | collective-permute-done | bytes 49184 | tf_op jit(solution)/shard_map/ppermute | solution.py:35
  79.1 3.1 %collective-permute-done.12.refs_1_ = f32[8,1536]{1,0:T(8,128)S(1)} collective-permute-done((f32[8,1536]{1,0:T(8,128)S(1)}, f32[8,1536]{1,0:T(8,128)S(1)}, u32[]{:S(2)}, u32[]{:S(2)}) %collective-permute-start.12) | collective-permute-done | bytes 49184 | tf_op jit(solution)/shard_map/ppermute | solution.py:35
  82.4 7.3 %collective-permute-start.18 = (f32[128,2048]{1,0:T(8,128)S(1)}, f32[128,2048]{1,0:T(8,128)S(1)}, u32[]{:S(2)}, u32[]{:S(2)}) collective-permute-start(f32[128,2048]{1,0:T(8,128)S(1)} %join.3.own_ref), channel_id=1, source_target_pairs={{0,1},{1,0},{2,3},{3,2},{4,5},{5,4},{6,7},{7,6},{8,9},{9,8},{10,11... | collective-permute-start | bytes 3145736 | tf_op jit(solution)/shard_map/ppermute | solution.py:35
  89.7 2.3 %collective-permute-done.18.other_ref = f32[128,2048]{1,0:T(8,128)S(1)} collective-permute-done((f32[128,2048]{1,0:T(8,128)S(1)}, f32[128,2048]{1,0:T(8,128)S(1)}, u32[]{:S(2)}, u32[]{:S(2)}) %collective-permute-start.18) | collective-permute-done | bytes 1048608 | tf_op jit(solution)/shard_map/ppermute | solution.py:35
  94.0 1.8 %collective-permute-start.21 = (f32[32,256]{1,0:T(8,128)S(1)}, f32[32,256]{1,0:T(8,128)S(1)}, u32[]{:S(2)}, u32[]{:S(2)}) collective-permute-start(f32[32,256]{1,0:T(8,128)S(1)} %slice.3), channel_id=1, source_target_pairs={{0,192},{1,193},{2,194},{3,195},{4,196},{5,197},{6,198},{7,199},{8... | collective-permute-start | bytes 98312 | tf_op jit(solution)/shard_map/ppermute | solution.py:35
  96.5 4.5 %stage.1 = (bf16[2048,2048]{1,0:T(8,128)(2,1)S(1)}, bf16[3,2048,256]{2,1,0:T(8,128)(2,1)S(1)}) custom-call(bf16[2048,2048]{1,0:T(8,128)(2,1)} %f_ref.2, bf16[3,2048,256]{2,1,0:T(8,128)(2,1)} %u_ref.4), custom_call_target="tpu_custom_call" | custom-call | bytes 16777216 | tf_op jit(solution)/shard_map/stage/pallas_call | solution.py:350
  104.4 3.2 %last.1 = bf16[64,2048]{1,0:T(8,128)(2,1)} custom-call(f32[32,768]{1,0:T(8,128)S(1)} %down.1.own_ref, f32[32,768]{1,0:T(8,128)S(1)} %collective-permute-done.22.other_ref, bf16[3,2048,256]{2,1,0:T(8,128)(2,1)S(1)} %get-tuple-element.55.u_ref, f32[64,2048]{1,0:T(8,128)S(1)} %copy-done.2, bf16[2048,2048]{1,0:T(8,128)(2,1)S(1)} %get-tuple-element.53.f_ref), custom_call_target="tpu_custom_call" | custom-call | flops 536870912 | bytes 8388608 | tf_op jit(solution)/shard_map/last/pallas_call | solution.py:325
  (52 shorter events, 17.8 us)
Async XLA Ops:
  5.2 5.5 %collective-permute-start = (f32[128,1536]{1,0:T(8,128)}, f32[128,1536]{1,0:T(8,128)S(1)}, u32[]{:S(2)}, u32[]{:S(2)}) collective-permute-start(f32[128,1536]{1,0:T(8,128)} %get-tuple-element.32), channel_id=1, source_target_pairs={{0,1},{1,0},{2,3},{3,2},{4,5},{5,4},{6,7},{7,6},{8,9},{9,8},{10,11... | collective-permute-start | bytes 2359304 | tf_op jit(solution)/shard_map/ppermute | solution.py:35
  11.8 14.6 %collective-permute-start.1 = (f32[32,1536]{1,0:T(8,128)S(1)}, f32[32,1536]{1,0:T(8,128)S(1)}, u32[]{:S(2)}, u32[]{:S(2)}) collective-permute-start(f32[32,1536]{1,0:T(8,128)S(1)} %get-tuple-element.34), channel_id=1, source_target_pairs={{0,2},{1,3},{2,0},{3,1},{4,6},{5,7},{6,4},{7,5},{8,10},{9,11},{10,... | collective-permute-start | bytes 589832 | tf_op jit(solution)/shard_map/ppermute | solution.py:35
  11.9 14.5 %collective-permute-start.2 = (f32[32,1536]{1,0:T(8,128)S(1)}, f32[32,1536]{1,0:T(8,128)S(1)}, u32[]{:S(2)}, u32[]{:S(2)}) collective-permute-start(f32[32,1536]{1,0:T(8,128)S(1)} %get-tuple-element.35), channel_id=1, source_target_pairs={{0,4},{1,5},{2,6},{3,7},{4,0},{5,1},{6,2},{7,3},{8,12},{9,13},{10,... | collective-permute-start | bytes 589832 | tf_op jit(solution)/shard_map/ppermute | solution.py:35
  14.1 12.3 %collective-permute-start.3 = (f32[32,1536]{1,0:T(8,128)S(1)}, f32[32,1536]{1,0:T(8,128)S(1)}, u32[]{:S(2)}, u32[]{:S(2)}) collective-permute-start(f32[32,1536]{1,0:T(8,128)S(1)} %get-tuple-element.36), channel_id=1, source_target_pairs={{0,6},{1,7},{2,4},{3,5},{4,2},{5,3},{6,0},{7,1},{8,14},{9,15},{10,... | collective-permute-start | bytes 589832 | tf_op jit(solution)/shard_map/ppermute | solution.py:35
  23.0 2.5 %collective-permute-start.4 = (f32[32,768]{1,0:T(8,128)}, f32[32,768]{1,0:T(8,128)S(1)}, u32[]{:S(2)}, u32[]{:S(2)}) collective-permute-start(f32[32,768]{1,0:T(8,128)} %get-tuple-element.39), channel_id=1, source_target_pairs={{0,1},{1,0},{2,3},{3,2},{4,5},{5,4},{6,7},{7,6},{8,9},{9,8},{10,11... | collective-permute-start | bytes 294920 | tf_op jit(solution)/shard_map/ppermute | solution.py:35
  27.2 20.6 %all-to-all-start = ((f32[32,1,1536]{2,1,0:T(1,128)}), f32[32,1,1536]{2,1,0:T(1,128)S(1)}, u32[]{:S(2)}, u32[]{:S(2)}) async-start(f32[32,1,1536]{2,1,0:T(1,128)} %add_rows.1), calls=%async_computation | async-start | bytes 393216 | tf_op jit(solution)/shard_map/all_to_all | solution.py:47
  37.1 3.9 %collective-permute-start.5 = (f32[8,768]{1,0:T(8,128)S(1)}, f32[8,768]{1,0:T(8,128)S(1)}, u32[]{:S(2)}, u32[]{:S(2)}) collective-permute-start(f32[8,768]{1,0:T(8,128)S(1)} %get-tuple-element.42), channel_id=1, source_target_pairs={{0,2},{1,3},{2,0},{3,1},{4,6},{5,7},{6,4},{7,5},{8,10},{9,11},{10,... | collective-permute-start | bytes 73736 | tf_op jit(solution)/shard_map/ppermute | solution.py:35
  37.2 4.7 %collective-permute-start.6 = (f32[8,768]{1,0:T(8,128)S(1)}, f32[8,768]{1,0:T(8,128)S(1)}, u32[]{:S(2)}, u32[]{:S(2)}) collective-permute-start(f32[8,768]{1,0:T(8,128)S(1)} %get-tuple-element.43), channel_id=1, source_target_pairs={{0,4},{1,5},{2,6},{3,7},{4,0},{5,1},{6,2},{7,3},{8,12},{9,13},{10,... | collective-permute-start | bytes 73736 | tf_op jit(solution)/shard_map/ppermute | solution.py:35
  40.5 4.2 %collective-permute-start.7 = (f32[8,768]{1,0:T(8,128)S(1)}, f32[8,768]{1,0:T(8,128)S(1)}, u32[]{:S(2)}, u32[]{:S(2)}) collective-permute-start(f32[8,768]{1,0:T(8,128)S(1)} %get-tuple-element.44), channel_id=1, source_target_pairs={{0,6},{1,7},{2,4},{3,5},{4,2},{5,3},{6,0},{7,1},{8,14},{9,15},{10,... | collective-permute-start | bytes 73736 | tf_op jit(solution)/shard_map/ppermute | solution.py:35
  44.7 3.1 %collective-permute-start.8 = (f32[8,768]{1,0:T(8,128)S(1)}, f32[8,768]{1,0:T(8,128)S(1)}, u32[]{:S(2)}, u32[]{:S(2)}) collective-permute-start(f32[8,768]{1,0:T(8,128)S(1)} %add_add_fusion), channel_id=1, source_target_pairs={{0,8},{1,9},{2,10},{3,11},{4,12},{5,13},{6,14},{7,15},{8,0},{9,1},... | collective-permute-start | bytes 73736 | tf_op jit(solution)/shard_map/ppermute | solution.py:35
  48.6 19.5 %all-to-all-start.1 = ((f32[32,1,2048]{2,1,0:T(1,128)}), f32[32,1,2048]{2,1,0:T(1,128)S(1)}, u32[]{:S(2)}, u32[]{:S(2)}) async-start(f32[32,1,2048]{2,1,0:T(1,128)} %table.1), calls=%async_computation.1 | async-start | bytes 524288 | tf_op jit(solution)/shard_map/all_to_all | solution.py:47
  57.2 5.8 %collective-permute-start.9 = (f32[8,768]{1,0:T(8,128)S(1)}, f32[8,768]{1,0:T(8,128)S(1)}, u32[]{:S(2)}, u32[]{:S(2)}) collective-permute-start(f32[8,768]{1,0:T(8,128)S(1)} %add.21), channel_id=1, source_target_pairs={{0,16},{1,17},{2,18},{3,19},{4,20},{5,21},{6,22},{7,23},{8,24},{9,... | collective-permute-start | bytes 73736 | tf_op jit(solution)/shard_map/ppermute | solution.py:35
  59.4 3.9 %collective-permute-start.11 = (f32[8,768]{1,0:T(8,128)S(1)}, f32[8,768]{1,0:T(8,128)S(1)}, u32[]{:S(2)}, u32[]{:S(2)}) collective-permute-start(f32[8,768]{1,0:T(8,128)S(1)} %add.21), channel_id=1, source_target_pairs={{0,56},{1,57},{2,58},{3,59},{4,60},{5,61},{6,62},{7,63},{8,48},{9,... | collective-permute-start | bytes 73736 | tf_op jit(solution)/shard_map/ppermute | solution.py:35
  61.8 6.2 %collective-permute-start.10 = (f32[8,768]{1,0:T(8,128)S(1)}, f32[8,768]{1,0:T(8,128)S(1)}, u32[]{:S(2)}, u32[]{:S(2)}) collective-permute-start(f32[8,768]{1,0:T(8,128)S(1)} %add.21), channel_id=1, source_target_pairs={{0,40},{1,41},{2,42},{3,43},{4,44},{5,45},{6,46},{7,47},{8,32},{9,... | collective-permute-start | bytes 73736 | tf_op jit(solution)/shard_map/ppermute | solution.py:35
  68.1 14.1 %collective-permute-start.17 = (f32[32,1,2048]{2,1,0:T(1,128)S(1)}, f32[32,1,2048]{2,1,0:T(1,128)S(1)}, u32[]{:S(2)}, u32[]{:S(2)}) collective-permute-start(f32[32,1,2048]{2,1,0:T(1,128)S(1)} %all-to-all-done.1.refs_0_), channel_id=1, source_target_pairs={{0,6},{1,7},{2,4},{3,5},{4,2},{5,3},{6,0},{7,1},{8,14},{9,15},{10,... | collective-permute-start | bytes 786440 | tf_op jit(solution)/shard_map/ppermute | solution.py:35
  68.9 13.3 %collective-permute-start.16 = (f32[32,1,2048]{2,1,0:T(1,128)S(1)}, f32[32,1,2048]{2,1,0:T(1,128)S(1)}, u32[]{:S(2)}, u32[]{:S(2)}) collective-permute-start(f32[32,1,2048]{2,1,0:T(1,128)S(1)} %all-to-all-done.1.refs_0_), channel_id=1, source_target_pairs={{0,4},{1,5},{2,6},{3,7},{4,0},{5,1},{6,2},{7,3},{8,12},{9,13},{10,... | collective-permute-start | bytes 786440 | tf_op jit(solution)/shard_map/ppermute | solution.py:35
  68.9 13.3 %collective-permute-start.15 = (f32[32,1,2048]{2,1,0:T(1,128)S(1)}, f32[32,1,2048]{2,1,0:T(1,128)S(1)}, u32[]{:S(2)}, u32[]{:S(2)}) collective-permute-start(f32[32,1,2048]{2,1,0:T(1,128)S(1)} %all-to-all-done.1.refs_0_), channel_id=1, source_target_pairs={{0,2},{1,3},{2,0},{3,1},{4,6},{5,7},{6,4},{7,5},{8,10},{9,11},{10,... | collective-permute-start | bytes 786440 | tf_op jit(solution)/shard_map/ppermute | solution.py:35
  71.4 6.9 %collective-permute-start.14 = (f32[8,1536]{1,0:T(8,128)S(1)}, f32[8,1536]{1,0:T(8,128)S(1)}, u32[]{:S(2)}, u32[]{:S(2)}) collective-permute-start(f32[8,1536]{1,0:T(8,128)S(1)} %pad_maximum_fusion.refs_0_), channel_id=1, source_target_pairs={{0,6},{1,7},{2,4},{3,5},{4,2},{5,3},{6,0},{7,1},{8,14},{9,15},{10,... | collective-permute-start | bytes 147464 | tf_op jit(solution)/shard_map/ppermute | solution.py:35
  72.2 7.0 %collective-permute-start.13 = (f32[8,1536]{1,0:T(8,128)S(1)}, f32[8,1536]{1,0:T(8,128)S(1)}, u32[]{:S(2)}, u32[]{:S(2)}) collective-permute-start(f32[8,1536]{1,0:T(8,128)S(1)} %pad_maximum_fusion.refs_0_), channel_id=1, source_target_pairs={{0,4},{1,5},{2,6},{3,7},{4,0},{5,1},{6,2},{7,3},{8,12},{9,13},{10,... | collective-permute-start | bytes 147464 | tf_op jit(solution)/shard_map/ppermute | solution.py:35
  78.4 3.8 %collective-permute-start.12 = (f32[8,1536]{1,0:T(8,128)S(1)}, f32[8,1536]{1,0:T(8,128)S(1)}, u32[]{:S(2)}, u32[]{:S(2)}) collective-permute-start(f32[8,1536]{1,0:T(8,128)S(1)} %pad_maximum_fusion.refs_0_), channel_id=1, source_target_pairs={{0,2},{1,3},{2,0},{3,1},{4,6},{5,7},{6,4},{7,5},{8,10},{9,11},{10,... | collective-permute-start | bytes 147464 | tf_op jit(solution)/shard_map/ppermute | solution.py:35
  82.4 9.6 %collective-permute-start.18 = (f32[128,2048]{1,0:T(8,128)S(1)}, f32[128,2048]{1,0:T(8,128)S(1)}, u32[]{:S(2)}, u32[]{:S(2)}) collective-permute-start(f32[128,2048]{1,0:T(8,128)S(1)} %join.3.own_ref), channel_id=1, source_target_pairs={{0,1},{1,0},{2,3},{3,2},{4,5},{5,4},{6,7},{7,6},{8,9},{9,8},{10,11... | collective-permute-start | bytes 3145736 | tf_op jit(solution)/shard_map/ppermute | solution.py:35
  92.8 8.2 %collective-permute-start.19 = (f32[32,512]{1,0:T(8,128)S(1)}, f32[32,512]{1,0:T(8,128)S(1)}, u32[]{:S(2)}, u32[]{:S(2)}) collective-permute-start(f32[32,512]{1,0:T(8,128)S(1)} %get-tuple-element.49.vs_ref), channel_id=1, source_target_pairs={{0,64},{1,65},{2,66},{3,67},{4,68},{5,69},{6,70},{7,71},{8,72},{9,... | collective-permute-start | bytes 196616 | tf_op jit(solution)/shard_map/ppermute | solution.py:35
  94.0 6.9 %collective-permute-start.21 = (f32[32,256]{1,0:T(8,128)S(1)}, f32[32,256]{1,0:T(8,128)S(1)}, u32[]{:S(2)}, u32[]{:S(2)}) collective-permute-start(f32[32,256]{1,0:T(8,128)S(1)} %slice.3), channel_id=1, source_target_pairs={{0,192},{1,193},{2,194},{3,195},{4,196},{5,197},{6,198},{7,199},{8... | collective-permute-start | bytes 98312 | tf_op jit(solution)/shard_map/ppermute | solution.py:35
  95.8 5.1 %collective-permute-start.20 = (f32[32,256]{1,0:T(8,128)S(1)}, f32[32,256]{1,0:T(8,128)S(1)}, u32[]{:S(2)}, u32[]{:S(2)}) collective-permute-start(f32[32,256]{1,0:T(8,128)S(1)} %slice.3), channel_id=1, source_target_pairs={{0,128},{1,129},{2,130},{3,131},{4,132},{5,133},{6,134},{7,135},{8... | collective-permute-start | bytes 98312 | tf_op jit(solution)/shard_map/ppermute | solution.py:35
  (5 other events, 102.4 us)

commit v4 on v3

--- a/solution.py
+++ b/solution.py
@@ -102,25 +102,53 @@
     )(keep, other)
 
 
-def join_kernel(*refs):
-    parts, out_ref = refs[:4], refs[4]
-    rows = parts[0].shape[0]
+def pack_kernel(sums_ref, p_ref, po_ref, out_ref):
+    rows, rank = sums_ref.shape[0], p_ref.shape[1] // 3
+    out_ref[:rows] = sums_ref[...]
+    for k in range(6):
+        value = (p_ref if k < 3 else po_ref)[:, k % 3 * rank : (k % 3 + 1) * rank]
+        for r in range(value.shape[0]):
+            out_ref[rows + k, :, r * rank : (r + 1) * rank] = value[r : r + 1]
+
+
+def pack(sums, p, po):
+    rows, _, width = sums.shape
+    return pl.pallas_call(
+        pack_kernel,
+        in_specs=whole(3),
+        out_specs=whole(1)[0],
+        out_shape=jax.ShapeDtypeStruct((rows + 6, 1, width), F32),
+        compiler_params=params(16),
+        cost_estimate=cost(0, 8 * rows * width),
+        name="pack",
+    )(sums, p, po)
+
+
+def unpack_kernel(*refs):
+    parts, own_ref, half_ref = refs[:4], refs[4], refs[5]
+    rows, rank = own_ref.shape[0] // 4, half_ref.shape[1] // 6
+    cols = half_ref.shape[0] // 4
     y = (lax.axis_index(AXIS) >> 1) & 3
     for m, part in enumerate(parts):
         at = pl.ds(pl.multiple_of((y ^ m) * rows, rows), rows)
-        out_ref[at, :] = part[...].reshape(rows, out_ref.shape[1])
-
-
-def join(parts):
-    rows, width = parts[0].shape[0], parts[0].shape[-1]
-    return pl.pallas_call(
-        join_kernel,
+        own_ref[at, :] = part[:rows].reshape(rows, own_ref.shape[1])
+        at = pl.ds(pl.multiple_of((y ^ m) * cols, cols), cols)
+        for k in range(6):
+            row = part[rows + k]
+            value = jnp.concatenate([row[:, r * rank : (r + 1) * rank] for r in range(cols)], axis=0)
+            half_ref[at, k * rank : (k + 1) * rank] = value
+
+
+def unpack(parts, cols, rank):
+    rows, width = parts[0].shape[0] - 6, parts[0].shape[2]
+    return pl.pallas_call(
+        unpack_kernel,
         in_specs=whole(4),
-        out_specs=whole(1)[0],
-        out_shape=jax.ShapeDtypeStruct((4 * rows, width), F32),
+        out_specs=whole(2),
+        out_shape=[jax.ShapeDtypeStruct((4 * rows, width), F32), jax.ShapeDtypeStruct((4 * cols, 6 * rank), F32)],
         compiler_params=params(16),
         cost_estimate=cost(0, 32 * rows * width),
-        name="join",
+        name="unpack",
     )(*parts)
 
 
@@ -169,36 +197,24 @@
 PAIRS = ((1, 0), (2, 0), (0, 0), (1, 1), (1, 2), (2, 2))
 
 
-def gram_kernel(u_ref, keep_ref, send_ref, u_buf, g_buf, sems):
+def gram_kernel(u_ref, keep_ref, send_ref, g_buf):
     rank = u_ref.shape[2]
-    copies = [pltpu.make_async_copy(u_ref.at[k], u_buf.at[k], sems.at[k]) for k in range(3)]
-    for copy in copies:
-        copy.start()
-    ready = 0
-    for a, b in sorted(PAIRS, key=max):
-        while ready <= max(a, b):
-            copies[ready].wait()
-            ready += 1
-        place = PAIRS.index((a, b))
-        g_buf[:, place * rank : (place + 1) * rank] = dot(u_buf[a], u_buf[b], TN)
+    for place, (a, b) in enumerate(PAIRS):
+        g_buf[:, place * rank : (place + 1) * rank] = dot(u_ref[a], u_ref[b], TN)
     split_halves(g_buf[...], keep_ref, send_ref)
 
 
 def gram(bases):
-    levels, leaf, rank = bases.shape
+    leaf, rank = bases.shape[1:]
     width = len(PAIRS) * rank
     shape = jax.ShapeDtypeStruct((rank // 2, width), F32)
     return pl.pallas_call(
         gram_kernel,
-        in_specs=whole(1, pltpu.HBM),
+        in_specs=whole(1),
         out_specs=whole(2),
         out_shape=[shape, shape],
-        scratch_shapes=[
-            pltpu.VMEM((levels, leaf, rank), BF16),
-            pltpu.VMEM((rank, width), F32),
-            pltpu.SemaphoreType.DMA((levels,)),
-        ],
-        compiler_params=params(56),
+        scratch_shapes=[pltpu.VMEM((rank, width), F32)],
+        compiler_params=params(24),
         cost_estimate=cost(12 * leaf * rank * rank, 6 * leaf * rank),
         name="gram",
     )(bases)
@@ -378,10 +394,8 @@
     p = pair + swap(pair, 16)
     po = swap(pair, 40) + swap(pair, 56)
 
-    back, mine = lax.optimization_barrier((back, jnp.concatenate([p, po], axis=1)))
-    parts = [swap(back, 2 * m) for m in (1, 2, 3)]
-    half = join([mine] + [swap(mine, 2 * m) for m in (1, 2, 3)])
-    own = join([after(back, half)] + parts)
+    mine = pack(back, p, po)
+    own, half = unpack([mine] + [swap(mine, 2 * m) for m in (1, 2, 3)], p.shape[0], rank)
     sums = (own, swap(own, 1), coupling)
 
     vs, q = up(*sums, half)

time: 108 us -> 103 us (0.954)
  Pallas kernels: 23.9 us -> 20.6 us
  starting transfers between devices: 55.5 us -> 53.4 us
    pallas_call x3, Pallas kernels: 5.34 us -> 2.08 us  [the longest x1 1.84 us: gram(): pl.pallas_call(gram_kernel, in_specs=whole(1), out_specs=whole(2), out_sh...]
    ppermute x23 -> x20, starting transfers between devices: 36.9 us -> 34.8 us  [swap(): return lax.ppermute(value, AXIS, [(i, i ^ mask) for i in range(N)])]
    ppermute x23 -> x20, waiting for transfers between devices: 25.9 us -> 25.1 us  [swap(): return lax.ppermute(value, AXIS, [(i, i ^ mask) for i in range(N)])]
  transfers between devices with their start and end apart: 25 -> 22, of which waited for: 13 -> 12; matrix products, arithmetic and copies ran while one was open for 0% -> 0% of each run, Pallas kernels for 11% -> 11%
where the time goes in v4:
time: 103 us; the launch traced here: 102 us
  starting transfers between devices  53.4 us (52%)
  waiting for transfers between devices  25.1 us (24%)
  Pallas kernels  20.6 us (20%)
  local copies, waits for them, and re-layouts  2.79 us (3%)
    ppermute x20, starting transfers between devices, swap(): return lax.ppermute(value, AXIS, [(i, i ^ mask) for i in range(N)])  34.8 us
    ppermute x20, waiting for transfers between devices, swap(): return lax.ppermute(value, AXIS, [(i, i ^ mask) for i in range(N)])  25.1 us
    all_to_all x2, starting transfers between devices, over_xz(): lax.all_to_all(value, AXIS, 0, 0, axis_index_groups=line(32, 8), tiled=True)  18.6 us
    pallas_call x1, Pallas kernels, first(): pl.pallas_call(first_kernel, in_specs=whole(1) + whole(2, pltpu.HBM), out...  7.18 us
    pallas_call x1, Pallas kernels, stage(): pl.pallas_call(stage_kernel, in_specs=whole(2, pltpu.HBM), out_specs=whol...  4.46 us
    pallas_call x1, Pallas kernels, last(): pl.pallas_call(last_kernel, in_specs=whole(5), out_specs=whole(1)[0], out...  3.24 us
    unnamed x8, local copies, waits for them, and re-layouts  2.79 us
  transfers between devices with their start and end apart: 22, of which 12 were waited for; matrix products, arithmetic and copies ran while one was open for 0% of the time, Pallas kernels for 11%

profile of v4, /device:TPU:1, one launch (start us, length us, event | category | flops | bytes accessed | tf_op | source)
XLA Modules:
  0.0 102.1 jit_solution(5857929670742483745)
XLA Ops:
  0.0 1.9 %copy-done = bf16[3,2048,256]{2,1,0:T(8,128)(2,1)S(1)} copy-done((bf16[3,2048,256]{2,1,0:T(8,128)(2,1)S(1)}, bf16[3,2048,256]{2,1,0:T(8,128)(2,1)}, u32[]{:S(2)}) %copy-start) | copy-done | bytes 3145752
  1.9 1.8 %gram.1 = (f32[128,1536]{1,0:T(8,128)S(1)}, f32[128,1536]{1,0:T(8,128)S(1)}) custom-call(bf16[3,2048,256]{2,1,0:T(8,128)(2,1)S(1)} %copy-done), custom_call_target="tpu_custom_call" | custom-call | flops 1610612736 | bytes 3145728 | tf_op jit(solution)/shard_map/gram/pallas_call | solution.py:211
  3.7 3.3 %collective-permute-start = (f32[128,1536]{1,0:T(8,128)S(1)}, f32[128,1536]{1,0:T(8,128)S(1)}, u32[]{:S(2)}, u32[]{:S(2)}) collective-permute-start(f32[128,1536]{1,0:T(8,128)S(1)} %get-tuple-element.31), channel_id=1, source_target_pairs={{0,1},{1,0},{2,3},{3,2},{4,5},{5,4},{6,7},{7,6},{8,9},{9,8},{10,11... | collective-permute-start | bytes 2359304 | tf_op jit(solution)/shard_map/ppermute | solution.py:35
  7.1 1.9 %collective-permute-done.other_ref = f32[128,1536]{1,0:T(8,128)S(1)} collective-permute-done((f32[128,1536]{1,0:T(8,128)S(1)}, f32[128,1536]{1,0:T(8,128)S(1)}, u32[]{:S(2)}, u32[]{:S(2)}) %collective-permute-start) | collective-permute-done | bytes 786464 | tf_op jit(solution)/shard_map/ppermute | solution.py:35
  9.2 2.2 %collective-permute-start.2 = (f32[32,1536]{1,0:T(8,128)S(1)}, f32[32,1536]{1,0:T(8,128)S(1)}, u32[]{:S(2)}, u32[]{:S(2)}) collective-permute-start(f32[32,1536]{1,0:T(8,128)S(1)} %get-tuple-element.34), channel_id=1, source_target_pairs={{0,4},{1,5},{2,6},{3,7},{4,0},{5,1},{6,2},{7,3},{8,12},{9,13},{10,... | collective-permute-start | bytes 589832 | tf_op jit(solution)/shard_map/ppermute | solution.py:35
  11.3 1.7 %collective-permute-start.3 = (f32[32,1536]{1,0:T(8,128)S(1)}, f32[32,1536]{1,0:T(8,128)S(1)}, u32[]{:S(2)}, u32[]{:S(2)}) collective-permute-start(f32[32,1536]{1,0:T(8,128)S(1)} %get-tuple-element.35), channel_id=1, source_target_pairs={{0,6},{1,7},{2,4},{3,5},{4,2},{5,3},{6,0},{7,1},{8,14},{9,15},{10,... | collective-permute-start | bytes 589832 | tf_op jit(solution)/shard_map/ppermute | solution.py:35
  13.0 7.2 %first.1 = (f32[64,2048]{1,0:T(8,128)}, f32[32,768]{1,0:T(8,128)}, f32[32,768]{1,0:T(8,128)}) custom-call(bf16[64,2048]{1,0:T(8,128)(2,1)} %bitcast.2, bf16[2048,2048]{1,0:T(8,128)(2,1)} %f_ref.2, bf16[3,2048,256]{2,1,0:T(8,128)(2,1)} %u_ref.4), custom_call_target="tpu_custom_call" | custom-call | flops 536870912 | bytes 8388608 | tf_op jit(solution)/shard_map/first/pallas_call | solution.py:246
  20.2 1.3 %collective-permute-start.4 = (f32[32,768]{1,0:T(8,128)}, f32[32,768]{1,0:T(8,128)S(1)}, u32[]{:S(2)}, u32[]{:S(2)}) collective-permute-start(f32[32,768]{1,0:T(8,128)} %get-tuple-element.38), channel_id=1, source_target_pairs={{0,1},{1,0},{2,3},{3,2},{4,5},{5,4},{6,7},{7,6},{8,9},{9,8},{10,11... | collective-permute-start | bytes 294920 | tf_op jit(solution)/shard_map/ppermute | solution.py:35
  24.3 10.0 %all-to-all-start = ((f32[32,1,1536]{2,1,0:T(1,128)}), f32[32,1,1536]{2,1,0:T(1,128)S(1)}, u32[]{:S(2)}, u32[]{:S(2)}) async-start(f32[32,1,1536]{2,1,0:T(1,128)} %add_rows.1), calls=%async_computation | async-start | bytes 393216 | tf_op jit(solution)/shard_map/all_to_all | solution.py:47
  34.5 3.2 %collective-permute-start.6 = (f32[8,768]{1,0:T(8,128)S(1)}, f32[8,768]{1,0:T(8,128)S(1)}, u32[]{:S(2)}, u32[]{:S(2)}) collective-permute-start(f32[8,768]{1,0:T(8,128)S(1)} %get-tuple-element.42), channel_id=1, source_target_pairs={{0,4},{1,5},{2,6},{3,7},{4,0},{5,1},{6,2},{7,3},{8,12},{9,13},{10,... | collective-permute-start | bytes 73736 | tf_op jit(solution)/shard_map/ppermute | solution.py:35
  39.1 2.7 %collective-permute-done.7 = f32[8,768]{1,0:T(8,128)S(1)} collective-permute-done((f32[8,768]{1,0:T(8,128)S(1)}, f32[8,768]{1,0:T(8,128)S(1)}, u32[]{:S(2)}, u32[]{:S(2)}) %collective-permute-start.7) | collective-permute-done | bytes 24608 | tf_op jit(solution)/shard_map/ppermute | solution.py:35
  41.9 1.3 %collective-permute-start.8 = (f32[8,768]{1,0:T(8,128)S(1)}, f32[8,768]{1,0:T(8,128)S(1)}, u32[]{:S(2)}, u32[]{:S(2)}) collective-permute-start(f32[8,768]{1,0:T(8,128)S(1)} %add_add_fusion), channel_id=1, source_target_pairs={{0,8},{1,9},{2,10},{3,11},{4,12},{5,13},{6,14},{7,15},{8,0},{9,1},... | collective-permute-start | bytes 73736 | tf_op jit(solution)/shard_map/ppermute | solution.py:35
  43.2 1.7 %collective-permute-done.8 = f32[8,768]{1,0:T(8,128)S(1)} collective-permute-done((f32[8,768]{1,0:T(8,128)S(1)}, f32[8,768]{1,0:T(8,128)S(1)}, u32[]{:S(2)}, u32[]{:S(2)}) %collective-permute-start.8) | collective-permute-done | bytes 24608 | tf_op jit(solution)/shard_map/ppermute | solution.py:35
  45.8 8.6 %all-to-all-start.1 = ((f32[32,1,2048]{2,1,0:T(1,128)}), f32[32,1,2048]{2,1,0:T(1,128)S(1)}, u32[]{:S(2)}, u32[]{:S(2)}) async-start(f32[32,1,2048]{2,1,0:T(1,128)} %table.1), calls=%async_computation.1 | async-start | bytes 524288 | tf_op jit(solution)/shard_map/all_to_all | solution.py:47
  54.4 2.2 %collective-permute-start.9 = (f32[8,768]{1,0:T(8,128)S(1)}, f32[8,768]{1,0:T(8,128)S(1)}, u32[]{:S(2)}, u32[]{:S(2)}) collective-permute-start(f32[8,768]{1,0:T(8,128)S(1)} %add.21), channel_id=1, source_target_pairs={{0,16},{1,17},{2,18},{3,19},{4,20},{5,21},{6,22},{7,23},{8,24},{9,... | collective-permute-start | bytes 73736 | tf_op jit(solution)/shard_map/ppermute | solution.py:35
  56.6 2.4 %collective-permute-start.11 = (f32[8,768]{1,0:T(8,128)S(1)}, f32[8,768]{1,0:T(8,128)S(1)}, u32[]{:S(2)}, u32[]{:S(2)}) collective-permute-start(f32[8,768]{1,0:T(8,128)S(1)} %add.21), channel_id=1, source_target_pairs={{0,56},{1,57},{2,58},{3,59},{4,60},{5,61},{6,62},{7,63},{8,48},{9,... | collective-permute-start | bytes 73736 | tf_op jit(solution)/shard_map/ppermute | solution.py:35
  60.6 4.7 %collective-permute-done.10 = f32[8,768]{1,0:T(8,128)S(1)} collective-permute-done((f32[8,768]{1,0:T(8,128)S(1)}, f32[8,768]{1,0:T(8,128)S(1)}, u32[]{:S(2)}, u32[]{:S(2)}) %collective-permute-start.10) | collective-permute-done | bytes 24608 | tf_op jit(solution)/shard_map/ppermute | solution.py:35
  66.4 2.5 %collective-permute-start.12 = (f32[38,1,2048]{2,1,0:T(1,128)S(1)}, f32[38,1,2048]{2,1,0:T(1,128)S(1)}, u32[]{:S(2)}, u32[]{:S(2)}) collective-permute-start(f32[38,1,2048]{2,1,0:T(1,128)S(1)} %pack.1.refs_0_), channel_id=1, source_target_pairs={{0,2},{1,3},{2,0},{3,1},{4,6},{5,7},{6,4},{7,5},{8,10},{9,11},{10,... | collective-permute-start | bytes 933896 | tf_op jit(solution)/shard_map/ppermute | solution.py:35
  68.8 8.0 %collective-permute-done.14.refs_3_ = f32[38,1,2048]{2,1,0:T(1,128)S(1)} collective-permute-done((f32[38,1,2048]{2,1,0:T(1,128)S(1)}, f32[38,1,2048]{2,1,0:T(1,128)S(1)}, u32[]{:S(2)}, u32[]{:S(2)}) %collective-permute-start.14) | collective-permute-done | bytes 311328 | tf_op jit(solution)/shard_map/ppermute | solution.py:35
  77.4 6.8 %collective-permute-start.15 = (f32[128,2048]{1,0:T(8,128)S(1)}, f32[128,2048]{1,0:T(8,128)S(1)}, u32[]{:S(2)}, u32[]{:S(2)}) collective-permute-start(f32[128,2048]{1,0:T(8,128)S(1)} %get-tuple-element.45.own_ref), channel_id=1, source_target_pairs={{0,1},{1,0},{2,3},{3,2},{4,5},{5,4},{6,7},{7,6},{8,9},{9,8},{10,11... | collective-permute-start | bytes 3145736 | tf_op jit(solution)/shard_map/ppermute | solution.py:35
  84.2 2.3 %collective-permute-done.15.other_ref = f32[128,2048]{1,0:T(8,128)S(1)} collective-permute-done((f32[128,2048]{1,0:T(8,128)S(1)}, f32[128,2048]{1,0:T(8,128)S(1)}, u32[]{:S(2)}, u32[]{:S(2)}) %collective-permute-start.15) | collective-permute-done | bytes 1048608 | tf_op jit(solution)/shard_map/ppermute | solution.py:35
  88.5 1.8 %collective-permute-start.18 = (f32[32,256]{1,0:T(8,128)S(1)}, f32[32,256]{1,0:T(8,128)S(1)}, u32[]{:S(2)}, u32[]{:S(2)}) collective-permute-start(f32[32,256]{1,0:T(8,128)S(1)} %slice.3), channel_id=1, source_target_pairs={{0,192},{1,193},{2,194},{3,195},{4,196},{5,197},{6,198},{7,199},{8... | collective-permute-start | bytes 98312 | tf_op jit(solution)/shard_map/ppermute | solution.py:35
  91.0 4.5 %stage.1 = (bf16[2048,2048]{1,0:T(8,128)(2,1)S(1)}, bf16[3,2048,256]{2,1,0:T(8,128)(2,1)S(1)}) custom-call(bf16[2048,2048]{1,0:T(8,128)(2,1)} %f_ref.2, bf16[3,2048,256]{2,1,0:T(8,128)(2,1)} %u_ref.4), custom_call_target="tpu_custom_call" | custom-call | bytes 16777216 | tf_op jit(solution)/shard_map/stage/pallas_call | solution.py:366
  98.9 3.2 %last.1 = bf16[64,2048]{1,0:T(8,128)(2,1)} custom-call(f32[32,768]{1,0:T(8,128)S(1)} %down.1.own_ref, f32[32,768]{1,0:T(8,128)S(1)} %collective-permute-done.19.other_ref, bf16[3,2048,256]{2,1,0:T(8,128)(2,1)S(1)} %get-tuple-element.53.u_ref, f32[64,2048]{1,0:T(8,128)S(1)} %copy-done.2, bf16[2048,2048]{1,0:T(8,128)(2,1)S(1)} %get-tuple-element.51.f_ref), custom_call_target="tpu_custom_call" | custom-call | flops 536870912 | bytes 8388608 | tf_op jit(solution)/shard_map/last/pallas_call | solution.py:341
  (45 shorter events, 14.7 us)
Async XLA Ops:
  3.7 5.2 %collective-permute-start = (f32[128,1536]{1,0:T(8,128)S(1)}, f32[128,1536]{1,0:T(8,128)S(1)}, u32[]{:S(2)}, u32[]{:S(2)}) collective-permute-start(f32[128,1536]{1,0:T(8,128)S(1)} %get-tuple-element.31), channel_id=1, source_target_pairs={{0,1},{1,0},{2,3},{3,2},{4,5},{5,4},{6,7},{7,6},{8,9},{9,8},{10,11... | collective-permute-start | bytes 2359304 | tf_op jit(solution)/shard_map/ppermute | solution.py:35
  9.1 77.4 %copy-start.1 = (bf16[3,256,256]{2,1,0:T(8,128)(2,1)S(1)}, bf16[3,256,256]{2,1,0:T(8,128)(2,1)}, u32[]{:S(2)}) copy-start(bf16[3,256,256]{2,1,0:T(8,128)(2,1)} %w_ref.3) | copy-start | bytes 1179652
  9.1 14.5 %collective-permute-start.1 = (f32[32,1536]{1,0:T(8,128)S(1)}, f32[32,1536]{1,0:T(8,128)S(1)}, u32[]{:S(2)}, u32[]{:S(2)}) collective-permute-start(f32[32,1536]{1,0:T(8,128)S(1)} %get-tuple-element.33), channel_id=1, source_target_pairs={{0,2},{1,3},{2,0},{3,1},{4,6},{5,7},{6,4},{7,5},{8,10},{9,11},{10,... | collective-permute-start | bytes 589832 | tf_op jit(solution)/shard_map/ppermute | solution.py:35
  9.2 14.4 %collective-permute-start.2 = (f32[32,1536]{1,0:T(8,128)S(1)}, f32[32,1536]{1,0:T(8,128)S(1)}, u32[]{:S(2)}, u32[]{:S(2)}) collective-permute-start(f32[32,1536]{1,0:T(8,128)S(1)} %get-tuple-element.34), channel_id=1, source_target_pairs={{0,4},{1,5},{2,6},{3,7},{4,0},{5,1},{6,2},{7,3},{8,12},{9,13},{10,... | collective-permute-start | bytes 589832 | tf_op jit(solution)/shard_map/ppermute | solution.py:35
  11.3 12.3 %collective-permute-start.3 = (f32[32,1536]{1,0:T(8,128)S(1)}, f32[32,1536]{1,0:T(8,128)S(1)}, u32[]{:S(2)}, u32[]{:S(2)}) collective-permute-start(f32[32,1536]{1,0:T(8,128)S(1)} %get-tuple-element.35), channel_id=1, source_target_pairs={{0,6},{1,7},{2,4},{3,5},{4,2},{5,3},{6,0},{7,1},{8,14},{9,15},{10,... | collective-permute-start | bytes 589832 | tf_op jit(solution)/shard_map/ppermute | solution.py:35
  20.2 2.5 %collective-permute-start.4 = (f32[32,768]{1,0:T(8,128)}, f32[32,768]{1,0:T(8,128)S(1)}, u32[]{:S(2)}, u32[]{:S(2)}) collective-permute-start(f32[32,768]{1,0:T(8,128)} %get-tuple-element.38), channel_id=1, source_target_pairs={{0,1},{1,0},{2,3},{3,2},{4,5},{5,4},{6,7},{7,6},{8,9},{9,8},{10,11... | collective-permute-start | bytes 294920 | tf_op jit(solution)/shard_map/ppermute | solution.py:35
  24.3 20.6 %all-to-all-start = ((f32[32,1,1536]{2,1,0:T(1,128)}), f32[32,1,1536]{2,1,0:T(1,128)S(1)}, u32[]{:S(2)}, u32[]{:S(2)}) async-start(f32[32,1,1536]{2,1,0:T(1,128)} %add_rows.1), calls=%async_computation | async-start | bytes 393216 | tf_op jit(solution)/shard_map/all_to_all | solution.py:47
  34.4 3.9 %collective-permute-start.5 = (f32[8,768]{1,0:T(8,128)S(1)}, f32[8,768]{1,0:T(8,128)S(1)}, u32[]{:S(2)}, u32[]{:S(2)}) collective-permute-start(f32[8,768]{1,0:T(8,128)S(1)} %get-tuple-element.41), channel_id=1, source_target_pairs={{0,2},{1,3},{2,0},{3,1},{4,6},{5,7},{6,4},{7,5},{8,10},{9,11},{10,... | collective-permute-start | bytes 73736 | tf_op jit(solution)/shard_map/ppermute | solution.py:35
  34.5 4.7 %collective-permute-start.6 = (f32[8,768]{1,0:T(8,128)S(1)}, f32[8,768]{1,0:T(8,128)S(1)}, u32[]{:S(2)}, u32[]{:S(2)}) collective-permute-start(f32[8,768]{1,0:T(8,128)S(1)} %get-tuple-element.42), channel_id=1, source_target_pairs={{0,4},{1,5},{2,6},{3,7},{4,0},{5,1},{6,2},{7,3},{8,12},{9,13},{10,... | collective-permute-start | bytes 73736 | tf_op jit(solution)/shard_map/ppermute | solution.py:35
  37.7 4.2 %collective-permute-start.7 = (f32[8,768]{1,0:T(8,128)S(1)}, f32[8,768]{1,0:T(8,128)S(1)}, u32[]{:S(2)}, u32[]{:S(2)}) collective-permute-start(f32[8,768]{1,0:T(8,128)S(1)} %get-tuple-element.43), channel_id=1, source_target_pairs={{0,6},{1,7},{2,4},{3,5},{4,2},{5,3},{6,0},{7,1},{8,14},{9,15},{10,... | collective-permute-start | bytes 73736 | tf_op jit(solution)/shard_map/ppermute | solution.py:35
  41.9 3.1 %collective-permute-start.8 = (f32[8,768]{1,0:T(8,128)S(1)}, f32[8,768]{1,0:T(8,128)S(1)}, u32[]{:S(2)}, u32[]{:S(2)}) collective-permute-start(f32[8,768]{1,0:T(8,128)S(1)} %add_add_fusion), channel_id=1, source_target_pairs={{0,8},{1,9},{2,10},{3,11},{4,12},{5,13},{6,14},{7,15},{8,0},{9,1},... | collective-permute-start | bytes 73736 | tf_op jit(solution)/shard_map/ppermute | solution.py:35
  45.8 19.5 %all-to-all-start.1 = ((f32[32,1,2048]{2,1,0:T(1,128)}), f32[32,1,2048]{2,1,0:T(1,128)S(1)}, u32[]{:S(2)}, u32[]{:S(2)}) async-start(f32[32,1,2048]{2,1,0:T(1,128)} %table.1), calls=%async_computation.1 | async-start | bytes 524288 | tf_op jit(solution)/shard_map/all_to_all | solution.py:47
  54.4 5.8 %collective-permute-start.9 = (f32[8,768]{1,0:T(8,128)S(1)}, f32[8,768]{1,0:T(8,128)S(1)}, u32[]{:S(2)}, u32[]{:S(2)}) collective-permute-start(f32[8,768]{1,0:T(8,128)S(1)} %add.21), channel_id=1, source_target_pairs={{0,16},{1,17},{2,18},{3,19},{4,20},{5,21},{6,22},{7,23},{8,24},{9,... | collective-permute-start | bytes 73736 | tf_op jit(solution)/shard_map/ppermute | solution.py:35
  56.6 3.9 %collective-permute-start.11 = (f32[8,768]{1,0:T(8,128)S(1)}, f32[8,768]{1,0:T(8,128)S(1)}, u32[]{:S(2)}, u32[]{:S(2)}) collective-permute-start(f32[8,768]{1,0:T(8,128)S(1)} %add.21), channel_id=1, source_target_pairs={{0,56},{1,57},{2,58},{3,59},{4,60},{5,61},{6,62},{7,63},{8,48},{9,... | collective-permute-start | bytes 73736 | tf_op jit(solution)/shard_map/ppermute | solution.py:35
  59.0 6.2 %collective-permute-start.10 = (f32[8,768]{1,0:T(8,128)S(1)}, f32[8,768]{1,0:T(8,128)S(1)}, u32[]{:S(2)}, u32[]{:S(2)}) collective-permute-start(f32[8,768]{1,0:T(8,128)S(1)} %add.21), channel_id=1, source_target_pairs={{0,40},{1,41},{2,42},{3,43},{4,44},{5,45},{6,46},{7,47},{8,32},{9,... | collective-permute-start | bytes 73736 | tf_op jit(solution)/shard_map/ppermute | solution.py:35
  65.3 11.5 %collective-permute-start.14 = (f32[38,1,2048]{2,1,0:T(1,128)S(1)}, f32[38,1,2048]{2,1,0:T(1,128)S(1)}, u32[]{:S(2)}, u32[]{:S(2)}) collective-permute-start(f32[38,1,2048]{2,1,0:T(1,128)S(1)} %pack.1.refs_0_), channel_id=1, source_target_pairs={{0,6},{1,7},{2,4},{3,5},{4,2},{5,3},{6,0},{7,1},{8,14},{9,15},{10,... | collective-permute-start | bytes 933896 | tf_op jit(solution)/shard_map/ppermute | solution.py:35
  66.4 10.4 %collective-permute-start.13 = (f32[38,1,2048]{2,1,0:T(1,128)S(1)}, f32[38,1,2048]{2,1,0:T(1,128)S(1)}, u32[]{:S(2)}, u32[]{:S(2)}) collective-permute-start(f32[38,1,2048]{2,1,0:T(1,128)S(1)} %pack.1.refs_0_), channel_id=1, source_target_pairs={{0,4},{1,5},{2,6},{3,7},{4,0},{5,1},{6,2},{7,3},{8,12},{9,13},{10,... | collective-permute-start | bytes 933896 | tf_op jit(solution)/shard_map/ppermute | solution.py:35
  66.4 10.8 %collective-permute-start.12 = (f32[38,1,2048]{2,1,0:T(1,128)S(1)}, f32[38,1,2048]{2,1,0:T(1,128)S(1)}, u32[]{:S(2)}, u32[]{:S(2)}) collective-permute-start(f32[38,1,2048]{2,1,0:T(1,128)S(1)} %pack.1.refs_0_), channel_id=1, source_target_pairs={{0,2},{1,3},{2,0},{3,1},{4,6},{5,7},{6,4},{7,5},{8,10},{9,11},{10,... | collective-permute-start | bytes 933896 | tf_op jit(solution)/shard_map/ppermute | solution.py:35
  77.4 9.1 %collective-permute-start.15 = (f32[128,2048]{1,0:T(8,128)S(1)}, f32[128,2048]{1,0:T(8,128)S(1)}, u32[]{:S(2)}, u32[]{:S(2)}) collective-permute-start(f32[128,2048]{1,0:T(8,128)S(1)} %get-tuple-element.45.own_ref), channel_id=1, source_target_pairs={{0,1},{1,0},{2,3},{3,2},{4,5},{5,4},{6,7},{7,6},{8,9},{9,8},{10,11... | collective-permute-start | bytes 3145736 | tf_op jit(solution)/shard_map/ppermute | solution.py:35
  86.5 12.4 %copy-start.2 = (f32[64,2048]{1,0:T(8,128)S(1)}, f32[64,2048]{1,0:T(8,128)}, u32[]{:S(2)}) copy-start(f32[64,2048]{1,0:T(8,128)} %get-tuple-element.54.z_ref) | copy-start | bytes 1572868
  87.3 8.2 %collective-permute-start.16 = (f32[32,512]{1,0:T(8,128)S(1)}, f32[32,512]{1,0:T(8,128)S(1)}, u32[]{:S(2)}, u32[]{:S(2)}) collective-permute-start(f32[32,512]{1,0:T(8,128)S(1)} %get-tuple-element.47.vs_ref), channel_id=1, source_target_pairs={{0,64},{1,65},{2,66},{3,67},{4,68},{5,69},{6,70},{7,71},{8,72},{9,... | collective-permute-start | bytes 196616 | tf_op jit(solution)/shard_map/ppermute | solution.py:35
  88.5 6.9 %collective-permute-start.18 = (f32[32,256]{1,0:T(8,128)S(1)}, f32[32,256]{1,0:T(8,128)S(1)}, u32[]{:S(2)}, u32[]{:S(2)}) collective-permute-start(f32[32,256]{1,0:T(8,128)S(1)} %slice.3), channel_id=1, source_target_pairs={{0,192},{1,193},{2,194},{3,195},{4,196},{5,197},{6,198},{7,199},{8... | collective-permute-start | bytes 98312 | tf_op jit(solution)/shard_map/ppermute | solution.py:35
  90.3 5.1 %collective-permute-start.17 = (f32[32,256]{1,0:T(8,128)S(1)}, f32[32,256]{1,0:T(8,128)S(1)}, u32[]{:S(2)}, u32[]{:S(2)}) collective-permute-start(f32[32,256]{1,0:T(8,128)S(1)} %slice.3), channel_id=1, source_target_pairs={{0,128},{1,129},{2,130},{3,131},{4,132},{5,133},{6,134},{7,135},{8... | collective-permute-start | bytes 98312 | tf_op jit(solution)/shard_map/ppermute | solution.py:35
  96.7 2.2 %collective-permute-start.19 = (f32[32,768]{1,0:T(8,128)S(1)}, f32[32,768]{1,0:T(8,128)S(1)}, u32[]{:S(2)}, u32[]{:S(2)}) collective-permute-start(f32[32,768]{1,0:T(8,128)S(1)} %down.1.own_ref), channel_id=1, source_target_pairs={{0,1},{1,0},{2,3},{3,2},{4,5},{5,4},{6,7},{7,6},{8,9},{9,8},{10,11... | collective-permute-start | bytes 294920 | tf_op jit(solution)/shard_map/ppermute | solution.py:35
  (2 other events, 2.8 us)

commit v5 on v4

--- a/solution.py
+++ b/solution.py
@@ -107,8 +107,9 @@
     out_ref[:rows] = sums_ref[...]
     for k in range(6):
         value = (p_ref if k < 3 else po_ref)[:, k % 3 * rank : (k % 3 + 1) * rank]
-        for r in range(value.shape[0]):
-            out_ref[rows + k, :, r * rank : (r + 1) * rank] = value[r : r + 1]
+        for r in range(8):
+            row, place = divmod(8 * k + r, 7)
+            out_ref[rows + row, :, place * rank : (place + 1) * rank] = value[r : r + 1]
 
 
 def pack(sums, p, po):
@@ -117,7 +118,7 @@
         pack_kernel,
         in_specs=whole(3),
         out_specs=whole(1)[0],
-        out_shape=jax.ShapeDtypeStruct((rows + 6, 1, width), F32),
+        out_shape=jax.ShapeDtypeStruct((rows + 7, 1, width), F32),
         compiler_params=params(16),
         cost_estimate=cost(0, 8 * rows * width),
         name="pack",
@@ -134,13 +135,13 @@
         own_ref[at, :] = part[:rows].reshape(rows, own_ref.shape[1])
         at = pl.ds(pl.multiple_of((y ^ m) * cols, cols), cols)
         for k in range(6):
-            row = part[rows + k]
-            value = jnp.concatenate([row[:, r * rank : (r + 1) * rank] for r in range(cols)], axis=0)
+            places = [divmod(8 * k + r, 7) for r in range(8)]
+            value = jnp.concatenate([part[rows + i, :, j * rank : (j + 1) * rank] for i, j in places], axis=0)
             half_ref[at, k * rank : (k + 1) * rank] = value
 
 
 def unpack(parts, cols, rank):
-    rows, width = parts[0].shape[0] - 6, parts[0].shape[2]
+    rows, width = parts[0].shape[0] - 7, parts[0].shape[2]
     return pl.pallas_call(
         unpack_kernel,
         in_specs=whole(4),
@@ -170,14 +171,22 @@
 
 
 def table_kernel(rows_ref, out_ref):
-    rank = rows_ref.shape[2] // 6
+    unit = rows_ref.shape[2] // 11
+    low = core_index() == 0
     sub = [rows_ref[4 * c : 4 * c + 4].sum(axis=0) for c in range(8)]
     node = [sub[2 * c] + sub[2 * c + 1] for c in range(4)]
     child = [node[0] + node[1], node[2] + node[3]]
     for c in range(8):
         own, other, beside, across = sub[c], sub[c ^ 1], node[(c >> 1) ^ 1], child[(c >> 2) ^ 1]
         row = jnp.concatenate(
-            [own[:, : 2 * rank], other[:, : 3 * rank], beside[:, 3 * rank : 5 * rank], across[:, 5 * rank :]], axis=1
+            [
+                own[:, : 4 * unit],
+                other[:, : 5 * unit],
+                jnp.where(low, other[:, 5 * unit : 6 * unit], beside[:, 5 * unit : 6 * unit]),
+                beside[:, 6 * unit : 9 * unit],
+                across[:, 9 * unit :],
+            ],
+            axis=1,
         )
         out_ref[4 * c : 4 * c + 4] = jnp.broadcast_to(row[None], (4, 1, row.shape[1]))
 
@@ -187,7 +196,7 @@
         table_kernel,
         in_specs=whole(1),
         out_specs=whole(1)[0],
-        out_shape=jax.ShapeDtypeStruct((32, 1, rows.shape[2] // 6 * 8), F32),
+        out_shape=jax.ShapeDtypeStruct((32, 1, rows.shape[2] // 11 * 15), F32),
         compiler_params=params(16),
         cost_estimate=cost(rows.size, 8 * rows.size),
         name="table",
@@ -201,13 +210,18 @@
     rank = u_ref.shape[2]
     for place, (a, b) in enumerate(PAIRS):
         g_buf[:, place * rank : (place + 1) * rank] = dot(u_ref[a], u_ref[b], TN)
-    split_halves(g_buf[...], keep_ref, send_ref)
+    half = rank // 2
+    low = jnp.concatenate([g_buf[:half, : 3 * rank + half], g_buf[:half, 4 * rank :]], axis=1)
+    high = jnp.concatenate([g_buf[half:, : 2 * rank], g_buf[half:, 2 * rank + half :]], axis=1)
+    first_core = core_index() == 0
+    keep_ref[...] = jnp.where(first_core, low, high)
+    send_ref[...] = jnp.where(first_core, high, low)
 
 
 def gram(bases):
     leaf, rank = bases.shape[1:]
     width = len(PAIRS) * rank
-    shape = jax.ShapeDtypeStruct((rank // 2, width), F32)
+    shape = jax.ShapeDtypeStruct((rank // 2, width - rank // 2), F32)
     return pl.pallas_call(
         gram_kernel,
         in_specs=whole(1),
@@ -259,14 +273,27 @@
     )(rhs, inverse, bases)
 
 
-def block(own_ref, other_ref, place):
-    rank = own_ref.shape[1] // 8
-    at = slice(place * rank, (place + 1) * rank)
-    return both(own_ref[:, at], other_ref[:, at])
+def blocks(own_ref, other_ref):
+    own, other = own_ref[...], other_ref[...]
+    first_core = core_index() == 0
+    low, high = jnp.where(first_core, own, other), jnp.where(first_core, other, own)
+    unit = low.shape[1] // 15
+
+    def at(half, k, count=1):
+        return half[:, k * unit : (k + count) * unit]
+
+    def square(left_top, right_top, left_bottom, right_bottom):
+        top = jnp.concatenate([left_top, right_top], axis=1)
+        return jnp.concatenate([top, jnp.concatenate([left_bottom, right_bottom], axis=1)], axis=0)
+
+    m00 = square(at(low, 8), at(low, 9), at(low, 9).T, at(high, 8))
+    m11 = square(at(low, 10), at(high, 9).T, at(high, 9), at(high, 10))
+    plain = [jnp.concatenate([at(low, k, 2), at(high, k, 2)], axis=0) for k in (0, 2, 4, 6, 11, 13)]
+    return plain[:4] + [m00, m11] + plain[4:]
 
 
 def up_kernel(own_ref, other_ref, w_ref, both_ref, vs_ref, q_ref):
-    m10, m20, m10o, m20o, m00o, _, m12o = (block(own_ref, other_ref, k) for k in range(7))
+    m10, m20, m10o, m20o, m00o, _, m12o, _ = blocks(own_ref, other_ref)
     rank = m10.shape[0]
     p_ref, po_ref = both_ref[:, : 3 * rank], both_ref[:, 3 * rank :]
     q0 = exact(po_ref[:, :rank], w_ref[0], NT)
@@ -294,7 +321,7 @@
 
 
 def down_kernel(own_ref, other_ref, w_ref, vs_ref, b_ref, r2_ref, r3_ref, q_ref, out_ref):
-    m10o, m20o, _, m11o, m12o, m22o = (block(own_ref, other_ref, k) for k in range(2, 8))
+    m10o, m20o, _, m11o, m12o, m22o = blocks(own_ref, other_ref)[2:]
     rank = m10o.shape[0]
     s0o, q0, q1o = (q_ref[:, k * rank : (k + 1) * rank] for k in range(3))
     c2 = vs_ref[:, :rank] + b_ref[:, :rank]
@@ -392,7 +419,7 @@
     pair = part + swap(part, 8)
     back = over_xz(after(summed, pair))
     p = pair + swap(pair, 16)
-    po = swap(pair, 40) + swap(pair, 56)
+    po = swap(p, 56)
 
     mine = pack(back, p, po)
     own, half = unpack([mine] + [swap(mine, 2 * m) for m in (1, 2, 3)], p.shape[0], rank)

time: 103 us -> 101 us (0.981)
  starting transfers between devices: 53.4 us -> 50.8 us
  waiting for transfers between devices: 25.1 us -> 26.8 us
    ppermute x20 -> x19, starting transfers between devices: 34.8 us -> 32.7 us  [swap(): return lax.ppermute(value, AXIS, [(i, i ^ mask) for i in range(N)])]
    ppermute x20 -> x19, waiting for transfers between devices: 25.1 us -> 26.8 us  [swap(): return lax.ppermute(value, AXIS, [(i, i ^ mask) for i in range(N)])]
  transfers between devices with their start and end apart: 22 -> 21, of which waited for: 12 -> 11; matrix products, arithmetic and copies ran while one was open for 0% -> 0% of each run, Pallas kernels for 11% -> 12%
where the time goes in v5:
time: 101 us
  starting transfers between devices  50.8 us (50%)
  waiting for transfers between devices  26.8 us (27%)
  Pallas kernels  20.6 us (20%)
  local copies, waits for them, and re-layouts  2.79 us (3%)
    ppermute x19, starting transfers between devices, swap(): return lax.ppermute(value, AXIS, [(i, i ^ mask) for i in range(N)])  32.7 us
    ppermute x19, waiting for transfers between devices, swap(): return lax.ppermute(value, AXIS, [(i, i ^ mask) for i in range(N)])  26.8 us
    all_to_all x2, starting transfers between devices, over_xz(): lax.all_to_all(value, AXIS, 0, 0, axis_index_groups=line(32, 8), tiled=True)  18.1 us
    pallas_call x1, Pallas kernels, first(): pl.pallas_call(first_kernel, in_specs=whole(1) + whole(2, pltpu.HBM), out...  7.18 us
    pallas_call x1, Pallas kernels, stage(): pl.pallas_call(stage_kernel, in_specs=whole(2, pltpu.HBM), out_specs=whol...  4.46 us
    pallas_call x1, Pallas kernels, last(): pl.pallas_call(last_kernel, in_specs=whole(5), out_specs=whole(1)[0], out...  3.24 us
    unnamed x8, local copies, waits for them, and re-layouts  2.79 us
  transfers between devices with their start and end apart: 21, of which 11 were waited for; matrix products, arithmetic and copies ran while one was open for 0% of the time, Pallas kernels for 12%

profile of v5, /device:TPU:1, one launch (start us, length us, event | category | flops | bytes accessed | tf_op | source)
XLA Modules:
  0.0 101.1 jit_solution(4903870852922139982)
XLA Ops:
  0.0 1.9 %copy-done = bf16[3,2048,256]{2,1,0:T(8,128)(2,1)S(1)} copy-done((bf16[3,2048,256]{2,1,0:T(8,128)(2,1)S(1)}, bf16[3,2048,256]{2,1,0:T(8,128)(2,1)}, u32[]{:S(2)}) %copy-start) | copy-done | bytes 3145752
  1.9 1.8 %gram.1 = (f32[128,1408]{1,0:T(8,128)S(1)}, f32[128,1408]{1,0:T(8,128)S(1)}) custom-call(bf16[3,2048,256]{2,1,0:T(8,128)(2,1)S(1)} %copy-done), custom_call_target="tpu_custom_call" | custom-call | flops 1610612736 | bytes 3145728 | tf_op jit(solution)/shard_map/gram/pallas_call | solution.py:225
  3.7 3.3 %collective-permute-start = (f32[128,1408]{1,0:T(8,128)S(1)}, f32[128,1408]{1,0:T(8,128)S(1)}, u32[]{:S(2)}, u32[]{:S(2)}) collective-permute-start(f32[128,1408]{1,0:T(8,128)S(1)} %get-tuple-element.31), channel_id=1, source_target_pairs={{0,1},{1,0},{2,3},{3,2},{4,5},{5,4},{6,7},{7,6},{8,9},{9,8},{10,11... | collective-permute-start | bytes 2162696 | tf_op jit(solution)/shard_map/ppermute | solution.py:35
  7.1 1.8 %collective-permute-done.other_ref = f32[128,1408]{1,0:T(8,128)S(1)} collective-permute-done((f32[128,1408]{1,0:T(8,128)S(1)}, f32[128,1408]{1,0:T(8,128)S(1)}, u32[]{:S(2)}, u32[]{:S(2)}) %collective-permute-start) | collective-permute-done | bytes 720928 | tf_op jit(solution)/shard_map/ppermute | solution.py:35
  9.1 2.2 %collective-permute-start.2 = (f32[32,1408]{1,0:T(8,128)S(1)}, f32[32,1408]{1,0:T(8,128)S(1)}, u32[]{:S(2)}, u32[]{:S(2)}) collective-permute-start(f32[32,1408]{1,0:T(8,128)S(1)} %get-tuple-element.34), channel_id=1, source_target_pairs={{0,4},{1,5},{2,6},{3,7},{4,0},{5,1},{6,2},{7,3},{8,12},{9,13},{10,... | collective-permute-start | bytes 540680 | tf_op jit(solution)/shard_map/ppermute | solution.py:35
  11.2 1.7 %collective-permute-start.3 = (f32[32,1408]{1,0:T(8,128)S(1)}, f32[32,1408]{1,0:T(8,128)S(1)}, u32[]{:S(2)}, u32[]{:S(2)}) collective-permute-start(f32[32,1408]{1,0:T(8,128)S(1)} %get-tuple-element.35), channel_id=1, source_target_pairs={{0,6},{1,7},{2,4},{3,5},{4,2},{5,3},{6,0},{7,1},{8,14},{9,15},{10,... | collective-permute-start | bytes 540680 | tf_op jit(solution)/shard_map/ppermute | solution.py:35
  12.9 7.2 %first.1 = (f32[64,2048]{1,0:T(8,128)}, f32[32,768]{1,0:T(8,128)}, f32[32,768]{1,0:T(8,128)}) custom-call(bf16[64,2048]{1,0:T(8,128)(2,1)} %bitcast.2, bf16[2048,2048]{1,0:T(8,128)(2,1)} %f_ref.2, bf16[3,2048,256]{2,1,0:T(8,128)(2,1)} %u_ref.4), custom_call_target="tpu_custom_call" | custom-call | flops 536870912 | bytes 8388608 | tf_op jit(solution)/shard_map/first/pallas_call | solution.py:260
  24.2 9.5 %all-to-all-start = ((f32[32,1,1408]{2,1,0:T(1,128)}), f32[32,1,1408]{2,1,0:T(1,128)S(1)}, u32[]{:S(2)}, u32[]{:S(2)}) async-start(f32[32,1,1408]{2,1,0:T(1,128)} %add_rows.1), calls=%async_computation | async-start | bytes 360448 | tf_op jit(solution)/shard_map/all_to_all | solution.py:47
  33.8 3.7 %collective-permute-start.6 = (f32[8,768]{1,0:T(8,128)S(1)}, f32[8,768]{1,0:T(8,128)S(1)}, u32[]{:S(2)}, u32[]{:S(2)}) collective-permute-start(f32[8,768]{1,0:T(8,128)S(1)} %get-tuple-element.42), channel_id=1, source_target_pairs={{0,4},{1,5},{2,6},{3,7},{4,0},{5,1},{6,2},{7,3},{8,12},{9,13},{10,... | collective-permute-start | bytes 73736 | tf_op jit(solution)/shard_map/ppermute | solution.py:35
  37.7 1.4 %collective-permute-done.6 = f32[8,768]{1,0:T(8,128)S(1)} collective-permute-done((f32[8,768]{1,0:T(8,128)S(1)}, f32[8,768]{1,0:T(8,128)S(1)}, u32[]{:S(2)}, u32[]{:S(2)}) %collective-permute-start.6) | collective-permute-done | bytes 24608 | tf_op jit(solution)/shard_map/ppermute | solution.py:35
  39.0 2.7 %collective-permute-done.7 = f32[8,768]{1,0:T(8,128)S(1)} collective-permute-done((f32[8,768]{1,0:T(8,128)S(1)}, f32[8,768]{1,0:T(8,128)S(1)}, u32[]{:S(2)}, u32[]{:S(2)}) %collective-permute-start.7) | collective-permute-done | bytes 24608 | tf_op jit(solution)/shard_map/ppermute | solution.py:35
  43.1 1.7 %collective-permute-done.8 = f32[8,768]{1,0:T(8,128)S(1)} collective-permute-done((f32[8,768]{1,0:T(8,128)S(1)}, f32[8,768]{1,0:T(8,128)S(1)}, u32[]{:S(2)}, u32[]{:S(2)}) %collective-permute-start.8) | collective-permute-done | bytes 24608 | tf_op jit(solution)/shard_map/ppermute | solution.py:35
  45.6 8.6 %all-to-all-start.1 = ((f32[32,1,1920]{2,1,0:T(1,128)}), f32[32,1,1920]{2,1,0:T(1,128)S(1)}, u32[]{:S(2)}, u32[]{:S(2)}) async-start(f32[32,1,1920]{2,1,0:T(1,128)} %table.1), calls=%async_computation.1 | async-start | bytes 491520 | tf_op jit(solution)/shard_map/all_to_all | solution.py:47
  54.3 2.2 %collective-permute-start.9 = (f32[8,768]{1,0:T(8,128)S(1)}, f32[8,768]{1,0:T(8,128)S(1)}, u32[]{:S(2)}, u32[]{:S(2)}) collective-permute-start(f32[8,768]{1,0:T(8,128)S(1)} %add.18), channel_id=1, source_target_pairs={{0,16},{1,17},{2,18},{3,19},{4,20},{5,21},{6,22},{7,23},{8,24},{9,... | collective-permute-start | bytes 73736 | tf_op jit(solution)/shard_map/ppermute | solution.py:35
  56.5 3.5 %collective-permute-done.9 = f32[8,768]{1,0:T(8,128)S(1)} collective-permute-done((f32[8,768]{1,0:T(8,128)S(1)}, f32[8,768]{1,0:T(8,128)S(1)}, u32[]{:S(2)}, u32[]{:S(2)}) %collective-permute-start.9) | collective-permute-done | bytes 24608 | tf_op jit(solution)/shard_map/ppermute | solution.py:35
  59.9 1.6 %collective-permute-start.10 = (f32[8,768]{1,0:T(8,128)S(1)}, f32[8,768]{1,0:T(8,128)S(1)}, u32[]{:S(2)}, u32[]{:S(2)}) collective-permute-start(f32[8,768]{1,0:T(8,128)S(1)} %add.19.p_ref), channel_id=1, source_target_pairs={{0,56},{1,57},{2,58},{3,59},{4,60},{5,61},{6,62},{7,63},{8,48},{9,... | collective-permute-start | bytes 73736 | tf_op jit(solution)/shard_map/ppermute | solution.py:35
  61.5 3.5 %collective-permute-done.10.po_ref = f32[8,768]{1,0:T(8,128)S(1)} collective-permute-done((f32[8,768]{1,0:T(8,128)S(1)}, f32[8,768]{1,0:T(8,128)S(1)}, u32[]{:S(2)}, u32[]{:S(2)}) %collective-permute-start.10) | collective-permute-done | bytes 24608 | tf_op jit(solution)/shard_map/ppermute | solution.py:35
  66.2 2.2 %collective-permute-start.11 = (f32[39,1,1920]{2,1,0:T(1,128)S(1)}, f32[39,1,1920]{2,1,0:T(1,128)S(1)}, u32[]{:S(2)}, u32[]{:S(2)}) collective-permute-start(f32[39,1,1920]{2,1,0:T(1,128)S(1)} %pack.1.refs_0_), channel_id=1, source_target_pairs={{0,2},{1,3},{2,0},{3,1},{4,6},{5,7},{6,4},{7,5},{8,10},{9,11},{10,... | collective-permute-start | bytes 898568 | tf_op jit(solution)/shard_map/ppermute | solution.py:35
  68.4 7.5 %collective-permute-done.13.refs_3_ = f32[39,1,1920]{2,1,0:T(1,128)S(1)} collective-permute-done((f32[39,1,1920]{2,1,0:T(1,128)S(1)}, f32[39,1,1920]{2,1,0:T(1,128)S(1)}, u32[]{:S(2)}, u32[]{:S(2)}) %collective-permute-start.13) | collective-permute-done | bytes 299552 | tf_op jit(solution)/shard_map/ppermute | solution.py:35
  76.5 6.8 %collective-permute-start.14 = (f32[128,1920]{1,0:T(8,128)S(1)}, f32[128,1920]{1,0:T(8,128)S(1)}, u32[]{:S(2)}, u32[]{:S(2)}) collective-permute-start(f32[128,1920]{1,0:T(8,128)S(1)} %get-tuple-element.45.own_ref), channel_id=1, source_target_pairs={{0,1},{1,0},{2,3},{3,2},{4,5},{5,4},{6,7},{7,6},{8,9},{9,8},{10,11... | collective-permute-start | bytes 2949128 | tf_op jit(solution)/shard_map/ppermute | solution.py:35
  83.3 2.2 %collective-permute-done.14.other_ref = f32[128,1920]{1,0:T(8,128)S(1)} collective-permute-done((f32[128,1920]{1,0:T(8,128)S(1)}, f32[128,1920]{1,0:T(8,128)S(1)}, u32[]{:S(2)}, u32[]{:S(2)}) %collective-permute-start.14) | collective-permute-done | bytes 983072 | tf_op jit(solution)/shard_map/ppermute | solution.py:35
  87.5 1.8 %collective-permute-start.17 = (f32[32,256]{1,0:T(8,128)S(1)}, f32[32,256]{1,0:T(8,128)S(1)}, u32[]{:S(2)}, u32[]{:S(2)}) collective-permute-start(f32[32,256]{1,0:T(8,128)S(1)} %slice.3), channel_id=1, source_target_pairs={{0,192},{1,193},{2,194},{3,195},{4,196},{5,197},{6,198},{7,199},{8... | collective-permute-start | bytes 98312 | tf_op jit(solution)/shard_map/ppermute | solution.py:35
  90.0 4.5 %stage.1 = (bf16[2048,2048]{1,0:T(8,128)(2,1)S(1)}, bf16[3,2048,256]{2,1,0:T(8,128)(2,1)S(1)}) custom-call(bf16[2048,2048]{1,0:T(8,128)(2,1)} %f_ref.2, bf16[3,2048,256]{2,1,0:T(8,128)(2,1)} %u_ref.4), custom_call_target="tpu_custom_call" | custom-call | bytes 16777216 | tf_op jit(solution)/shard_map/stage/pallas_call | solution.py:393
  97.9 3.2 %last.1 = bf16[64,2048]{1,0:T(8,128)(2,1)} custom-call(f32[32,768]{1,0:T(8,128)S(1)} %down.1.own_ref, f32[32,768]{1,0:T(8,128)S(1)} %collective-permute-done.18.other_ref, bf16[3,2048,256]{2,1,0:T(8,128)(2,1)S(1)} %get-tuple-element.53.u_ref, f32[64,2048]{1,0:T(8,128)S(1)} %copy-done.2, bf16[2048,2048]{1,0:T(8,128)(2,1)S(1)} %get-tuple-element.51.f_ref), custom_call_target="tpu_custom_call" | custom-call | flops 536870912 | bytes 8388608 | tf_op jit(solution)/shard_map/last/pallas_call | solution.py:368
  (42 shorter events, 14.5 us)
Async XLA Ops:
  0.0 1.9 %copy-start = (bf16[3,2048,256]{2,1,0:T(8,128)(2,1)S(1)}, bf16[3,2048,256]{2,1,0:T(8,128)(2,1)}, u32[]{:S(2)}) copy-start(bf16[3,2048,256]{2,1,0:T(8,128)(2,1)} %u_ref.4) | copy-start | bytes 9437188
  3.7 5.1 %collective-permute-start = (f32[128,1408]{1,0:T(8,128)S(1)}, f32[128,1408]{1,0:T(8,128)S(1)}, u32[]{:S(2)}, u32[]{:S(2)}) collective-permute-start(f32[128,1408]{1,0:T(8,128)S(1)} %get-tuple-element.31), channel_id=1, source_target_pairs={{0,1},{1,0},{2,3},{3,2},{4,5},{5,4},{6,7},{7,6},{8,9},{9,8},{10,11... | collective-permute-start | bytes 2162696 | tf_op jit(solution)/shard_map/ppermute | solution.py:35
  9.0 76.5 %copy-start.1 = (bf16[3,256,256]{2,1,0:T(8,128)(2,1)S(1)}, bf16[3,256,256]{2,1,0:T(8,128)(2,1)}, u32[]{:S(2)}) copy-start(bf16[3,256,256]{2,1,0:T(8,128)(2,1)} %w_ref.3) | copy-start | bytes 1179652
  9.0 14.5 %collective-permute-start.1 = (f32[32,1408]{1,0:T(8,128)S(1)}, f32[32,1408]{1,0:T(8,128)S(1)}, u32[]{:S(2)}, u32[]{:S(2)}) collective-permute-start(f32[32,1408]{1,0:T(8,128)S(1)} %get-tuple-element.33), channel_id=1, source_target_pairs={{0,2},{1,3},{2,0},{3,1},{4,6},{5,7},{6,4},{7,5},{8,10},{9,11},{10,... | collective-permute-start | bytes 540680 | tf_op jit(solution)/shard_map/ppermute | solution.py:35
  9.1 14.4 %collective-permute-start.2 = (f32[32,1408]{1,0:T(8,128)S(1)}, f32[32,1408]{1,0:T(8,128)S(1)}, u32[]{:S(2)}, u32[]{:S(2)}) collective-permute-start(f32[32,1408]{1,0:T(8,128)S(1)} %get-tuple-element.34), channel_id=1, source_target_pairs={{0,4},{1,5},{2,6},{3,7},{4,0},{5,1},{6,2},{7,3},{8,12},{9,13},{10,... | collective-permute-start | bytes 540680 | tf_op jit(solution)/shard_map/ppermute | solution.py:35
  11.2 12.2 %collective-permute-start.3 = (f32[32,1408]{1,0:T(8,128)S(1)}, f32[32,1408]{1,0:T(8,128)S(1)}, u32[]{:S(2)}, u32[]{:S(2)}) collective-permute-start(f32[32,1408]{1,0:T(8,128)S(1)} %get-tuple-element.35), channel_id=1, source_target_pairs={{0,6},{1,7},{2,4},{3,5},{4,2},{5,3},{6,0},{7,1},{8,14},{9,15},{10,... | collective-permute-start | bytes 540680 | tf_op jit(solution)/shard_map/ppermute | solution.py:35
  20.1 2.5 %collective-permute-start.4 = (f32[32,768]{1,0:T(8,128)}, f32[32,768]{1,0:T(8,128)S(1)}, u32[]{:S(2)}, u32[]{:S(2)}) collective-permute-start(f32[32,768]{1,0:T(8,128)} %get-tuple-element.38), channel_id=1, source_target_pairs={{0,1},{1,0},{2,3},{3,2},{4,5},{5,4},{6,7},{7,6},{8,9},{9,8},{10,11... | collective-permute-start | bytes 294920 | tf_op jit(solution)/shard_map/ppermute | solution.py:35
  24.2 20.6 %all-to-all-start = ((f32[32,1,1408]{2,1,0:T(1,128)}), f32[32,1,1408]{2,1,0:T(1,128)S(1)}, u32[]{:S(2)}, u32[]{:S(2)}) async-start(f32[32,1,1408]{2,1,0:T(1,128)} %add_rows.1), calls=%async_computation | async-start | bytes 360448 | tf_op jit(solution)/shard_map/all_to_all | solution.py:47
  33.7 3.9 %collective-permute-start.5 = (f32[8,768]{1,0:T(8,128)S(1)}, f32[8,768]{1,0:T(8,128)S(1)}, u32[]{:S(2)}, u32[]{:S(2)}) collective-permute-start(f32[8,768]{1,0:T(8,128)S(1)} %get-tuple-element.41), channel_id=1, source_target_pairs={{0,2},{1,3},{2,0},{3,1},{4,6},{5,7},{6,4},{7,5},{8,10},{9,11},{10,... | collective-permute-start | bytes 73736 | tf_op jit(solution)/shard_map/ppermute | solution.py:35
  33.8 5.2 %collective-permute-start.6 = (f32[8,768]{1,0:T(8,128)S(1)}, f32[8,768]{1,0:T(8,128)S(1)}, u32[]{:S(2)}, u32[]{:S(2)}) collective-permute-start(f32[8,768]{1,0:T(8,128)S(1)} %get-tuple-element.42), channel_id=1, source_target_pairs={{0,4},{1,5},{2,6},{3,7},{4,0},{5,1},{6,2},{7,3},{8,12},{9,13},{10,... | collective-permute-start | bytes 73736 | tf_op jit(solution)/shard_map/ppermute | solution.py:35
  37.5 4.2 %collective-permute-start.7 = (f32[8,768]{1,0:T(8,128)S(1)}, f32[8,768]{1,0:T(8,128)S(1)}, u32[]{:S(2)}, u32[]{:S(2)}) collective-permute-start(f32[8,768]{1,0:T(8,128)S(1)} %get-tuple-element.43), channel_id=1, source_target_pairs={{0,6},{1,7},{2,4},{3,5},{4,2},{5,3},{6,0},{7,1},{8,14},{9,15},{10,... | collective-permute-start | bytes 73736 | tf_op jit(solution)/shard_map/ppermute | solution.py:35
  41.7 3.1 %collective-permute-start.8 = (f32[8,768]{1,0:T(8,128)S(1)}, f32[8,768]{1,0:T(8,128)S(1)}, u32[]{:S(2)}, u32[]{:S(2)}) collective-permute-start(f32[8,768]{1,0:T(8,128)S(1)} %add_add_fusion), channel_id=1, source_target_pairs={{0,8},{1,9},{2,10},{3,11},{4,12},{5,13},{6,14},{7,15},{8,0},{9,1},... | collective-permute-start | bytes 73736 | tf_op jit(solution)/shard_map/ppermute | solution.py:35
  45.6 19.4 %all-to-all-start.1 = ((f32[32,1,1920]{2,1,0:T(1,128)}), f32[32,1,1920]{2,1,0:T(1,128)S(1)}, u32[]{:S(2)}, u32[]{:S(2)}) async-start(f32[32,1,1920]{2,1,0:T(1,128)} %table.1), calls=%async_computation.1 | async-start | bytes 491520 | tf_op jit(solution)/shard_map/all_to_all | solution.py:47
  54.3 5.7 %collective-permute-start.9 = (f32[8,768]{1,0:T(8,128)S(1)}, f32[8,768]{1,0:T(8,128)S(1)}, u32[]{:S(2)}, u32[]{:S(2)}) collective-permute-start(f32[8,768]{1,0:T(8,128)S(1)} %add.18), channel_id=1, source_target_pairs={{0,16},{1,17},{2,18},{3,19},{4,20},{5,21},{6,22},{7,23},{8,24},{9,... | collective-permute-start | bytes 73736 | tf_op jit(solution)/shard_map/ppermute | solution.py:35
  59.9 5.1 %collective-permute-start.10 = (f32[8,768]{1,0:T(8,128)S(1)}, f32[8,768]{1,0:T(8,128)S(1)}, u32[]{:S(2)}, u32[]{:S(2)}) collective-permute-start(f32[8,768]{1,0:T(8,128)S(1)} %add.19.p_ref), channel_id=1, source_target_pairs={{0,56},{1,57},{2,58},{3,59},{4,60},{5,61},{6,62},{7,63},{8,48},{9,... | collective-permute-start | bytes 73736 | tf_op jit(solution)/shard_map/ppermute | solution.py:35
  65.1 10.8 %collective-permute-start.13 = (f32[39,1,1920]{2,1,0:T(1,128)S(1)}, f32[39,1,1920]{2,1,0:T(1,128)S(1)}, u32[]{:S(2)}, u32[]{:S(2)}) collective-permute-start(f32[39,1,1920]{2,1,0:T(1,128)S(1)} %pack.1.refs_0_), channel_id=1, source_target_pairs={{0,6},{1,7},{2,4},{3,5},{4,2},{5,3},{6,0},{7,1},{8,14},{9,15},{10,... | collective-permute-start | bytes 898568 | tf_op jit(solution)/shard_map/ppermute | solution.py:35
  66.2 9.7 %collective-permute-start.12 = (f32[39,1,1920]{2,1,0:T(1,128)S(1)}, f32[39,1,1920]{2,1,0:T(1,128)S(1)}, u32[]{:S(2)}, u32[]{:S(2)}) collective-permute-start(f32[39,1,1920]{2,1,0:T(1,128)S(1)} %pack.1.refs_0_), channel_id=1, source_target_pairs={{0,4},{1,5},{2,6},{3,7},{4,0},{5,1},{6,2},{7,3},{8,12},{9,13},{10,... | collective-permute-start | bytes 898568 | tf_op jit(solution)/shard_map/ppermute | solution.py:35
  66.2 10.1 %collective-permute-start.11 = (f32[39,1,1920]{2,1,0:T(1,128)S(1)}, f32[39,1,1920]{2,1,0:T(1,128)S(1)}, u32[]{:S(2)}, u32[]{:S(2)}) collective-permute-start(f32[39,1,1920]{2,1,0:T(1,128)S(1)} %pack.1.refs_0_), channel_id=1, source_target_pairs={{0,2},{1,3},{2,0},{3,1},{4,6},{5,7},{6,4},{7,5},{8,10},{9,11},{10,... | collective-permute-start | bytes 898568 | tf_op jit(solution)/shard_map/ppermute | solution.py:35
  76.5 9.0 %collective-permute-start.14 = (f32[128,1920]{1,0:T(8,128)S(1)}, f32[128,1920]{1,0:T(8,128)S(1)}, u32[]{:S(2)}, u32[]{:S(2)}) collective-permute-start(f32[128,1920]{1,0:T(8,128)S(1)} %get-tuple-element.45.own_ref), channel_id=1, source_target_pairs={{0,1},{1,0},{2,3},{3,2},{4,5},{5,4},{6,7},{7,6},{8,9},{9,8},{10,11... | collective-permute-start | bytes 2949128 | tf_op jit(solution)/shard_map/ppermute | solution.py:35
  85.5 12.4 %copy-start.2 = (f32[64,2048]{1,0:T(8,128)S(1)}, f32[64,2048]{1,0:T(8,128)}, u32[]{:S(2)}) copy-start(f32[64,2048]{1,0:T(8,128)} %get-tuple-element.54.z_ref) | copy-start | bytes 1572868
  86.2 8.2 %collective-permute-start.15 = (f32[32,512]{1,0:T(8,128)S(1)}, f32[32,512]{1,0:T(8,128)S(1)}, u32[]{:S(2)}, u32[]{:S(2)}) collective-permute-start(f32[32,512]{1,0:T(8,128)S(1)} %get-tuple-element.47.vs_ref), channel_id=1, source_target_pairs={{0,64},{1,65},{2,66},{3,67},{4,68},{5,69},{6,70},{7,71},{8,72},{9,... | collective-permute-start | bytes 196616 | tf_op jit(solution)/shard_map/ppermute | solution.py:35
  87.5 6.9 %collective-permute-start.17 = (f32[32,256]{1,0:T(8,128)S(1)}, f32[32,256]{1,0:T(8,128)S(1)}, u32[]{:S(2)}, u32[]{:S(2)}) collective-permute-start(f32[32,256]{1,0:T(8,128)S(1)} %slice.3), channel_id=1, source_target_pairs={{0,192},{1,193},{2,194},{3,195},{4,196},{5,197},{6,198},{7,199},{8... | collective-permute-start | bytes 98312 | tf_op jit(solution)/shard_map/ppermute | solution.py:35
  89.3 5.1 %collective-permute-start.16 = (f32[32,256]{1,0:T(8,128)S(1)}, f32[32,256]{1,0:T(8,128)S(1)}, u32[]{:S(2)}, u32[]{:S(2)}) collective-permute-start(f32[32,256]{1,0:T(8,128)S(1)} %slice.3), channel_id=1, source_target_pairs={{0,128},{1,129},{2,130},{3,131},{4,132},{5,133},{6,134},{7,135},{8... | collective-permute-start | bytes 98312 | tf_op jit(solution)/shard_map/ppermute | solution.py:35
  95.7 2.2 %collective-permute-start.18 = (f32[32,768]{1,0:T(8,128)S(1)}, f32[32,768]{1,0:T(8,128)S(1)}, u32[]{:S(2)}, u32[]{:S(2)}) collective-permute-start(f32[32,768]{1,0:T(8,128)S(1)} %down.1.own_ref), channel_id=1, source_target_pairs={{0,1},{1,0},{2,3},{3,2},{4,5},{5,4},{6,7},{7,6},{8,9},{9,8},{10,11... | collective-permute-start | bytes 294920 | tf_op jit(solution)/shard_map/ppermute | solution.py:35
  (1 other events, 0.9 us)

commit v6 on v5

--- a/solution.py
+++ b/solution.py
@@ -35,16 +35,9 @@
     return lax.ppermute(value, AXIS, [(i, i ^ mask) for i in range(N)])
 
 
-def line(size, stride):
-    return [
-        [base + low + stride * k for k in range(size)]
-        for base in range(0, N, size * stride)
-        for low in range(stride)
-    ]
-
-
 def over_xz(value):
-    return lax.all_to_all(value, AXIS, 0, 0, axis_index_groups=line(32, 8), tiled=True)
+    groups = [[(x * 8 + z) * 8 + low for z in range(8) for x in range(4)] for low in range(8)]
+    return lax.all_to_all(value, AXIS, 0, 0, axis_index_groups=groups, tiled=True)
 
 
 def thrice(value):
@@ -173,7 +166,10 @@
 def table_kernel(rows_ref, out_ref):
     unit = rows_ref.shape[2] // 11
     low = core_index() == 0
-    sub = [rows_ref[4 * c : 4 * c + 4].sum(axis=0) for c in range(8)]
+    sub = []
+    for c in range(8):
+        at = c % 2 * 16 + c // 2
+        sub.append(rows_ref[at] + rows_ref[at + 4] + rows_ref[at + 8] + rows_ref[at + 12])
     node = [sub[2 * c] + sub[2 * c + 1] for c in range(4)]
     child = [node[0] + node[1], node[2] + node[3]]
     for c in range(8):
@@ -188,7 +184,8 @@
             ],
             axis=1,
         )
-        out_ref[4 * c : 4 * c + 4] = jnp.broadcast_to(row[None], (4, 1, row.shape[1]))
+        for k in range(4):
+            out_ref[c % 2 * 16 + c // 2 + 4 * k] = row
 
 
 def table(rows):
@@ -414,10 +411,10 @@
     state, keep, send = first(after(rhs.T, *rows), leaf_inverse, bases)
     parts = split(keep, swap(send, 1))
     mine = add_rows([rows[0]] + [swap(rows[m], 2 * m) for m in (1, 2, 3)])
-    summed = table(over_xz(after(mine, parts[0])))
+    summed = table(over_xz(after(mine, send)))
     part = parts[0] + swap(parts[1], 2) + swap(parts[2], 4) + swap(parts[3], 6)
     pair = part + swap(part, 8)
-    back = over_xz(after(summed, pair))
+    back = over_xz(after(summed, part))
     p = pair + swap(pair, 16)
     po = swap(p, 56)
 

time: 101 us -> 101 us (level)
  starting transfers between devices: 50.8 us -> 47.9 us
  waiting for transfers between devices: 26.8 us -> 29.5 us
    all_to_all x2, waiting for transfers between devices: 0.01 us -> 2.87 us  [over_xz(): lax.all_to_all(value, AXIS, 0, 0, axis_index_groups=groups, tiled=True)]
    ppermute x19, starting transfers between devices: 32.7 us -> 30.8 us  [swap(): return lax.ppermute(value, AXIS, [(i, i ^ mask) for i in range(N)])]
  transfers between devices with their start and end apart: 21 -> 21, of which waited for: 11 -> 12; matrix products, arithmetic and copies ran while one was open for 0% -> 0% of each run, Pallas kernels for 12% -> 12%
where the time goes in v6:
time: 101 us
  starting transfers between devices  47.9 us (47%)
  waiting for transfers between devices  29.5 us (29%)
  Pallas kernels  20.5 us (20%)
  local copies, waits for them, and re-layouts  2.79 us (3%)
    ppermute x19, starting transfers between devices, swap(): return lax.ppermute(value, AXIS, [(i, i ^ mask) for i in range(N)])  30.8 us
    ppermute x19, waiting for transfers between devices, swap(): return lax.ppermute(value, AXIS, [(i, i ^ mask) for i in range(N)])  26.7 us
    all_to_all x2, starting transfers between devices, over_xz(): lax.all_to_all(value, AXIS, 0, 0, axis_index_groups=groups, tiled=True)  17.1 us
    pallas_call x1, Pallas kernels, first(): pl.pallas_call(first_kernel, in_specs=whole(1) + whole(2, pltpu.HBM), out...  7.2 us
    pallas_call x1, Pallas kernels, stage(): pl.pallas_call(stage_kernel, in_specs=whole(2, pltpu.HBM), out_specs=whol...  4.46 us
    pallas_call x1, Pallas kernels, last(): pl.pallas_call(last_kernel, in_specs=whole(5), out_specs=whole(1)[0], out...  3.24 us
    all_to_all x2, waiting for transfers between devices, over_xz(): lax.all_to_all(value, AXIS, 0, 0, axis_index_groups=groups, tiled=True)  2.87 us
    unnamed x8, local copies, waits for them, and re-layouts  2.78 us
  transfers between devices with their start and end apart: 21, of which 12 were waited for; matrix products, arithmetic and copies ran while one was open for 0% of the time, Pallas kernels for 12%

profile of v6, /device:TPU:1, one launch (start us, length us, event | category | flops | bytes accessed | tf_op | source)
XLA Modules:
  0.0 100.9 jit_solution(10727971000652460462)
XLA Ops:
  0.0 1.9 %copy-done = bf16[3,2048,256]{2,1,0:T(8,128)(2,1)S(1)} copy-done((bf16[3,2048,256]{2,1,0:T(8,128)(2,1)S(1)}, bf16[3,2048,256]{2,1,0:T(8,128)(2,1)}, u32[]{:S(2)}) %copy-start) | copy-done | bytes 3145752
  1.9 1.8 %gram.1 = (f32[128,1408]{1,0:T(8,128)S(1)}, f32[128,1408]{1,0:T(8,128)S(1)}) custom-call(bf16[3,2048,256]{2,1,0:T(8,128)(2,1)S(1)} %copy-done), custom_call_target="tpu_custom_call" | custom-call | flops 1610612736 | bytes 3145728 | tf_op jit(solution)/shard_map/gram/pallas_call | solution.py:222
  3.7 3.3 %collective-permute-start = (f32[128,1408]{1,0:T(8,128)S(1)}, f32[128,1408]{1,0:T(8,128)S(1)}, u32[]{:S(2)}, u32[]{:S(2)}) collective-permute-start(f32[128,1408]{1,0:T(8,128)S(1)} %get-tuple-element.31), channel_id=1, source_target_pairs={{0,1},{1,0},{2,3},{3,2},{4,5},{5,4},{6,7},{7,6},{8,9},{9,8},{10,11... | collective-permute-start | bytes 2162696 | tf_op jit(solution)/shard_map/ppermute | solution.py:35
  7.1 1.8 %collective-permute-done.other_ref = f32[128,1408]{1,0:T(8,128)S(1)} collective-permute-done((f32[128,1408]{1,0:T(8,128)S(1)}, f32[128,1408]{1,0:T(8,128)S(1)}, u32[]{:S(2)}, u32[]{:S(2)}) %collective-permute-start) | collective-permute-done | bytes 720928 | tf_op jit(solution)/shard_map/ppermute | solution.py:35
  9.1 2.2 %collective-permute-start.2 = (f32[32,1408]{1,0:T(8,128)S(1)}, f32[32,1408]{1,0:T(8,128)S(1)}, u32[]{:S(2)}, u32[]{:S(2)}) collective-permute-start(f32[32,1408]{1,0:T(8,128)S(1)} %get-tuple-element.34), channel_id=1, source_target_pairs={{0,4},{1,5},{2,6},{3,7},{4,0},{5,1},{6,2},{7,3},{8,12},{9,13},{10,... | collective-permute-start | bytes 540680 | tf_op jit(solution)/shard_map/ppermute | solution.py:35
  11.2 1.7 %collective-permute-start.3 = (f32[32,1408]{1,0:T(8,128)S(1)}, f32[32,1408]{1,0:T(8,128)S(1)}, u32[]{:S(2)}, u32[]{:S(2)}) collective-permute-start(f32[32,1408]{1,0:T(8,128)S(1)} %get-tuple-element.35), channel_id=1, source_target_pairs={{0,6},{1,7},{2,4},{3,5},{4,2},{5,3},{6,0},{7,1},{8,14},{9,15},{10,... | collective-permute-start | bytes 540680 | tf_op jit(solution)/shard_map/ppermute | solution.py:35
  12.9 7.2 %first.1 = (f32[64,2048]{1,0:T(8,128)}, f32[32,768]{1,0:T(8,128)}, f32[32,768]{1,0:T(8,128)}) custom-call(bf16[64,2048]{1,0:T(8,128)(2,1)} %bitcast.2, bf16[2048,2048]{1,0:T(8,128)(2,1)} %f_ref.2, bf16[3,2048,256]{2,1,0:T(8,128)(2,1)} %u_ref.4), custom_call_target="tpu_custom_call" | custom-call | flops 536870912 | bytes 8388608 | tf_op jit(solution)/shard_map/first/pallas_call | solution.py:257
  22.7 11.0 %all-to-all-start = ((f32[32,1,1408]{2,1,0:T(1,128)}), f32[32,1,1408]{2,1,0:T(1,128)S(1)}, u32[]{:S(2)}, u32[]{:S(2)}) async-start(f32[32,1,1408]{2,1,0:T(1,128)} %add_rows.1), calls=%async_computation | async-start | bytes 360448 | tf_op jit(solution)/shard_map/all_to_all | solution.py:40
  34.7 1.7 %collective-permute-start.6 = (f32[8,768]{1,0:T(8,128)S(1)}, f32[8,768]{1,0:T(8,128)S(1)}, u32[]{:S(2)}, u32[]{:S(2)}) collective-permute-start(f32[8,768]{1,0:T(8,128)S(1)} %get-tuple-element.42), channel_id=1, source_target_pairs={{0,4},{1,5},{2,6},{3,7},{4,0},{5,1},{6,2},{7,3},{8,12},{9,13},{10,... | collective-permute-start | bytes 73736 | tf_op jit(solution)/shard_map/ppermute | solution.py:35
  36.4 2.2 %collective-permute-start.7 = (f32[8,768]{1,0:T(8,128)S(1)}, f32[8,768]{1,0:T(8,128)S(1)}, u32[]{:S(2)}, u32[]{:S(2)}) collective-permute-start(f32[8,768]{1,0:T(8,128)S(1)} %get-tuple-element.43), channel_id=1, source_target_pairs={{0,6},{1,7},{2,4},{3,5},{4,2},{5,3},{6,0},{7,1},{8,14},{9,15},{10,... | collective-permute-start | bytes 73736 | tf_op jit(solution)/shard_map/ppermute | solution.py:35
  39.1 1.5 %collective-permute-done.7 = f32[8,768]{1,0:T(8,128)S(1)} collective-permute-done((f32[8,768]{1,0:T(8,128)S(1)}, f32[8,768]{1,0:T(8,128)S(1)}, u32[]{:S(2)}, u32[]{:S(2)}) %collective-permute-start.7) | collective-permute-done | bytes 24608 | tf_op jit(solution)/shard_map/ppermute | solution.py:35
  40.6 2.9 %all-to-all-done.rows_ref = f32[32,1,1408]{2,1,0:T(1,128)S(1)} async-done(((f32[32,1,1408]{2,1,0:T(1,128)}), f32[32,1,1408]{2,1,0:T(1,128)S(1)}, u32[]{:S(2)}, u32[]{:S(2)}) %all-to-all-start) | async-done | bytes 180256 | tf_op jit(solution)/shard_map/all_to_all | solution.py:40
  44.2 6.1 %all-to-all-start.1 = ((f32[32,1,1920]{2,1,0:T(1,128)}), f32[32,1,1920]{2,1,0:T(1,128)S(1)}, u32[]{:S(2)}, u32[]{:S(2)}) async-start(f32[32,1,1920]{2,1,0:T(1,128)} %table.1), calls=%async_computation.1 | async-start | bytes 491520 | tf_op jit(solution)/shard_map/all_to_all | solution.py:40
  51.6 3.5 %collective-permute-done.8 = f32[8,768]{1,0:T(8,128)S(1)} collective-permute-done((f32[8,768]{1,0:T(8,128)S(1)}, f32[8,768]{1,0:T(8,128)S(1)}, u32[]{:S(2)}, u32[]{:S(2)}) %collective-permute-start.8) | collective-permute-done | bytes 24608 | tf_op jit(solution)/shard_map/ppermute | solution.py:35
  56.2 4.3 %collective-permute-done.9 = f32[8,768]{1,0:T(8,128)S(1)} collective-permute-done((f32[8,768]{1,0:T(8,128)S(1)}, f32[8,768]{1,0:T(8,128)S(1)}, u32[]{:S(2)}, u32[]{:S(2)}) %collective-permute-start.9) | collective-permute-done | bytes 24608 | tf_op jit(solution)/shard_map/ppermute | solution.py:35
  60.5 2.0 %collective-permute-start.10 = (f32[8,768]{1,0:T(8,128)S(1)}, f32[8,768]{1,0:T(8,128)S(1)}, u32[]{:S(2)}, u32[]{:S(2)}) collective-permute-start(f32[8,768]{1,0:T(8,128)S(1)} %add.19.p_ref), channel_id=1, source_target_pairs={{0,56},{1,57},{2,58},{3,59},{4,60},{5,61},{6,62},{7,63},{8,48},{9,... | collective-permute-start | bytes 73736 | tf_op jit(solution)/shard_map/ppermute | solution.py:35
  62.6 2.4 %collective-permute-done.10.po_ref = f32[8,768]{1,0:T(8,128)S(1)} collective-permute-done((f32[8,768]{1,0:T(8,128)S(1)}, f32[8,768]{1,0:T(8,128)S(1)}, u32[]{:S(2)}, u32[]{:S(2)}) %collective-permute-start.10) | collective-permute-done | bytes 24608 | tf_op jit(solution)/shard_map/ppermute | solution.py:35
  65.0 2.4 %collective-permute-start.13 = (f32[39,1,1920]{2,1,0:T(1,128)S(1)}, f32[39,1,1920]{2,1,0:T(1,128)S(1)}, u32[]{:S(2)}, u32[]{:S(2)}) collective-permute-start(f32[39,1,1920]{2,1,0:T(1,128)S(1)} %pack.1.refs_0_), channel_id=1, source_target_pairs={{0,6},{1,7},{2,4},{3,5},{4,2},{5,3},{6,0},{7,1},{8,14},{9,15},{10,... | collective-permute-start | bytes 898568 | tf_op jit(solution)/shard_map/ppermute | solution.py:35
  68.4 8.2 %collective-permute-done.13.refs_3_ = f32[39,1,1920]{2,1,0:T(1,128)S(1)} collective-permute-done((f32[39,1,1920]{2,1,0:T(1,128)S(1)}, f32[39,1,1920]{2,1,0:T(1,128)S(1)}, u32[]{:S(2)}, u32[]{:S(2)}) %collective-permute-start.13) | collective-permute-done | bytes 299552 | tf_op jit(solution)/shard_map/ppermute | solution.py:35
  77.5 5.7 %collective-permute-start.14 = (f32[128,1920]{1,0:T(8,128)S(1)}, f32[128,1920]{1,0:T(8,128)S(1)}, u32[]{:S(2)}, u32[]{:S(2)}) collective-permute-start(f32[128,1920]{1,0:T(8,128)S(1)} %get-tuple-element.45.own_ref), channel_id=1, source_target_pairs={{0,1},{1,0},{2,3},{3,2},{4,5},{5,4},{6,7},{7,6},{8,9},{9,8},{10,11... | collective-permute-start | bytes 2949128 | tf_op jit(solution)/shard_map/ppermute | solution.py:35
  83.2 2.2 %collective-permute-done.14.other_ref = f32[128,1920]{1,0:T(8,128)S(1)} collective-permute-done((f32[128,1920]{1,0:T(8,128)S(1)}, f32[128,1920]{1,0:T(8,128)S(1)}, u32[]{:S(2)}, u32[]{:S(2)}) %collective-permute-start.14) | collective-permute-done | bytes 983072 | tf_op jit(solution)/shard_map/ppermute | solution.py:35
  87.1 2.0 %collective-permute-start.17 = (f32[32,256]{1,0:T(8,128)S(1)}, f32[32,256]{1,0:T(8,128)S(1)}, u32[]{:S(2)}, u32[]{:S(2)}) collective-permute-start(f32[32,256]{1,0:T(8,128)S(1)} %slice.3), channel_id=1, source_target_pairs={{0,192},{1,193},{2,194},{3,195},{4,196},{5,197},{6,198},{7,199},{8... | collective-permute-start | bytes 98312 | tf_op jit(solution)/shard_map/ppermute | solution.py:35
  89.7 4.5 %stage.1 = (bf16[2048,2048]{1,0:T(8,128)(2,1)S(1)}, bf16[3,2048,256]{2,1,0:T(8,128)(2,1)S(1)}) custom-call(bf16[2048,2048]{1,0:T(8,128)(2,1)} %f_ref.2, bf16[3,2048,256]{2,1,0:T(8,128)(2,1)} %u_ref.4), custom_call_target="tpu_custom_call" | custom-call | bytes 16777216 | tf_op jit(solution)/shard_map/stage/pallas_call | solution.py:390
  97.6 3.2 %last.1 = bf16[64,2048]{1,0:T(8,128)(2,1)} custom-call(f32[32,768]{1,0:T(8,128)S(1)} %down.1.own_ref, f32[32,768]{1,0:T(8,128)S(1)} %collective-permute-done.18.other_ref, bf16[3,2048,256]{2,1,0:T(8,128)(2,1)S(1)} %get-tuple-element.53.u_ref, f32[64,2048]{1,0:T(8,128)S(1)} %copy-done.2, bf16[2048,2048]{1,0:T(8,128)(2,1)S(1)} %get-tuple-element.51.f_ref), custom_call_target="tpu_custom_call" | custom-call | flops 536870912 | bytes 8388608 | tf_op jit(solution)/shard_map/last/pallas_call | solution.py:365
  (42 shorter events, 15.1 us)
Async XLA Ops:
  0.0 1.9 %copy-start = (bf16[3,2048,256]{2,1,0:T(8,128)(2,1)S(1)}, bf16[3,2048,256]{2,1,0:T(8,128)(2,1)}, u32[]{:S(2)}) copy-start(bf16[3,2048,256]{2,1,0:T(8,128)(2,1)} %u_ref.4) | copy-start | bytes 9437188
  3.7 5.1 %collective-permute-start = (f32[128,1408]{1,0:T(8,128)S(1)}, f32[128,1408]{1,0:T(8,128)S(1)}, u32[]{:S(2)}, u32[]{:S(2)}) collective-permute-start(f32[128,1408]{1,0:T(8,128)S(1)} %get-tuple-element.31), channel_id=1, source_target_pairs={{0,1},{1,0},{2,3},{3,2},{4,5},{5,4},{6,7},{7,6},{8,9},{9,8},{10,11... | collective-permute-start | bytes 2162696 | tf_op jit(solution)/shard_map/ppermute | solution.py:35
  9.0 76.4 %copy-start.1 = (bf16[3,256,256]{2,1,0:T(8,128)(2,1)S(1)}, bf16[3,256,256]{2,1,0:T(8,128)(2,1)}, u32[]{:S(2)}) copy-start(bf16[3,256,256]{2,1,0:T(8,128)(2,1)} %w_ref.3) | copy-start | bytes 1179652
  9.0 12.5 %collective-permute-start.1 = (f32[32,1408]{1,0:T(8,128)S(1)}, f32[32,1408]{1,0:T(8,128)S(1)}, u32[]{:S(2)}, u32[]{:S(2)}) collective-permute-start(f32[32,1408]{1,0:T(8,128)S(1)} %get-tuple-element.33), channel_id=1, source_target_pairs={{0,2},{1,3},{2,0},{3,1},{4,6},{5,7},{6,4},{7,5},{8,10},{9,11},{10,... | collective-permute-start | bytes 540680 | tf_op jit(solution)/shard_map/ppermute | solution.py:35
  9.1 12.4 %collective-permute-start.2 = (f32[32,1408]{1,0:T(8,128)S(1)}, f32[32,1408]{1,0:T(8,128)S(1)}, u32[]{:S(2)}, u32[]{:S(2)}) collective-permute-start(f32[32,1408]{1,0:T(8,128)S(1)} %get-tuple-element.34), channel_id=1, source_target_pairs={{0,4},{1,5},{2,6},{3,7},{4,0},{5,1},{6,2},{7,3},{8,12},{9,13},{10,... | collective-permute-start | bytes 540680 | tf_op jit(solution)/shard_map/ppermute | solution.py:35
  11.2 10.7 %collective-permute-start.3 = (f32[32,1408]{1,0:T(8,128)S(1)}, f32[32,1408]{1,0:T(8,128)S(1)}, u32[]{:S(2)}, u32[]{:S(2)}) collective-permute-start(f32[32,1408]{1,0:T(8,128)S(1)} %get-tuple-element.35), channel_id=1, source_target_pairs={{0,6},{1,7},{2,4},{3,5},{4,2},{5,3},{6,0},{7,1},{8,14},{9,15},{10,... | collective-permute-start | bytes 540680 | tf_op jit(solution)/shard_map/ppermute | solution.py:35
  20.1 13.6 %collective-permute-start.4 = (f32[32,768]{1,0:T(8,128)}, f32[32,768]{1,0:T(8,128)S(1)}, u32[]{:S(2)}, u32[]{:S(2)}) collective-permute-start(f32[32,768]{1,0:T(8,128)} %get-tuple-element.37), channel_id=1, source_target_pairs={{0,1},{1,0},{2,3},{3,2},{4,5},{5,4},{6,7},{7,6},{8,9},{9,8},{10,11... | collective-permute-start | bytes 294920 | tf_op jit(solution)/shard_map/ppermute | solution.py:35
  22.7 20.8 %all-to-all-start = ((f32[32,1,1408]{2,1,0:T(1,128)}), f32[32,1,1408]{2,1,0:T(1,128)S(1)}, u32[]{:S(2)}, u32[]{:S(2)}) async-start(f32[32,1,1408]{2,1,0:T(1,128)} %add_rows.1), calls=%async_computation | async-start | bytes 360448 | tf_op jit(solution)/shard_map/all_to_all | solution.py:40
  34.6 3.9 %collective-permute-start.5 = (f32[8,768]{1,0:T(8,128)S(1)}, f32[8,768]{1,0:T(8,128)S(1)}, u32[]{:S(2)}, u32[]{:S(2)}) collective-permute-start(f32[8,768]{1,0:T(8,128)S(1)} %get-tuple-element.41), channel_id=1, source_target_pairs={{0,2},{1,3},{2,0},{3,1},{4,6},{5,7},{6,4},{7,5},{8,10},{9,11},{10,... | collective-permute-start | bytes 73736 | tf_op jit(solution)/shard_map/ppermute | solution.py:35
  34.7 4.3 %collective-permute-start.6 = (f32[8,768]{1,0:T(8,128)S(1)}, f32[8,768]{1,0:T(8,128)S(1)}, u32[]{:S(2)}, u32[]{:S(2)}) collective-permute-start(f32[8,768]{1,0:T(8,128)S(1)} %get-tuple-element.42), channel_id=1, source_target_pairs={{0,4},{1,5},{2,6},{3,7},{4,0},{5,1},{6,2},{7,3},{8,12},{9,13},{10,... | collective-permute-start | bytes 73736 | tf_op jit(solution)/shard_map/ppermute | solution.py:35
  36.4 4.2 %collective-permute-start.7 = (f32[8,768]{1,0:T(8,128)S(1)}, f32[8,768]{1,0:T(8,128)S(1)}, u32[]{:S(2)}, u32[]{:S(2)}) collective-permute-start(f32[8,768]{1,0:T(8,128)S(1)} %get-tuple-element.43), channel_id=1, source_target_pairs={{0,6},{1,7},{2,4},{3,5},{4,2},{5,3},{6,0},{7,1},{8,14},{9,15},{10,... | collective-permute-start | bytes 73736 | tf_op jit(solution)/shard_map/ppermute | solution.py:35
  44.2 20.8 %all-to-all-start.1 = ((f32[32,1,1920]{2,1,0:T(1,128)}), f32[32,1,1920]{2,1,0:T(1,128)S(1)}, u32[]{:S(2)}, u32[]{:S(2)}) async-start(f32[32,1,1920]{2,1,0:T(1,128)} %table.1), calls=%async_computation.1 | async-start | bytes 491520 | tf_op jit(solution)/shard_map/all_to_all | solution.py:40
  50.3 4.8 %collective-permute-start.8 = (f32[8,768]{1,0:T(8,128)S(1)}, f32[8,768]{1,0:T(8,128)S(1)}, u32[]{:S(2)}, u32[]{:S(2)}) collective-permute-start(f32[8,768]{1,0:T(8,128)S(1)} %add_add_fusion), channel_id=1, source_target_pairs={{0,8},{1,9},{2,10},{3,11},{4,12},{5,13},{6,14},{7,15},{8,0},{9,1},... | collective-permute-start | bytes 73736 | tf_op jit(solution)/shard_map/ppermute | solution.py:35
  55.1 5.4 %collective-permute-start.9 = (f32[8,768]{1,0:T(8,128)S(1)}, f32[8,768]{1,0:T(8,128)S(1)}, u32[]{:S(2)}, u32[]{:S(2)}) collective-permute-start(f32[8,768]{1,0:T(8,128)S(1)} %add.18), channel_id=1, source_target_pairs={{0,16},{1,17},{2,18},{3,19},{4,20},{5,21},{6,22},{7,23},{8,24},{9,... | collective-permute-start | bytes 73736 | tf_op jit(solution)/shard_map/ppermute | solution.py:35
  60.5 4.4 %collective-permute-start.10 = (f32[8,768]{1,0:T(8,128)S(1)}, f32[8,768]{1,0:T(8,128)S(1)}, u32[]{:S(2)}, u32[]{:S(2)}) collective-permute-start(f32[8,768]{1,0:T(8,128)S(1)} %add.19.p_ref), channel_id=1, source_target_pairs={{0,56},{1,57},{2,58},{3,59},{4,60},{5,61},{6,62},{7,63},{8,48},{9,... | collective-permute-start | bytes 73736 | tf_op jit(solution)/shard_map/ppermute | solution.py:35
  65.0 11.6 %collective-permute-start.13 = (f32[39,1,1920]{2,1,0:T(1,128)S(1)}, f32[39,1,1920]{2,1,0:T(1,128)S(1)}, u32[]{:S(2)}, u32[]{:S(2)}) collective-permute-start(f32[39,1,1920]{2,1,0:T(1,128)S(1)} %pack.1.refs_0_), channel_id=1, source_target_pairs={{0,6},{1,7},{2,4},{3,5},{4,2},{5,3},{6,0},{7,1},{8,14},{9,15},{10,... | collective-permute-start | bytes 898568 | tf_op jit(solution)/shard_map/ppermute | solution.py:35
  67.4 9.2 %collective-permute-start.12 = (f32[39,1,1920]{2,1,0:T(1,128)S(1)}, f32[39,1,1920]{2,1,0:T(1,128)S(1)}, u32[]{:S(2)}, u32[]{:S(2)}) collective-permute-start(f32[39,1,1920]{2,1,0:T(1,128)S(1)} %pack.1.refs_0_), channel_id=1, source_target_pairs={{0,4},{1,5},{2,6},{3,7},{4,0},{5,1},{6,2},{7,3},{8,12},{9,13},{10,... | collective-permute-start | bytes 898568 | tf_op jit(solution)/shard_map/ppermute | solution.py:35
  67.4 9.9 %collective-permute-start.11 = (f32[39,1,1920]{2,1,0:T(1,128)S(1)}, f32[39,1,1920]{2,1,0:T(1,128)S(1)}, u32[]{:S(2)}, u32[]{:S(2)}) collective-permute-start(f32[39,1,1920]{2,1,0:T(1,128)S(1)} %pack.1.refs_0_), channel_id=1, source_target_pairs={{0,2},{1,3},{2,0},{3,1},{4,6},{5,7},{6,4},{7,5},{8,10},{9,11},{10,... | collective-permute-start | bytes 898568 | tf_op jit(solution)/shard_map/ppermute | solution.py:35
  77.5 7.9 %collective-permute-start.14 = (f32[128,1920]{1,0:T(8,128)S(1)}, f32[128,1920]{1,0:T(8,128)S(1)}, u32[]{:S(2)}, u32[]{:S(2)}) collective-permute-start(f32[128,1920]{1,0:T(8,128)S(1)} %get-tuple-element.45.own_ref), channel_id=1, source_target_pairs={{0,1},{1,0},{2,3},{3,2},{4,5},{5,4},{6,7},{7,6},{8,9},{9,8},{10,11... | collective-permute-start | bytes 2949128 | tf_op jit(solution)/shard_map/ppermute | solution.py:35
  85.4 12.2 %copy-start.2 = (f32[64,2048]{1,0:T(8,128)S(1)}, f32[64,2048]{1,0:T(8,128)}, u32[]{:S(2)}) copy-start(f32[64,2048]{1,0:T(8,128)} %get-tuple-element.54.z_ref) | copy-start | bytes 1572868
  86.2 8.0 %collective-permute-start.15 = (f32[32,512]{1,0:T(8,128)S(1)}, f32[32,512]{1,0:T(8,128)S(1)}, u32[]{:S(2)}, u32[]{:S(2)}) collective-permute-start(f32[32,512]{1,0:T(8,128)S(1)} %get-tuple-element.47.vs_ref), channel_id=1, source_target_pairs={{0,64},{1,65},{2,66},{3,67},{4,68},{5,69},{6,70},{7,71},{8,72},{9,... | collective-permute-start | bytes 196616 | tf_op jit(solution)/shard_map/ppermute | solution.py:35
  87.1 7.0 %collective-permute-start.17 = (f32[32,256]{1,0:T(8,128)S(1)}, f32[32,256]{1,0:T(8,128)S(1)}, u32[]{:S(2)}, u32[]{:S(2)}) collective-permute-start(f32[32,256]{1,0:T(8,128)S(1)} %slice.3), channel_id=1, source_target_pairs={{0,192},{1,193},{2,194},{3,195},{4,196},{5,197},{6,198},{7,199},{8... | collective-permute-start | bytes 98312 | tf_op jit(solution)/shard_map/ppermute | solution.py:35
  89.1 5.1 %collective-permute-start.16 = (f32[32,256]{1,0:T(8,128)S(1)}, f32[32,256]{1,0:T(8,128)S(1)}, u32[]{:S(2)}, u32[]{:S(2)}) collective-permute-start(f32[32,256]{1,0:T(8,128)S(1)} %slice.3), channel_id=1, source_target_pairs={{0,128},{1,129},{2,130},{3,131},{4,132},{5,133},{6,134},{7,135},{8... | collective-permute-start | bytes 98312 | tf_op jit(solution)/shard_map/ppermute | solution.py:35
  95.4 2.2 %collective-permute-start.18 = (f32[32,768]{1,0:T(8,128)S(1)}, f32[32,768]{1,0:T(8,128)S(1)}, u32[]{:S(2)}, u32[]{:S(2)}) collective-permute-start(f32[32,768]{1,0:T(8,128)S(1)} %down.1.own_ref), channel_id=1, source_target_pairs={{0,1},{1,0},{2,3},{3,2},{4,5},{5,4},{6,7},{7,6},{8,9},{9,8},{10,11... | collective-permute-start | bytes 294920 | tf_op jit(solution)/shard_map/ppermute | solution.py:35
  (1 other events, 0.9 us)

commit v7 on v6

--- a/solution.py
+++ b/solution.py
@@ -410,7 +410,7 @@
     rows = split(keep, swap(send, 1))
     state, keep, send = first(after(rhs.T, *rows), leaf_inverse, bases)
     parts = split(keep, swap(send, 1))
-    mine = add_rows([rows[0]] + [swap(rows[m], 2 * m) for m in (1, 2, 3)])
+    mine = add_rows([rows[0]] + [swap(rows[m], 2 * m) for m in (2, 1, 3)])
     summed = table(over_xz(after(mine, send)))
     part = parts[0] + swap(parts[1], 2) + swap(parts[2], 4) + swap(parts[3], 6)
     pair = part + swap(part, 8)

time: 101 us -> 100 us (0.990)
  starting transfers between devices: 47.9 us -> 44.4 us
  waiting for transfers between devices: 29.5 us -> 32 us
    ppermute x19, waiting for transfers between devices: 26.7 us -> 31.3 us  [swap(): return lax.ppermute(value, AXIS, [(i, i ^ mask) for i in range(N)])]
    ppermute x19, starting transfers between devices: 30.8 us -> 26.8 us  [swap(): return lax.ppermute(value, AXIS, [(i, i ^ mask) for i in range(N)])]
    all_to_all x2, waiting for transfers between devices: 2.87 us -> 0.73 us  [over_xz(): lax.all_to_all(value, AXIS, 0, 0, axis_index_groups=groups, tiled=True)]
  transfers between devices with their start and end apart: 21 -> 21, of which waited for: 12 -> 11; matrix products, arithmetic and copies ran while one was open for 0% -> 0% of each run, Pallas kernels for 12% -> 12%
where the time goes in v7:
time: 100 us; the launch traced here: 99.9 us
  starting transfers between devices  44.4 us (44%)
  waiting for transfers between devices  32 us (32%)
  Pallas kernels  20.5 us (20%)
  local copies, waits for them, and re-layouts  2.79 us (3%)
    ppermute x19, waiting for transfers between devices, swap(): return lax.ppermute(value, AXIS, [(i, i ^ mask) for i in range(N)])  31.3 us
    ppermute x19, starting transfers between devices, swap(): return lax.ppermute(value, AXIS, [(i, i ^ mask) for i in range(N)])  26.8 us
    all_to_all x2, starting transfers between devices, over_xz(): lax.all_to_all(value, AXIS, 0, 0, axis_index_groups=groups, tiled=True)  17.6 us
    pallas_call x1, Pallas kernels, first(): pl.pallas_call(first_kernel, in_specs=whole(1) + whole(2, pltpu.HBM), out...  7.2 us
    pallas_call x1, Pallas kernels, stage(): pl.pallas_call(stage_kernel, in_specs=whole(2, pltpu.HBM), out_specs=whol...  4.46 us
    pallas_call x1, Pallas kernels, last(): pl.pallas_call(last_kernel, in_specs=whole(5), out_specs=whole(1)[0], out...  3.24 us
    unnamed x8, local copies, waits for them, and re-layouts  2.78 us
  transfers between devices with their start and end apart: 21, of which 11 were waited for; matrix products, arithmetic and copies ran while one was open for 0% of the time, Pallas kernels for 12%

profile of v7, /device:TPU:1, one launch (start us, length us, event | category | flops | bytes accessed | tf_op | source)
XLA Modules:
  0.0 99.9 jit_solution(6585443189665443158)
XLA Ops:
  0.0 1.9 %copy-done = bf16[3,2048,256]{2,1,0:T(8,128)(2,1)S(1)} copy-done((bf16[3,2048,256]{2,1,0:T(8,128)(2,1)S(1)}, bf16[3,2048,256]{2,1,0:T(8,128)(2,1)}, u32[]{:S(2)}) %copy-start) | copy-done | bytes 3145752
  1.9 1.8 %gram.1 = (f32[128,1408]{1,0:T(8,128)S(1)}, f32[128,1408]{1,0:T(8,128)S(1)}) custom-call(bf16[3,2048,256]{2,1,0:T(8,128)(2,1)S(1)} %copy-done), custom_call_target="tpu_custom_call" | custom-call | flops 1610612736 | bytes 3145728 | tf_op jit(solution)/shard_map/gram/pallas_call | solution.py:222
  3.7 3.3 %collective-permute-start = (f32[128,1408]{1,0:T(8,128)S(1)}, f32[128,1408]{1,0:T(8,128)S(1)}, u32[]{:S(2)}, u32[]{:S(2)}) collective-permute-start(f32[128,1408]{1,0:T(8,128)S(1)} %get-tuple-element.31), channel_id=1, source_target_pairs={{0,1},{1,0},{2,3},{3,2},{4,5},{5,4},{6,7},{7,6},{8,9},{9,8},{10,11... | collective-permute-start | bytes 2162696 | tf_op jit(solution)/shard_map/ppermute | solution.py:35
  7.1 1.8 %collective-permute-done.other_ref = f32[128,1408]{1,0:T(8,128)S(1)} collective-permute-done((f32[128,1408]{1,0:T(8,128)S(1)}, f32[128,1408]{1,0:T(8,128)S(1)}, u32[]{:S(2)}, u32[]{:S(2)}) %collective-permute-start) | collective-permute-done | bytes 720928 | tf_op jit(solution)/shard_map/ppermute | solution.py:35
  10.6 1.7 %collective-permute-start.3 = (f32[32,1408]{1,0:T(8,128)S(1)}, f32[32,1408]{1,0:T(8,128)S(1)}, u32[]{:S(2)}, u32[]{:S(2)}) collective-permute-start(f32[32,1408]{1,0:T(8,128)S(1)} %get-tuple-element.35), channel_id=1, source_target_pairs={{0,6},{1,7},{2,4},{3,5},{4,2},{5,3},{6,0},{7,1},{8,14},{9,15},{10,... | collective-permute-start | bytes 540680 | tf_op jit(solution)/shard_map/ppermute | solution.py:35
  12.3 7.2 %first.1 = (f32[64,2048]{1,0:T(8,128)}, f32[32,768]{1,0:T(8,128)}, f32[32,768]{1,0:T(8,128)}) custom-call(bf16[64,2048]{1,0:T(8,128)(2,1)} %bitcast.2, bf16[2048,2048]{1,0:T(8,128)(2,1)} %f_ref.2, bf16[3,2048,256]{2,1,0:T(8,128)(2,1)} %u_ref.4), custom_call_target="tpu_custom_call" | custom-call | flops 536870912 | bytes 8388608 | tf_op jit(solution)/shard_map/first/pallas_call | solution.py:257
  19.5 1.3 %collective-permute-start.4 = (f32[32,768]{1,0:T(8,128)}, f32[32,768]{1,0:T(8,128)S(1)}, u32[]{:S(2)}, u32[]{:S(2)}) collective-permute-start(f32[32,768]{1,0:T(8,128)} %get-tuple-element.37), channel_id=1, source_target_pairs={{0,1},{1,0},{2,3},{3,2},{4,5},{5,4},{6,7},{7,6},{8,9},{9,8},{10,11... | collective-permute-start | bytes 294920 | tf_op jit(solution)/shard_map/ppermute | solution.py:35
  21.6 9.4 %all-to-all-start = ((f32[32,1,1408]{2,1,0:T(1,128)}), f32[32,1,1408]{2,1,0:T(1,128)S(1)}, u32[]{:S(2)}, u32[]{:S(2)}) async-start(f32[32,1,1408]{2,1,0:T(1,128)} %add_rows.1), calls=%async_computation | async-start | bytes 360448 | tf_op jit(solution)/shard_map/all_to_all | solution.py:40
  33.2 2.6 %collective-permute-start.6 = (f32[8,768]{1,0:T(8,128)S(1)}, f32[8,768]{1,0:T(8,128)S(1)}, u32[]{:S(2)}, u32[]{:S(2)}) collective-permute-start(f32[8,768]{1,0:T(8,128)S(1)} %get-tuple-element.42), channel_id=1, source_target_pairs={{0,4},{1,5},{2,6},{3,7},{4,0},{5,1},{6,2},{7,3},{8,12},{9,13},{10,... | collective-permute-start | bytes 73736 | tf_op jit(solution)/shard_map/ppermute | solution.py:35
  35.9 1.6 %collective-permute-done.6 = f32[8,768]{1,0:T(8,128)S(1)} collective-permute-done((f32[8,768]{1,0:T(8,128)S(1)}, f32[8,768]{1,0:T(8,128)S(1)}, u32[]{:S(2)}, u32[]{:S(2)}) %collective-permute-start.6) | collective-permute-done | bytes 24608 | tf_op jit(solution)/shard_map/ppermute | solution.py:35
  37.5 2.6 %collective-permute-done.7 = f32[8,768]{1,0:T(8,128)S(1)} collective-permute-done((f32[8,768]{1,0:T(8,128)S(1)}, f32[8,768]{1,0:T(8,128)S(1)}, u32[]{:S(2)}, u32[]{:S(2)}) %collective-permute-start.7) | collective-permute-done | bytes 24608 | tf_op jit(solution)/shard_map/ppermute | solution.py:35
  41.5 8.2 %all-to-all-start.1 = ((f32[32,1,1920]{2,1,0:T(1,128)}), f32[32,1,1920]{2,1,0:T(1,128)S(1)}, u32[]{:S(2)}, u32[]{:S(2)}) async-start(f32[32,1,1920]{2,1,0:T(1,128)} %table.1), calls=%async_computation.1 | async-start | bytes 491520 | tf_op jit(solution)/shard_map/all_to_all | solution.py:40
  49.7 1.3 %collective-permute-start.8 = (f32[8,768]{1,0:T(8,128)S(1)}, f32[8,768]{1,0:T(8,128)S(1)}, u32[]{:S(2)}, u32[]{:S(2)}) collective-permute-start(f32[8,768]{1,0:T(8,128)S(1)} %add_add_fusion), channel_id=1, source_target_pairs={{0,8},{1,9},{2,10},{3,11},{4,12},{5,13},{6,14},{7,15},{8,0},{9,1},... | collective-permute-start | bytes 73736 | tf_op jit(solution)/shard_map/ppermute | solution.py:35
  51.1 3.5 %collective-permute-done.8 = f32[8,768]{1,0:T(8,128)S(1)} collective-permute-done((f32[8,768]{1,0:T(8,128)S(1)}, f32[8,768]{1,0:T(8,128)S(1)}, u32[]{:S(2)}, u32[]{:S(2)}) %collective-permute-start.8) | collective-permute-done | bytes 24608 | tf_op jit(solution)/shard_map/ppermute | solution.py:35
  55.7 4.1 %collective-permute-done.9 = f32[8,768]{1,0:T(8,128)S(1)} collective-permute-done((f32[8,768]{1,0:T(8,128)S(1)}, f32[8,768]{1,0:T(8,128)S(1)}, u32[]{:S(2)}, u32[]{:S(2)}) %collective-permute-start.9) | collective-permute-done | bytes 24608 | tf_op jit(solution)/shard_map/ppermute | solution.py:35
  59.8 2.0 %collective-permute-start.10 = (f32[8,768]{1,0:T(8,128)S(1)}, f32[8,768]{1,0:T(8,128)S(1)}, u32[]{:S(2)}, u32[]{:S(2)}) collective-permute-start(f32[8,768]{1,0:T(8,128)S(1)} %add.19.p_ref), channel_id=1, source_target_pairs={{0,56},{1,57},{2,58},{3,59},{4,60},{5,61},{6,62},{7,63},{8,48},{9,... | collective-permute-start | bytes 73736 | tf_op jit(solution)/shard_map/ppermute | solution.py:35
  61.8 2.4 %collective-permute-done.10.po_ref = f32[8,768]{1,0:T(8,128)S(1)} collective-permute-done((f32[8,768]{1,0:T(8,128)S(1)}, f32[8,768]{1,0:T(8,128)S(1)}, u32[]{:S(2)}, u32[]{:S(2)}) %collective-permute-start.10) | collective-permute-done | bytes 24608 | tf_op jit(solution)/shard_map/ppermute | solution.py:35
  64.8 2.8 %collective-permute-start.11 = (f32[39,1,1920]{2,1,0:T(1,128)S(1)}, f32[39,1,1920]{2,1,0:T(1,128)S(1)}, u32[]{:S(2)}, u32[]{:S(2)}) collective-permute-start(f32[39,1,1920]{2,1,0:T(1,128)S(1)} %pack.1.refs_0_), channel_id=1, source_target_pairs={{0,2},{1,3},{2,0},{3,1},{4,6},{5,7},{6,4},{7,5},{8,10},{9,11},{10,... | collective-permute-start | bytes 898568 | tf_op jit(solution)/shard_map/ppermute | solution.py:35
  67.6 12.1 %collective-permute-done.13.refs_3_ = f32[39,1,1920]{2,1,0:T(1,128)S(1)} collective-permute-done((f32[39,1,1920]{2,1,0:T(1,128)S(1)}, f32[39,1,1920]{2,1,0:T(1,128)S(1)}, u32[]{:S(2)}, u32[]{:S(2)}) %collective-permute-start.13) | collective-permute-done | bytes 299552 | tf_op jit(solution)/shard_map/ppermute | solution.py:35
  79.9 2.6 %collective-permute-start.14 = (f32[128,1920]{1,0:T(8,128)S(1)}, f32[128,1920]{1,0:T(8,128)S(1)}, u32[]{:S(2)}, u32[]{:S(2)}) collective-permute-start(f32[128,1920]{1,0:T(8,128)S(1)} %get-tuple-element.45.own_ref), channel_id=1, source_target_pairs={{0,1},{1,0},{2,3},{3,2},{4,5},{5,4},{6,7},{7,6},{8,9},{9,8},{10,11... | collective-permute-start | bytes 2949128 | tf_op jit(solution)/shard_map/ppermute | solution.py:35
  82.5 2.2 %collective-permute-done.14.other_ref = f32[128,1920]{1,0:T(8,128)S(1)} collective-permute-done((f32[128,1920]{1,0:T(8,128)S(1)}, f32[128,1920]{1,0:T(8,128)S(1)}, u32[]{:S(2)}, u32[]{:S(2)}) %collective-permute-start.14) | collective-permute-done | bytes 983072 | tf_op jit(solution)/shard_map/ppermute | solution.py:35
  86.2 1.9 %collective-permute-start.17 = (f32[32,256]{1,0:T(8,128)S(1)}, f32[32,256]{1,0:T(8,128)S(1)}, u32[]{:S(2)}, u32[]{:S(2)}) collective-permute-start(f32[32,256]{1,0:T(8,128)S(1)} %slice.3), channel_id=1, source_target_pairs={{0,192},{1,193},{2,194},{3,195},{4,196},{5,197},{6,198},{7,199},{8... | collective-permute-start | bytes 98312 | tf_op jit(solution)/shard_map/ppermute | solution.py:35
  88.8 4.5 %stage.1 = (bf16[2048,2048]{1,0:T(8,128)(2,1)S(1)}, bf16[3,2048,256]{2,1,0:T(8,128)(2,1)S(1)}) custom-call(bf16[2048,2048]{1,0:T(8,128)(2,1)} %f_ref.2, bf16[3,2048,256]{2,1,0:T(8,128)(2,1)} %u_ref.4), custom_call_target="tpu_custom_call" | custom-call | bytes 16777216 | tf_op jit(solution)/shard_map/stage/pallas_call | solution.py:390
  96.7 3.2 %last.1 = bf16[64,2048]{1,0:T(8,128)(2,1)} custom-call(f32[32,768]{1,0:T(8,128)S(1)} %down.1.own_ref, f32[32,768]{1,0:T(8,128)S(1)} %collective-permute-done.18.other_ref, bf16[3,2048,256]{2,1,0:T(8,128)(2,1)S(1)} %get-tuple-element.53.u_ref, f32[64,2048]{1,0:T(8,128)S(1)} %copy-done.2, bf16[2048,2048]{1,0:T(8,128)(2,1)S(1)} %get-tuple-element.51.f_ref), custom_call_target="tpu_custom_call" | custom-call | flops 536870912 | bytes 8388608 | tf_op jit(solution)/shard_map/last/pallas_call | solution.py:365
  (42 shorter events, 13.8 us)
Async XLA Ops:
  0.0 1.9 %copy-start = (bf16[3,2048,256]{2,1,0:T(8,128)(2,1)S(1)}, bf16[3,2048,256]{2,1,0:T(8,128)(2,1)}, u32[]{:S(2)}) copy-start(bf16[3,2048,256]{2,1,0:T(8,128)(2,1)} %u_ref.4) | copy-start | bytes 9437188
  3.7 5.1 %collective-permute-start = (f32[128,1408]{1,0:T(8,128)S(1)}, f32[128,1408]{1,0:T(8,128)S(1)}, u32[]{:S(2)}, u32[]{:S(2)}) collective-permute-start(f32[128,1408]{1,0:T(8,128)S(1)} %get-tuple-element.31), channel_id=1, source_target_pairs={{0,1},{1,0},{2,3},{3,2},{4,5},{5,4},{6,7},{7,6},{8,9},{9,8},{10,11... | collective-permute-start | bytes 2162696 | tf_op jit(solution)/shard_map/ppermute | solution.py:35
  9.0 75.7 %copy-start.1 = (bf16[3,256,256]{2,1,0:T(8,128)(2,1)S(1)}, bf16[3,256,256]{2,1,0:T(8,128)(2,1)}, u32[]{:S(2)}) copy-start(bf16[3,256,256]{2,1,0:T(8,128)(2,1)} %w_ref.3) | copy-start | bytes 1179652
  9.0 11.8 %collective-permute-start.1 = (f32[32,1408]{1,0:T(8,128)S(1)}, f32[32,1408]{1,0:T(8,128)S(1)}, u32[]{:S(2)}, u32[]{:S(2)}) collective-permute-start(f32[32,1408]{1,0:T(8,128)S(1)} %get-tuple-element.33), channel_id=1, source_target_pairs={{0,4},{1,5},{2,6},{3,7},{4,0},{5,1},{6,2},{7,3},{8,12},{9,13},{10,... | collective-permute-start | bytes 540680 | tf_op jit(solution)/shard_map/ppermute | solution.py:35
  10.2 10.6 %collective-permute-start.2 = (f32[32,1408]{1,0:T(8,128)S(1)}, f32[32,1408]{1,0:T(8,128)S(1)}, u32[]{:S(2)}, u32[]{:S(2)}) collective-permute-start(f32[32,1408]{1,0:T(8,128)S(1)} %get-tuple-element.34), channel_id=1, source_target_pairs={{0,2},{1,3},{2,0},{3,1},{4,6},{5,7},{6,4},{7,5},{8,10},{9,11},{10,... | collective-permute-start | bytes 540680 | tf_op jit(solution)/shard_map/ppermute | solution.py:35
  10.6 10.3 %collective-permute-start.3 = (f32[32,1408]{1,0:T(8,128)S(1)}, f32[32,1408]{1,0:T(8,128)S(1)}, u32[]{:S(2)}, u32[]{:S(2)}) collective-permute-start(f32[32,1408]{1,0:T(8,128)S(1)} %get-tuple-element.35), channel_id=1, source_target_pairs={{0,6},{1,7},{2,4},{3,5},{4,2},{5,3},{6,0},{7,1},{8,14},{9,15},{10,... | collective-permute-start | bytes 540680 | tf_op jit(solution)/shard_map/ppermute | solution.py:35
  19.5 11.5 %collective-permute-start.4 = (f32[32,768]{1,0:T(8,128)}, f32[32,768]{1,0:T(8,128)S(1)}, u32[]{:S(2)}, u32[]{:S(2)}) collective-permute-start(f32[32,768]{1,0:T(8,128)} %get-tuple-element.37), channel_id=1, source_target_pairs={{0,1},{1,0},{2,3},{3,2},{4,5},{5,4},{6,7},{7,6},{8,9},{9,8},{10,11... | collective-permute-start | bytes 294920 | tf_op jit(solution)/shard_map/ppermute | solution.py:35
  21.6 19.2 %all-to-all-start = ((f32[32,1,1408]{2,1,0:T(1,128)}), f32[32,1,1408]{2,1,0:T(1,128)S(1)}, u32[]{:S(2)}, u32[]{:S(2)}) async-start(f32[32,1,1408]{2,1,0:T(1,128)} %add_rows.1), calls=%async_computation | async-start | bytes 360448 | tf_op jit(solution)/shard_map/all_to_all | solution.py:40
  32.0 3.9 %collective-permute-start.5 = (f32[8,768]{1,0:T(8,128)S(1)}, f32[8,768]{1,0:T(8,128)S(1)}, u32[]{:S(2)}, u32[]{:S(2)}) collective-permute-start(f32[8,768]{1,0:T(8,128)S(1)} %get-tuple-element.41), channel_id=1, source_target_pairs={{0,2},{1,3},{2,0},{3,1},{4,6},{5,7},{6,4},{7,5},{8,10},{9,11},{10,... | collective-permute-start | bytes 73736 | tf_op jit(solution)/shard_map/ppermute | solution.py:35
  33.2 4.2 %collective-permute-start.6 = (f32[8,768]{1,0:T(8,128)S(1)}, f32[8,768]{1,0:T(8,128)S(1)}, u32[]{:S(2)}, u32[]{:S(2)}) collective-permute-start(f32[8,768]{1,0:T(8,128)S(1)} %get-tuple-element.42), channel_id=1, source_target_pairs={{0,4},{1,5},{2,6},{3,7},{4,0},{5,1},{6,2},{7,3},{8,12},{9,13},{10,... | collective-permute-start | bytes 73736 | tf_op jit(solution)/shard_map/ppermute | solution.py:35
  35.9 4.2 %collective-permute-start.7 = (f32[8,768]{1,0:T(8,128)S(1)}, f32[8,768]{1,0:T(8,128)S(1)}, u32[]{:S(2)}, u32[]{:S(2)}) collective-permute-start(f32[8,768]{1,0:T(8,128)S(1)} %get-tuple-element.43), channel_id=1, source_target_pairs={{0,6},{1,7},{2,4},{3,5},{4,2},{5,3},{6,0},{7,1},{8,14},{9,15},{10,... | collective-permute-start | bytes 73736 | tf_op jit(solution)/shard_map/ppermute | solution.py:35
  41.5 22.7 %all-to-all-start.1 = ((f32[32,1,1920]{2,1,0:T(1,128)}), f32[32,1,1920]{2,1,0:T(1,128)S(1)}, u32[]{:S(2)}, u32[]{:S(2)}) async-start(f32[32,1,1920]{2,1,0:T(1,128)} %table.1), calls=%async_computation.1 | async-start | bytes 491520 | tf_op jit(solution)/shard_map/all_to_all | solution.py:40
  49.7 4.8 %collective-permute-start.8 = (f32[8,768]{1,0:T(8,128)S(1)}, f32[8,768]{1,0:T(8,128)S(1)}, u32[]{:S(2)}, u32[]{:S(2)}) collective-permute-start(f32[8,768]{1,0:T(8,128)S(1)} %add_add_fusion), channel_id=1, source_target_pairs={{0,8},{1,9},{2,10},{3,11},{4,12},{5,13},{6,14},{7,15},{8,0},{9,1},... | collective-permute-start | bytes 73736 | tf_op jit(solution)/shard_map/ppermute | solution.py:35
  54.6 5.2 %collective-permute-start.9 = (f32[8,768]{1,0:T(8,128)S(1)}, f32[8,768]{1,0:T(8,128)S(1)}, u32[]{:S(2)}, u32[]{:S(2)}) collective-permute-start(f32[8,768]{1,0:T(8,128)S(1)} %add.18), channel_id=1, source_target_pairs={{0,16},{1,17},{2,18},{3,19},{4,20},{5,21},{6,22},{7,23},{8,24},{9,... | collective-permute-start | bytes 73736 | tf_op jit(solution)/shard_map/ppermute | solution.py:35
  59.8 4.4 %collective-permute-start.10 = (f32[8,768]{1,0:T(8,128)S(1)}, f32[8,768]{1,0:T(8,128)S(1)}, u32[]{:S(2)}, u32[]{:S(2)}) collective-permute-start(f32[8,768]{1,0:T(8,128)S(1)} %add.19.p_ref), channel_id=1, source_target_pairs={{0,56},{1,57},{2,58},{3,59},{4,60},{5,61},{6,62},{7,63},{8,48},{9,... | collective-permute-start | bytes 73736 | tf_op jit(solution)/shard_map/ppermute | solution.py:35
  64.3 15.4 %collective-permute-start.13 = (f32[39,1,1920]{2,1,0:T(1,128)S(1)}, f32[39,1,1920]{2,1,0:T(1,128)S(1)}, u32[]{:S(2)}, u32[]{:S(2)}) collective-permute-start(f32[39,1,1920]{2,1,0:T(1,128)S(1)} %pack.1.refs_0_), channel_id=1, source_target_pairs={{0,6},{1,7},{2,4},{3,5},{4,2},{5,3},{6,0},{7,1},{8,14},{9,15},{10,... | collective-permute-start | bytes 898568 | tf_op jit(solution)/shard_map/ppermute | solution.py:35
  64.6 15.1 %collective-permute-start.12 = (f32[39,1,1920]{2,1,0:T(1,128)S(1)}, f32[39,1,1920]{2,1,0:T(1,128)S(1)}, u32[]{:S(2)}, u32[]{:S(2)}) collective-permute-start(f32[39,1,1920]{2,1,0:T(1,128)S(1)} %pack.1.refs_0_), channel_id=1, source_target_pairs={{0,4},{1,5},{2,6},{3,7},{4,0},{5,1},{6,2},{7,3},{8,12},{9,13},{10,... | collective-permute-start | bytes 898568 | tf_op jit(solution)/shard_map/ppermute | solution.py:35
  64.8 14.9 %collective-permute-start.11 = (f32[39,1,1920]{2,1,0:T(1,128)S(1)}, f32[39,1,1920]{2,1,0:T(1,128)S(1)}, u32[]{:S(2)}, u32[]{:S(2)}) collective-permute-start(f32[39,1,1920]{2,1,0:T(1,128)S(1)} %pack.1.refs_0_), channel_id=1, source_target_pairs={{0,2},{1,3},{2,0},{3,1},{4,6},{5,7},{6,4},{7,5},{8,10},{9,11},{10,... | collective-permute-start | bytes 898568 | tf_op jit(solution)/shard_map/ppermute | solution.py:35
  79.9 4.8 %collective-permute-start.14 = (f32[128,1920]{1,0:T(8,128)S(1)}, f32[128,1920]{1,0:T(8,128)S(1)}, u32[]{:S(2)}, u32[]{:S(2)}) collective-permute-start(f32[128,1920]{1,0:T(8,128)S(1)} %get-tuple-element.45.own_ref), channel_id=1, source_target_pairs={{0,1},{1,0},{2,3},{3,2},{4,5},{5,4},{6,7},{7,6},{8,9},{9,8},{10,11... | collective-permute-start | bytes 2949128 | tf_op jit(solution)/shard_map/ppermute | solution.py:35
  84.7 12.0 %copy-start.2 = (f32[64,2048]{1,0:T(8,128)S(1)}, f32[64,2048]{1,0:T(8,128)}, u32[]{:S(2)}) copy-start(f32[64,2048]{1,0:T(8,128)} %get-tuple-element.54.z_ref) | copy-start | bytes 1572868
  85.5 7.8 %collective-permute-start.15 = (f32[32,512]{1,0:T(8,128)S(1)}, f32[32,512]{1,0:T(8,128)S(1)}, u32[]{:S(2)}, u32[]{:S(2)}) collective-permute-start(f32[32,512]{1,0:T(8,128)S(1)} %get-tuple-element.47.vs_ref), channel_id=1, source_target_pairs={{0,64},{1,65},{2,66},{3,67},{4,68},{5,69},{6,70},{7,71},{8,72},{9,... | collective-permute-start | bytes 196616 | tf_op jit(solution)/shard_map/ppermute | solution.py:35
  86.2 7.1 %collective-permute-start.17 = (f32[32,256]{1,0:T(8,128)S(1)}, f32[32,256]{1,0:T(8,128)S(1)}, u32[]{:S(2)}, u32[]{:S(2)}) collective-permute-start(f32[32,256]{1,0:T(8,128)S(1)} %slice.3), channel_id=1, source_target_pairs={{0,192},{1,193},{2,194},{3,195},{4,196},{5,197},{6,198},{7,199},{8... | collective-permute-start | bytes 98312 | tf_op jit(solution)/shard_map/ppermute | solution.py:35
  88.0 5.2 %collective-permute-start.16 = (f32[32,256]{1,0:T(8,128)S(1)}, f32[32,256]{1,0:T(8,128)S(1)}, u32[]{:S(2)}, u32[]{:S(2)}) collective-permute-start(f32[32,256]{1,0:T(8,128)S(1)} %slice.3), channel_id=1, source_target_pairs={{0,128},{1,129},{2,130},{3,131},{4,132},{5,133},{6,134},{7,135},{8... | collective-permute-start | bytes 98312 | tf_op jit(solution)/shard_map/ppermute | solution.py:35
  94.5 2.2 %collective-permute-start.18 = (f32[32,768]{1,0:T(8,128)S(1)}, f32[32,768]{1,0:T(8,128)S(1)}, u32[]{:S(2)}, u32[]{:S(2)}) collective-permute-start(f32[32,768]{1,0:T(8,128)S(1)} %down.1.own_ref), channel_id=1, source_target_pairs={{0,1},{1,0},{2,3},{3,2},{4,5},{5,4},{6,7},{7,6},{8,9},{9,8},{10,11... | collective-permute-start | bytes 294920 | tf_op jit(solution)/shard_map/ppermute | solution.py:35
  (1 other events, 0.9 us)
